TPU v7x, 32 devices: a whole 2x2x4 slice. The times are simulated.
32 devices in a mesh: gx: 2 (over x), gy: 4 (over z), gz: 4 (over y, core).
Axes of the slice: x: 2, y: 2, z: 4, core: 2. Of those that a mesh axis runs over, the one named last changes fastest.
Arguments:
- positions: float32 [2, 4, 4, 3, 2048], P('gx', 'gy', 'gz'), may hold values from 0 to 1
- charges: float32 [2, 4, 4, 2048], P('gx', 'gy', 'gz'), may hold values from -1.8 to 1.8
- masses: float32 [2, 4, 4, 2048], P('gx', 'gy', 'gz'), may hold values from 1 to 16
- weights: float32 [2, 4, 4, 512], P('gx', 'gy', 'gz'), may hold values from 0 to 1, as said below
- mapping: int32 [2, 4, 4, 2048], P('gx', 'gy', 'gz'), may hold values from 0 to 511, as said below
- atom_lists: int32 [2, 4, 4, 16, 27], P('gx', 'gy', 'gz'), may hold values from 0 to 431, as said below
- bead_lists: int32 [2, 4, 4, 4, 12], P('gx', 'gy', 'gz'), may hold values from 0 to 107, as said below
- leaving: int32 [2, 4, 4, 2, 128], P('gx', 'gy', 'gz'), may hold values from 0 to 511, as said below
Outputs:
- forces: float32 [2, 4, 4, 3, 2048], P('gx', 'gy', 'gz')
- arrivals: float32 [2, 4, 4, 2, 8, 128], P('gx', 'gy', 'gz')
Inputs may be any that keep to these rules, and one draw needn't show every extreme that they name: `mapping`: every bead number of a cell names exactly 4 atoms of that cell. `atom_lists`: entry c of every row names a tile of neighbourhood cell c, and within one cell and one column the 16 rows name 16 different tiles. `bead_lists`: the entries of one row are distinct. `leaving`: the 256 entries of a cell are distinct. With s = (i + 0.5) / 2 for a cell at slab index i: all weights are 1 where |s - 0.5| < 0.15 and all are 0 where |s - 0.5| >= 0.35.
All inputs are finite; a program needn't handle non-finite values.
Results may differ from a plain program's by a relative error of at most 0.0003.
Values sent between devices are 32-bit elements; how exact they have to be, the bound alone decides.
No kernel may reach another device: no remote copies, remote signals or barrier semaphores. Data moves between devices by JAX's collectives and lax.ppermute only.
A program may use at most 64 MiB of HBM per device.

v0:
```python
import jax
import jax.numpy as jnp
from jax import lax
from jax.sharding import PartitionSpec as P

soft_core = 0.01
eps_coarse = 2.0
sigma_sq = 0.25
exact = lax.Precision.HIGHEST


def padded(x, sides, width):
    for axis, dim in sides:
        size, length = (lax.axis_size(axis), x.shape[dim])
        up = [(i, (i + 1) % size) for i in range(size)]
        down = [(j, i) for i, j in up]
        last = lax.slice_in_dim(x, length - width, length, axis=dim)
        first = lax.slice_in_dim(x, 0, width, axis=dim)
        before = lax.ppermute(last, axis, up)
        after = lax.ppermute(first, axis, down)
        x = jnp.concatenate([before, x, after], axis=dim)
    return x


def from_behind(x, axis, by):
    size = lax.axis_size(axis)
    return lax.ppermute(x, axis, [(i, (i + by) % size) for i in range(size)])


def neighbour_offsets():
    unit_steps = jnp.arange(3, dtype=jnp.float32) - 1.0
    shift_x = jnp.broadcast_to(unit_steps[:, None, None], (3, 3, 3))
    shift_y = jnp.broadcast_to(unit_steps[None, :, None], (3, 3, 3))
    shift_z = jnp.broadcast_to(unit_steps[None, None, :], (3, 3, 3))
    return jnp.stack([shift_x, shift_y, shift_z], axis=3).reshape(27, 3, 1)


def atom_tile(own_rows, listed):
    other = jnp.moveaxis(listed, 1, 0)
    displace = own_rows[:3, :, None, None] - other[:3, None, :, :]
    dist_sq = jnp.sum(displace * displace, axis=0)
    inv_root = lax.rsqrt(dist_sq + soft_core)
    strength = (
        (own_rows[3] * own_rows[4])[:, None, None]
        * (other[3] * other[4])[None, :, :]
        * (inv_root * inv_root * inv_root)
    )
    return jnp.sum(strength[None] * displace, axis=(2, 3))


def coarse_tile(own_rows, listed):
    other = jnp.moveaxis(listed, 1, 0)
    displace = own_rows[:3, :, None, None] - other[:3, None, :, :]
    dist_sq = jnp.sum(displace * displace, axis=0)
    strength = (
        eps_coarse
        * jnp.exp(-dist_sq / sigma_sq)
        * (1.0 - own_rows[3][:, None, None] * other[3][None, :, :])
    )
    return jnp.sum(strength[None] * displace, axis=(2, 3))


def bead_table(label, bead_count):
    return (label[None, :] == jnp.arange(bead_count, dtype=jnp.int32)[:, None]).astype(jnp.float32)


def listed_forces(near_rows, own_rows, lists, tile_fn):
    width = own_rows.shape[0]
    tile_count = own_rows.shape[1] // 128
    near_flat = jnp.moveaxis(near_rows.reshape(27, width, tile_count, 128), 2, 1).reshape(
        27 * tile_count, width * 128
    )
    own_tiles = jnp.moveaxis(own_rows.reshape(width, tile_count, 128), 1, 0)
    tile_ids = jnp.arange(27 * tile_count, dtype=jnp.int32)

    def one_tile(member):
        own_block, listed = member
        selector = (listed[:, None] == tile_ids[None, :]).astype(jnp.float32)
        picked = jnp.dot(selector, near_flat, precision=exact, preferred_element_type=jnp.float32)
        return tile_fn(own_block, picked.reshape(listed.shape[0], width, 128))

    result = lax.map(one_tile, (own_tiles, lists))
    return jnp.moveaxis(result, 0, 1).reshape(3, -1)


def per_device(positions, charges, masses, weights, mapping, atom_lists, bead_lists, leaving):
    own_pos = positions[0, 0, 0]
    own_charge = charges[0, 0, 0]
    own_mass = masses[0, 0, 0]
    own_weight = weights[0, 0, 0]
    own_label = mapping[0, 0, 0]
    atom_count = own_pos.shape[1]
    bead_count = own_weight.shape[0]
    table = bead_table(own_label, bead_count)
    atom_weight = jnp.dot(own_weight, table, precision=exact, preferred_element_type=jnp.float32)
    mass_sum = jnp.dot(table, own_mass, precision=exact, preferred_element_type=jnp.float32)
    centres = (
        jnp.dot(
            own_mass[None] * own_pos, table.T, precision=exact, preferred_element_type=jnp.float32
        )
        / mass_sum
    )
    offsets = neighbour_offsets()
    own_atoms = jnp.concatenate([own_pos, own_charge[None], atom_weight[None]], axis=0)
    own_beads = jnp.concatenate([centres, own_weight[None]], axis=0)
    near_rows = padded(own_atoms[None, None, None], (("gx", 0), ("gy", 1), ("gz", 2)), 1)
    near_atoms = near_rows.reshape(27, 5, atom_count)
    bead_rows = padded(own_beads[None, None, None], (("gx", 0), ("gy", 1), ("gz", 2)), 1)
    near_beads = bead_rows.reshape(27, 4, bead_count)
    near_atoms = near_atoms.at[:, :3].add(offsets)
    near_beads = near_beads.at[:, :3].add(offsets)
    atomic_force = listed_forces(near_atoms, own_atoms, atom_lists[0, 0, 0], atom_tile)
    coarse_force = listed_forces(near_beads, own_beads, bead_lists[0, 0, 0], coarse_tile)
    scaled_coarse = coarse_force / mass_sum[None]
    forces = atomic_force + own_mass[None] * jnp.dot(
        scaled_coarse, table, precision=exact, preferred_element_type=jnp.float32
    )
    molecule_force = jnp.dot(forces, table.T, precision=exact, preferred_element_type=jnp.float32)
    payload = jnp.concatenate([centres, molecule_force, own_weight[None], mass_sum[None]], axis=0)
    leave_lists = leaving[0, 0, 0]
    bead_ids = jnp.arange(bead_count, dtype=jnp.int32)[:, None]
    pick_up = (leave_lists[0][None, :] == bead_ids).astype(jnp.float32)
    pick_down = (leave_lists[1][None, :] == bead_ids).astype(jnp.float32)
    upward = jnp.dot(payload, pick_up, precision=exact, preferred_element_type=jnp.float32)
    downward = jnp.dot(payload, pick_down, precision=exact, preferred_element_type=jnp.float32)
    from_lower = from_behind(upward, "gx", 1)
    from_higher = from_behind(downward, "gx", -1)
    from_lower = from_lower.at[0].add(-1.0)
    from_higher = from_higher.at[0].add(1.0)
    arrivals = jnp.stack([from_lower, from_higher], axis=0)
    return (forces[None, None, None], arrivals[None, None, None])


def solution(mesh):
    placed = (
        P("gx", "gy", "gz", None, None),
        P("gx", "gy", "gz", None),
        P("gx", "gy", "gz", None),
        P("gx", "gy", "gz", None),
        P("gx", "gy", "gz", None),
        P("gx", "gy", "gz", None, None),
        P("gx", "gy", "gz", None, None),
        P("gx", "gy", "gz", None, None),
    )
    return jax.shard_map(
        per_device,
        mesh=mesh,
        in_specs=placed,
        out_specs=(P("gx", "gy", "gz", None, None), P("gx", "gy", "gz", None, None, None)),
        check_vma=False,
    )
```

profile of v0, /device:TPU:0, one launch (start us, length us, event | category | flops | bytes accessed | tf_op | source)
XLA Modules:
  0.0 109.6 jit_solution(12949153661891830546)
XLA Ops:
  0.7 0.8 copy.77
  1.5 2.1 %fusion.23 = f32[1,2048]{1,0:T(1,128)S(1)} fusion(s32[2048]{0:T(1024)} %bitcast.186, f32[1,1,1,512]{3,2,1,0:T(1,128)} %param.23), kind=kOutput, calls=%fused_computation.44 | convolution fusion | flops 13631488 | bytes 18432 | tf_op jit(solution)/shard_map/dot_general | solution.py:95
  3.6 0.7 maximum_bitcast_fusion
  4.3 3.0 %collective-permute-start = (f32[1,1,1,5,2048]{4,3,2,1,0:T(8,128)S(1)}, f32[1,1,1,5,2048]{4,3,2,1,0:T(8,128)S(1)}, u32[]{:S(2)}, u32[]{:S(2)}) collective-permute-start(f32[1,1,1,5,2048]{4,3,2,1,0:T(8,128)S(1)} %maximum_bitcast_fusion), channel_id=1, source_target_pairs={{0,16},{16,0},{1,17},{17,1},{2,18},{18,2},{3,19},{19,3},{4,20},{20... | collective-permute-start | bytes 122888 | tf_op jit(solution)/shard_map/ppermute | solution.py:19
  7.4 2.6 %fusion.21 = f32[1,512]{1,0:T(1,128)S(1)} fusion(s32[2048]{0:T(1024)} %bitcast.187, f32[1,1,1,2048]{3,2,1,0:T(1,128)} %param.22), kind=kOutput, calls=%fused_computation.42 | convolution fusion | flops 13631488 | bytes 18432 | tf_op jit(solution)/shard_map/dot_general | solution.py:96
  10.1 1.9 %fusion.31 = f32[3,512]{1,0:T(4,128)S(1)} fusion(s32[2048]{0:T(1024)S(1)} %bitcast.188, f32[2048]{0:T(1024)S(1)} %bitcast.184, f32[512]{0:T(512)S(1)} %bitcast.192, f32[1,1,1,3,2048]{4,2,3,1,0:T(1,128)S(1)} %copy-done), kind=kOutput, calls=%fused_computation.53 | convolution fusion | flops 38804992 | bytes 49152 | tf_op jit(solution)/shard_map/dot_general | solution.py:98
  12.0 2.0 %collective-permute-start.6 = (f32[1,1,1,4,512]{4,3,2,1,0:T(4,128)S(1)}, f32[1,1,1,4,512]{4,3,2,1,0:T(4,128)S(1)}, u32[]{:S(2)}, u32[]{:S(2)}) collective-permute-start(f32[1,1,1,4,512]{4,3,2,1,0:T(4,128)S(1)} %maximum_bitcast_fusion.3), channel_id=1, source_target_pairs={{0,16},{16,0},{1,17},{17,1},{2,18},{18,2},{3,19},{19,3},{4,20},{20... | collective-permute-start | bytes 24584 | tf_op jit(solution)/shard_map/ppermute | solution.py:19
  14.3 1.5 %collective-permute-done.6 = f32[1,1,1,4,512]{4,3,2,1,0:T(4,128)S(1)} collective-permute-done((f32[1,1,1,4,512]{4,3,2,1,0:T(4,128)S(1)}, f32[1,1,1,4,512]{4,3,2,1,0:T(4,128)S(1)}, u32[]{:S(2)}, u32[]{:S(2)}) %collective-permute-start.6) | collective-permute-done | bytes 8224 | tf_op jit(solution)/shard_map/ppermute | solution.py:19
  15.8 1.9 %collective-permute-done.7 = f32[1,1,1,4,512]{4,3,2,1,0:T(4,128)S(1)} collective-permute-done((f32[1,1,1,4,512]{4,3,2,1,0:T(4,128)S(1)}, f32[1,1,1,4,512]{4,3,2,1,0:T(4,128)S(1)}, u32[]{:S(2)}, u32[]{:S(2)}) %collective-permute-start.7) | collective-permute-done | bytes 8224 | tf_op jit(solution)/shard_map/ppermute | solution.py:20
  17.7 1.6 %collective-permute-start.8 = (f32[3,1,1,4,512]{4,3,2,1,0:T(4,128)S(1)}, f32[3,1,1,4,512]{4,3,2,1,0:T(4,128)S(1)}, u32[]{:S(2)}, u32[]{:S(2)}) collective-permute-start(f32[3,1,1,4,512]{4,3,2,1,0:T(4,128)S(1)} %pad_maximum_fusion.5), channel_id=1, source_target_pairs={{0,4},{4,8},{8,12},{12,0},{1,5},{5,9},{9,13},{13,1},{2,6},{6,10},{... | collective-permute-start | bytes 73736 | tf_op jit(solution)/shard_map/ppermute | solution.py:19
  19.3 2.2 %collective-permute-start.9 = (f32[3,1,1,4,512]{4,3,2,1,0:T(4,128)S(1)}, f32[3,1,1,4,512]{4,3,2,1,0:T(4,128)S(1)}, u32[]{:S(2)}, u32[]{:S(2)}) collective-permute-start(f32[3,1,1,4,512]{4,3,2,1,0:T(4,128)S(1)} %pad_maximum_fusion.5), channel_id=1, source_target_pairs={{4,0},{8,4},{12,8},{0,12},{5,1},{9,5},{13,9},{1,13},{6,2},{10,6},{... | collective-permute-start | bytes 73736 | tf_op jit(solution)/shard_map/ppermute | solution.py:20
  21.8 1.6 %collective-permute-done.8 = f32[3,1,1,4,512]{4,3,2,1,0:T(4,128)S(1)} collective-permute-done((f32[3,1,1,4,512]{4,3,2,1,0:T(4,128)S(1)}, f32[3,1,1,4,512]{4,3,2,1,0:T(4,128)S(1)}, u32[]{:S(2)}, u32[]{:S(2)}) %collective-permute-start.8) | collective-permute-done | bytes 24608 | tf_op jit(solution)/shard_map/ppermute | solution.py:19
  23.5 1.7 %collective-permute-start.11 = (f32[3,3,1,4,512]{4,3,2,1,0:T(4,128)S(1)}, f32[3,3,1,4,512]{4,3,2,1,0:T(4,128)S(1)}, u32[]{:S(2)}, u32[]{:S(2)}) collective-permute-start(f32[3,3,1,4,512]{4,3,2,1,0:T(4,128)S(1)} %pad_maximum_fusion.4), channel_id=1, source_target_pairs={{1,0},{2,1},{3,2},{0,3},{5,4},{6,5},{7,6},{4,7},{9,8},{10,9},{11,1... | collective-permute-start | bytes 221192 | tf_op jit(solution)/shard_map/ppermute | solution.py:20
  25.3 1.4 %collective-permute-start.2 = (f32[3,1,1,5,2048]{4,3,2,1,0:T(8,128)S(1)}, f32[3,1,1,5,2048]{4,3,2,1,0:T(8,128)S(1)}, u32[]{:S(2)}, u32[]{:S(2)}) collective-permute-start(f32[3,1,1,5,2048]{4,3,2,1,0:T(8,128)S(1)} %pad_maximum_fusion.3), channel_id=1, source_target_pairs={{0,4},{4,8},{8,12},{12,0},{1,5},{5,9},{9,13},{13,1},{2,6},{6,10},{... | collective-permute-start | bytes 368648 | tf_op jit(solution)/shard_map/ppermute | solution.py:19
  26.6 2.5 %collective-permute-start.3 = (f32[3,1,1,5,2048]{4,3,2,1,0:T(8,128)S(1)}, f32[3,1,1,5,2048]{4,3,2,1,0:T(8,128)S(1)}, u32[]{:S(2)}, u32[]{:S(2)}) collective-permute-start(f32[3,1,1,5,2048]{4,3,2,1,0:T(8,128)S(1)} %pad_maximum_fusion.3), channel_id=1, source_target_pairs={{4,0},{8,4},{12,8},{0,12},{5,1},{9,5},{13,9},{1,13},{6,2},{10,6},{... | collective-permute-start | bytes 368648 | tf_op jit(solution)/shard_map/ppermute | solution.py:20
  29.3 2.0 %scatter-add.15 = f32[27,4,512]{2,1,0:T(4,128)S(1)} dynamic-update-slice(f32[27,4,512]{2,1,0:T(4,128)S(1)} %bitcast.163, f32[27,3,512]{2,1,0:T(4,128)S(1)} %slice_add_fusion.1, s32[]{:T(128)} %constant.139.clone.1, s32[]{:T(128)} %constant.139.clone.1, s32[]{:T(128)} %constant.139.clone.1) | dynamic-update-slice | bytes 331780 | tf_op jit(solution)/shard_map/scatter-add | solution.py:111
  31.5 3.5 %collective-permute-done.2 = f32[3,1,1,5,2048]{4,3,2,1,0:T(8,128)S(1)} collective-permute-done((f32[3,1,1,5,2048]{4,3,2,1,0:T(8,128)S(1)}, f32[3,1,1,5,2048]{4,3,2,1,0:T(8,128)S(1)}, u32[]{:S(2)}, u32[]{:S(2)}) %collective-permute-start.2) | collective-permute-done | bytes 122912 | tf_op jit(solution)/shard_map/ppermute | solution.py:19
  34.9 2.4 %collective-permute-done.3 = f32[3,1,1,5,2048]{4,3,2,1,0:T(8,128)S(1)} collective-permute-done((f32[3,1,1,5,2048]{4,3,2,1,0:T(8,128)S(1)}, f32[3,1,1,5,2048]{4,3,2,1,0:T(8,128)S(1)}, u32[]{:S(2)}, u32[]{:S(2)}) %collective-permute-start.3) | collective-permute-done | bytes 122912 | tf_op jit(solution)/shard_map/ppermute | solution.py:20
  37.8 1.7 %collective-permute-start.5 = (f32[3,3,1,5,2048]{4,2,3,1,0:T(1,128)S(1)}, f32[3,3,1,5,2048]{4,2,3,1,0:T(1,128)S(1)}, u32[]{:S(2)}, u32[]{:S(2)}) collective-permute-start(f32[3,3,1,5,2048]{4,2,3,1,0:T(1,128)S(1)} %copy.44), channel_id=1, source_target_pairs={{1,0},{2,1},{3,2},{0,3},{5,4},{6,5},{7,6},{4,7},{9,8},{10,9},{11,1... | collective-permute-start | bytes 1105928 | tf_op jit(solution)/shard_map/ppermute | solution.py:20
  39.5 7.7 %while.27 = (s32[]{:T(128)}, f32[4,3,128]{2,1,0:T(4,128)S(1)}, f32[4,4,128]{2,1,0:T(4,128)S(1)}, s32[4,12]{1,0:T(4,128)}, f32[108,512]{1,0:T(8,128)S(1)}, /*index=5*/s32[]{:T(128)}) while((s32[]{:T(128)}, f32[4,3,128]{2,1,0:T(4,128)S(1)}, f32[4,4,128]{2,1,0:T(4,128)S(1)}, s32[4,12]{1,0:T(4,128)}, f32[108,512]{1,0:T(8,128)S(1)}, ...), condition=%wide.region_7.8_spmd.clone, body=%wide.region_4.7_spmd.clone.sunk | while | flops 12485522 | bytes 3562721 | solution.py:82
  50.2 50.8 %while.26 = (s32[]{:T(128)}, f32[16,3,128]{2,1,0:T(4,128)S(1)}, f32[16,5,128]{2,0,1:T(8,128)S(1)}, s32[16,27]{1,0:T(8,128)}, f32[432,640]{1,0:T(8,128)S(1)}, /*index=5*/s32[]{:T(128)}, s32[]{:T(128)}, s32[]{}, s32[]{}) while((s32[]{:T(128)}, f32[16,3,128]{2,1,0:T(4,128)S(1)}, f32[16,5,128]{2,0,1:T(8,128)S(1)}, s32[16,27]{1,0:T(8,128)}, ...), condition=%wide.region_3.4_spmd.clone, body=%wide.region_0.3_spmd.clone.sunk | while | flops 99326480 | bytes 8740305 | solution.py:82
  50.2 0.7 fusion.62
  56.6 0.7 fusion.62
  62.9 0.7 fusion.62
  66.1 0.7 fusion.62
  72.4 0.7 fusion.62
  75.6 0.7 fusion.62
  101.0 1.4 %fusion.25 = f32[3,2048]{1,0:T(4,128)S(1)} fusion(s32[2048]{0:T(1024)S(1)} %bitcast.189, f32[16,3,128]{2,1,0:T(4,128)S(1)} %get-tuple-element.114, f32[2048]{0:T(1024)S(1)} %bitcast.185, f32[4,3,128]{2,1,0:T(4,128)S(1)} %get-tuple-element.115, f32[512]{0:T(512)S(1)} %bitcast.193), kind=kOutput, calls=%fused_computation.46 | convolution fusion | flops 38811136 | bytes 73728 | tf_op jit(solution)/shard_map/dot_general | solution.py:115
  102.4 1.9 %fusion.19 = f32[3,512]{1,0:T(4,128)S(1)} fusion(f32[3,2048]{1,0:T(4,128)S(1)} %fusion.25, s32[2048]{0:T(1024)S(1)} %bitcast.190), kind=kOutput, calls=%fused_computation.40 | convolution fusion | flops 38797312 | bytes 38912 | tf_op jit(solution)/shard_map/dot_general | solution.py:118
  105.3 1.6 %collective-permute-start.13 = (f32[8,128]{1,0:T(8,128)S(1)}, f32[8,128]{1,0:T(8,128)S(1)}, u32[]{:S(2)}, u32[]{:S(2)}) collective-permute-start(f32[8,128]{1,0:T(8,128)S(1)} %fusion.34), channel_id=1, source_target_pairs={{0,16},{16,0},{1,17},{17,1},{2,18},{18,2},{3,19},{19,3},{4,20},{20... | collective-permute-start | bytes 12296 | tf_op jit(solution)/shard_map/ppermute | solution.py:27
  107.5 0.7 collective-permute-done.12
  108.3 0.7 collective-permute-done.13
  (332 shorter events, 59.1 us)
Async XLA Ops:
  0.6 9.4 %copy-start = (f32[1,1,1,3,2048]{4,2,3,1,0:T(1,128)S(1)}, f32[1,1,1,3,2048]{4,2,3,1,0:T(1,128)}, u32[]{:S(2)}) copy-start(f32[1,1,1,3,2048]{4,2,3,1,0:T(1,128)} %param.20) | copy-start | bytes 73732
  0.6 9.4 %copy-start.5 = (s32[1,1,1,2048]{3,2,1,0:T(1,128)S(1)}, s32[1,1,1,2048]{3,2,1,0:T(1,128)}, u32[]{:S(2)}) copy-start(s32[1,1,1,2048]{3,2,1,0:T(1,128)} %param.24) | copy-start | bytes 24580
  0.7 11.3 %copy-start.2 = (f32[1,1,1,512]{3,2,1,0:T(1,128)S(1)}, f32[1,1,1,512]{3,2,1,0:T(1,128)}, u32[]{:S(2)}) copy-start(f32[1,1,1,512]{3,2,1,0:T(1,128)} %param.23) | copy-start | bytes 6148
  0.7 13.5 %copy-start.1 = (f32[1,1,1,2048]{3,2,1,0:T(1,128)S(1)}, f32[1,1,1,2048]{3,2,1,0:T(1,128)}, u32[]{:S(2)}) copy-start(f32[1,1,1,2048]{3,2,1,0:T(1,128)} %param.21) | copy-start | bytes 24580
  0.7 9.4 %copy-start.4 = (f32[1,1,1,2048]{3,2,1,0:T(1,128)S(1)}, f32[1,1,1,2048]{3,2,1,0:T(1,128)}, u32[]{:S(2)}) copy-start(f32[1,1,1,2048]{3,2,1,0:T(1,128)} %param.22) | copy-start | bytes 24580
  0.7 13.4 %copy-start.3 = (s32[1,1,1,2,128]{4,3,2,1,0:T(2,128)S(1)}, s32[1,1,1,2,128]{4,3,2,1,0:T(2,128)}, u32[]{:S(2)}) copy-start(s32[1,1,1,2,128]{4,3,2,1,0:T(2,128)} %param.27) | copy-start | bytes 3076
  4.3 20.9 %collective-permute-start = (f32[1,1,1,5,2048]{4,3,2,1,0:T(8,128)S(1)}, f32[1,1,1,5,2048]{4,3,2,1,0:T(8,128)S(1)}, u32[]{:S(2)}, u32[]{:S(2)}) collective-permute-start(f32[1,1,1,5,2048]{4,3,2,1,0:T(8,128)S(1)} %maximum_bitcast_fusion), channel_id=1, source_target_pairs={{0,16},{16,0},{1,17},{17,1},{2,18},{18,2},{3,19},{19,3},{4,20},{20... | collective-permute-start | bytes 122888 | tf_op jit(solution)/shard_map/ppermute | solution.py:19
  7.3 17.9 %collective-permute-start.1 = (f32[1,1,1,5,2048]{4,3,2,1,0:T(8,128)S(1)}, f32[1,1,1,5,2048]{4,3,2,1,0:T(8,128)S(1)}, u32[]{:S(2)}, u32[]{:S(2)}) collective-permute-start(f32[1,1,1,5,2048]{4,3,2,1,0:T(8,128)S(1)} %maximum_bitcast_fusion), channel_id=1, source_target_pairs={{16,0},{0,16},{17,1},{1,17},{18,2},{2,18},{19,3},{3,19},{20,4},{4,... | collective-permute-start | bytes 122888 | tf_op jit(solution)/shard_map/ppermute | solution.py:20
  12.0 3.8 %collective-permute-start.6 = (f32[1,1,1,4,512]{4,3,2,1,0:T(4,128)S(1)}, f32[1,1,1,4,512]{4,3,2,1,0:T(4,128)S(1)}, u32[]{:S(2)}, u32[]{:S(2)}) collective-permute-start(f32[1,1,1,4,512]{4,3,2,1,0:T(4,128)S(1)} %maximum_bitcast_fusion.3), channel_id=1, source_target_pairs={{0,16},{16,0},{1,17},{17,1},{2,18},{18,2},{3,19},{19,3},{4,20},{20... | collective-permute-start | bytes 24584 | tf_op jit(solution)/shard_map/ppermute | solution.py:19
  14.0 3.7 %collective-permute-start.7 = (f32[1,1,1,4,512]{4,3,2,1,0:T(4,128)S(1)}, f32[1,1,1,4,512]{4,3,2,1,0:T(4,128)S(1)}, u32[]{:S(2)}, u32[]{:S(2)}) collective-permute-start(f32[1,1,1,4,512]{4,3,2,1,0:T(4,128)S(1)} %maximum_bitcast_fusion.3), channel_id=1, source_target_pairs={{16,0},{0,16},{17,1},{1,17},{18,2},{2,18},{19,3},{3,19},{20,4},{4,... | collective-permute-start | bytes 24584 | tf_op jit(solution)/shard_map/ppermute | solution.py:20
  17.7 5.7 %collective-permute-start.8 = (f32[3,1,1,4,512]{4,3,2,1,0:T(4,128)S(1)}, f32[3,1,1,4,512]{4,3,2,1,0:T(4,128)S(1)}, u32[]{:S(2)}, u32[]{:S(2)}) collective-permute-start(f32[3,1,1,4,512]{4,3,2,1,0:T(4,128)S(1)} %pad_maximum_fusion.5), channel_id=1, source_target_pairs={{0,4},{4,8},{8,12},{12,0},{1,5},{5,9},{9,13},{13,1},{2,6},{6,10},{... | collective-permute-start | bytes 73736 | tf_op jit(solution)/shard_map/ppermute | solution.py:19
  19.3 4.1 %collective-permute-start.9 = (f32[3,1,1,4,512]{4,3,2,1,0:T(4,128)S(1)}, f32[3,1,1,4,512]{4,3,2,1,0:T(4,128)S(1)}, u32[]{:S(2)}, u32[]{:S(2)}) collective-permute-start(f32[3,1,1,4,512]{4,3,2,1,0:T(4,128)S(1)} %pad_maximum_fusion.5), channel_id=1, source_target_pairs={{4,0},{8,4},{12,8},{0,12},{5,1},{9,5},{13,9},{1,13},{6,2},{10,6},{... | collective-permute-start | bytes 73736 | tf_op jit(solution)/shard_map/ppermute | solution.py:20
  23.4 5.7 %collective-permute-start.10 = (f32[3,3,1,4,512]{4,3,2,1,0:T(4,128)S(1)}, f32[3,3,1,4,512]{4,3,2,1,0:T(4,128)S(1)}, u32[]{:S(2)}, u32[]{:S(2)}) collective-permute-start(f32[3,3,1,4,512]{4,3,2,1,0:T(4,128)S(1)} %pad_maximum_fusion.4), channel_id=1, source_target_pairs={{0,1},{1,2},{2,3},{3,0},{4,5},{5,6},{6,7},{7,4},{8,9},{9,10},{10,1... | collective-permute-start | bytes 221192 | tf_op jit(solution)/shard_map/ppermute | solution.py:19
  23.5 5.7 %collective-permute-start.11 = (f32[3,3,1,4,512]{4,3,2,1,0:T(4,128)S(1)}, f32[3,3,1,4,512]{4,3,2,1,0:T(4,128)S(1)}, u32[]{:S(2)}, u32[]{:S(2)}) collective-permute-start(f32[3,3,1,4,512]{4,3,2,1,0:T(4,128)S(1)} %pad_maximum_fusion.4), channel_id=1, source_target_pairs={{1,0},{2,1},{3,2},{0,3},{5,4},{6,5},{7,6},{4,7},{9,8},{10,9},{11,1... | collective-permute-start | bytes 221192 | tf_op jit(solution)/shard_map/ppermute | solution.py:20
  25.3 9.6 %collective-permute-start.2 = (f32[3,1,1,5,2048]{4,3,2,1,0:T(8,128)S(1)}, f32[3,1,1,5,2048]{4,3,2,1,0:T(8,128)S(1)}, u32[]{:S(2)}, u32[]{:S(2)}) collective-permute-start(f32[3,1,1,5,2048]{4,3,2,1,0:T(8,128)S(1)} %pad_maximum_fusion.3), channel_id=1, source_target_pairs={{0,4},{4,8},{8,12},{12,0},{1,5},{5,9},{9,13},{13,1},{2,6},{6,10},{... | collective-permute-start | bytes 368648 | tf_op jit(solution)/shard_map/ppermute | solution.py:19
  26.6 10.6 %collective-permute-start.3 = (f32[3,1,1,5,2048]{4,3,2,1,0:T(8,128)S(1)}, f32[3,1,1,5,2048]{4,3,2,1,0:T(8,128)S(1)}, u32[]{:S(2)}, u32[]{:S(2)}) collective-permute-start(f32[3,1,1,5,2048]{4,3,2,1,0:T(8,128)S(1)} %pad_maximum_fusion.3), channel_id=1, source_target_pairs={{4,0},{8,4},{12,8},{0,12},{5,1},{9,5},{13,9},{1,13},{6,2},{10,6},{... | collective-permute-start | bytes 368648 | tf_op jit(solution)/shard_map/ppermute | solution.py:20
  37.7 10.2 %collective-permute-start.4 = (f32[3,3,1,5,2048]{4,2,3,1,0:T(1,128)S(1)}, f32[3,3,1,5,2048]{4,2,3,1,0:T(1,128)S(1)}, u32[]{:S(2)}, u32[]{:S(2)}) collective-permute-start(f32[3,3,1,5,2048]{4,2,3,1,0:T(1,128)S(1)} %copy.44), channel_id=1, source_target_pairs={{0,1},{1,2},{2,3},{3,0},{4,5},{5,6},{6,7},{7,4},{8,9},{9,10},{10,1... | collective-permute-start | bytes 1105928 | tf_op jit(solution)/shard_map/ppermute | solution.py:19
  37.8 10.2 %collective-permute-start.5 = (f32[3,3,1,5,2048]{4,2,3,1,0:T(1,128)S(1)}, f32[3,3,1,5,2048]{4,2,3,1,0:T(1,128)S(1)}, u32[]{:S(2)}, u32[]{:S(2)}) collective-permute-start(f32[3,3,1,5,2048]{4,2,3,1,0:T(1,128)S(1)} %copy.44), channel_id=1, source_target_pairs={{1,0},{2,1},{3,2},{0,3},{5,4},{6,5},{7,6},{4,7},{9,8},{10,9},{11,1... | collective-permute-start | bytes 1105928 | tf_op jit(solution)/shard_map/ppermute | solution.py:20
  104.5 3.7 %collective-permute-start.12 = (f32[8,128]{1,0:T(8,128)S(1)}, f32[8,128]{1,0:T(8,128)S(1)}, u32[]{:S(2)}, u32[]{:S(2)}) collective-permute-start(f32[8,128]{1,0:T(8,128)S(1)} %fusion.33), channel_id=1, source_target_pairs={{0,16},{16,0},{1,17},{17,1},{2,18},{18,2},{3,19},{19,3},{4,20},{20... | collective-permute-start | bytes 12296 | tf_op jit(solution)/shard_map/ppermute | solution.py:27
  105.3 3.7 %collective-permute-start.13 = (f32[8,128]{1,0:T(8,128)S(1)}, f32[8,128]{1,0:T(8,128)S(1)}, u32[]{:S(2)}, u32[]{:S(2)}) collective-permute-start(f32[8,128]{1,0:T(8,128)S(1)} %fusion.34), channel_id=1, source_target_pairs={{0,16},{16,0},{1,17},{17,1},{2,18},{18,2},{3,19},{19,3},{4,20},{20... | collective-permute-start | bytes 12296 | tf_op jit(solution)/shard_map/ppermute | solution.py:27
where the time goes:
time: 111 us; the launch traced here: 110 us
  other arithmetic  34.4 us (31%)
  local copies, waits for them, and re-layouts  21.3 us (19%)
  matrix products  19.6 us (18%)
  starting transfers between devices  18.7 us (17%)
  waiting for transfers between devices  12.9 us (12%)
  loops' own time  1.84 us (2%)
    eq x20, local copies, waits for them, and re-layouts, one_tile(): selector = (listed[:, None] == tile_ids[None, :]).astype(jnp.float32)  13.9 us
    reduce_sum x16, other arithmetic, atom_tile(): return jnp.sum(strength[None] * displace, axis=(2, 3))  11 us
    reduce_sum x16, other arithmetic, atom_tile(): dist_sq = jnp.sum(displace * displace, axis=0)  10.7 us
    dot_general x20, matrix products, one_tile(): jnp.dot(selector, near_flat, precision=exact, preferred_element_type=jnp....  9.2 us
    ppermute x6, starting transfers between devices, padded(): after = lax.ppermute(first, axis, down)  8.41 us
    ppermute x6, starting transfers between devices, padded(): before = lax.ppermute(last, axis, up)  8.12 us
    ppermute x6, waiting for transfers between devices, padded(): before = lax.ppermute(last, axis, up)  7.18 us
    mul x16, other arithmetic, atom_tile(): (own_rows[3] * own_rows[4])[:, None, None]  6.37 us
  transfers between devices with their start and end apart: 14, of which 8 were waited for; matrix products, arithmetic and copies ran while one was open for 14% of the time, Pallas kernels for 0%

commit v1 on v0

v1 whole, which is shorter than its diff:
```python
import functools

import jax
import jax.numpy as jnp
from jax import lax
from jax.experimental import pallas as pl
from jax.experimental.pallas import tpu as pltpu
from jax.sharding import PartitionSpec as P

SOFT_CORE = 0.01
EPS_COARSE = 2.0
SIGMA_SQ = 0.25
LANES = 128
ROWS = 32
F32, BF16 = jnp.float32, jnp.bfloat16
VMEM = pl.BlockSpec(memory_space=pltpu.VMEM)
SMEM = pl.BlockSpec(memory_space=pltpu.SMEM)
CONTRACT_LANES = (((1,), (1,)), ((), ()))


def split3(v):
    high = v.astype(BF16).astype(F32)
    rest = v - high
    mid = rest.astype(BF16).astype(F32)
    return high, mid, rest - mid


def far_rows(coords, soft):
    rows = []
    for v in coords:
        h, m, l = split3(v)
        rows += [h, h, h, m, m, l]
    norm = coords[0] * coords[0] + coords[1] * coords[1] + (coords[2] * coords[2] + soft)
    one = jnp.ones_like(norm)
    return rows + [one, one, one] + list(split3(norm))


def near_rows(coords, scale):
    rows = []
    for v in coords:
        h, m, l = (-2.0 * scale * part for part in split3(v))
        rows += [h, m, l, h, m, h]
    norm = scale * (coords[0] * coords[0] + coords[1] * coords[1] + coords[2] * coords[2])
    one = jnp.full_like(norm, scale)
    return rows + list(split3(norm)) + [one, one, one]


def store_rows(ref, rows):
    for r, row in enumerate(rows):
        ref[:, r, :] = row
    blank = jnp.zeros_like(rows[0])
    for r in range(len(rows), ROWS):
        ref[:, r, :] = blank


def one_hot(label_ref, out_ref, tiles):
    for t in range(tiles):
        at = slice(t * LANES, (t + 1) * LANES)
        low = lax.rem(label_ref[:, at], LANES)
        ids = lax.broadcasted_iota(jnp.int32, (LANES, LANES), 0)
        out_ref[:, at] = jnp.where(ids == low, 1.0, 0.0).astype(BF16)


def high_mask(label, groups, repeat):
    ids = lax.broadcasted_iota(jnp.int32, (groups, label.shape[1]), 0)
    hit = (ids == label // LANES).astype(F32)
    return jnp.concatenate([hit] * repeat, axis=0)


def stacked3(v):
    return jnp.concatenate(list(split3(v)), axis=0).astype(BF16)


def fold3(v):
    n = v.shape[0] // 3
    return v[:n] + v[n : 2 * n] + v[2 * n :]


def gather_rows(table, label, hot, groups):
    features = table.shape[0] // groups
    picked = fold3(jnp.dot(stacked3(table), hot, preferred_element_type=F32))
    picked = picked * high_mask(label, groups, features)
    return [
        jnp.sum(picked[f * groups : (f + 1) * groups], axis=0, keepdims=True)
        for f in range(features)
    ]


def sum_rows(values, label, hot, groups):
    spread = jnp.concatenate([jnp.broadcast_to(v, (groups, v.shape[1])) for v in values], axis=0)
    spread = spread * high_mask(label, groups, len(values))
    return fold3(
        lax.dot_general(stacked3(spread), hot, CONTRACT_LANES, preferred_element_type=F32)
    )


def prepare_kernel(pos, charge, mass, weight, label_ref, rows_out, mass_out, near_out, hot, near):
    atoms, beads = pos.shape[1], weight.shape[1]
    tiles, groups = atoms // LANES, beads // LANES
    one_hot(label_ref, hot, tiles)
    label = label_ref[...]
    m = mass[...]
    values = [m * pos[k : k + 1, :] for k in range(3)] + [m]
    sums = sum_rows(values, label, hot[...], groups)
    mass_sum = sums[3 * groups :]
    mass_out[...] = mass_sum
    table = jnp.concatenate(
        [weight[:, g * LANES : (g + 1) * LANES] for g in range(groups)], axis=0
    )
    charged = charge[...] * gather_rows(table, label, hot[...], groups)[0]
    for t in range(tiles):
        at = slice(t * LANES, (t + 1) * LANES)
        for k in range(3):
            rows_out[k * tiles + t : k * tiles + t + 1, :] = pos[k : k + 1, at]
        rows_out[3 * tiles + t : 3 * tiles + t + 1, :] = charged[:, at]
    base = 4 * tiles
    for k in range(3):
        rows_out[base + k * groups : base + (k + 1) * groups, :] = (
            sums[k * groups : (k + 1) * groups] / mass_sum
        )
    rows_out[base + 3 * groups : base + 4 * groups, :] = table
    coords = [rows_out[k * tiles : (k + 1) * tiles, :] - 0.5 for k in range(3)]
    store_rows(near, near_rows(coords, 1.0))
    for t in range(tiles):
        near_out[t] = near[t].T.astype(BF16)


def pair_kernel(tiles, groups, entries, sources, first, *refs):
    signs, lists, own, near = refs[:4]
    cells = refs[4 : 4 + sources]
    rest = refs[4 + sources :]
    before = None if first else rest[0]
    out, far, even, odd, total = rest[0 if first else 1 :]
    count = len(entries)
    height = 4 * (tiles + groups)
    columns = []
    for e, (source, cell, steps) in enumerate(entries):
        step = [steps[k] * signs[k] for k in range(3)]
        columns.append(9 * (step[0] + 1) + 3 * (step[1] + 1) + (step[2] + 1))
        base = cell * height
        coords = [
            cells[source][base + k * tiles : base + (k + 1) * tiles, :]
            + (step[k].astype(F32) - 0.5)
            for k in range(3)
        ]
        charged = cells[source][base + 3 * tiles : base + 4 * tiles, :]
        store_rows(far.at[e], far_rows(coords, SOFT_CORE) + coords + [charged])

    def distances(t, into):
        lhs = near[t]
        for e in range(0, count, 2):
            members = range(e, min(e + 2, count))
            rhs = [far[m, lists[t, columns[m]] - tiles * columns[m]].astype(BF16) for m in members]
            rhs = jnp.concatenate(rhs, axis=1) if len(rhs) > 1 else rhs[0]
            into[:, e * LANES : e * LANES + rhs.shape[1]] = jnp.dot(
                lhs, rhs, preferred_element_type=F32
            )

    def strengths(t, dist):
        block = 32
        for i in range(0, LANES, block):
            at = slice(i, i + block)
            acc = [jnp.zeros((block, LANES), F32)] * 4
            for e in range(count):
                k = lists[t, columns[e]] - tiles * columns[e]
                inv = lax.rsqrt(dist[at, e * LANES : (e + 1) * LANES])
                s = inv * inv * inv * far[e, k, 27:28, :]
                acc[3] = acc[3] + s
                for d in range(3):
                    acc[d] = acc[d] + s * far[e, k, 24 + d : 25 + d, :]
            for d in range(4):
                total[d, at, :] = acc[d]
        sums = [jnp.sum(total[d].T, axis=0, keepdims=True) for d in range(4)]
        scale = own[pl.ds(3 * tiles + t, 1), :]
        for d in range(3):
            here = own[pl.ds(d * tiles + t, 1), :] - 0.5
            force = scale * (here * sums[3] - sums[d])
            if before is not None:
                force = force + before[pl.ds(d * tiles + t, 1), :]
            out[pl.ds(d * tiles + t, 1), :] = force

    distances(0, even)

    def two_tiles(step, carry):
        t = 2 * step
        distances(t + 1, odd)
        strengths(t, even)
        distances(jnp.minimum(t + 2, tiles - 1), even)
        strengths(t + 1, odd)
        return carry

    lax.fori_loop(0, tiles // 2, two_tiles, 0)


def final_kernel(tiles, groups, entries, sources, *refs):
    signs, bead_lists, own, mass_sum_ref, atomic, mass, label_ref, leave_ref = refs[:8]
    cells = refs[8 : 8 + sources]
    forces_out, record_out, hot, leave_hot, far, near, nearest, dist, total, coarse = refs[
        8 + sources :
    ]
    listed = bead_lists.shape[1]
    height = 4 * (tiles + groups)
    for source, cell, steps in entries:
        step = [steps[k] * signs[k] for k in range(3)]
        column = 9 * (step[0] + 1) + 3 * (step[1] + 1) + (step[2] + 1)
        base = cell * height + 4 * tiles
        coords = [
            cells[source][base + k * groups : base + (k + 1) * groups, :]
            + (step[k].astype(F32) - 0.5)
            for k in range(3)
        ]
        weight = cells[source][base + 3 * groups : base + 4 * groups, :]
        store_rows(far.at[pl.ds(column * groups, groups)], far_rows(coords, 0.0) + coords + [weight])
    base = 4 * tiles
    coords = [own[base + k * groups : base + (k + 1) * groups, :] - 0.5 for k in range(3)]
    own_weight = own[base + 3 * groups : base + 4 * groups, :]
    store_rows(near, near_rows(coords, -1.0 / SIGMA_SQ) + [own_weight])
    for b in range(groups):
        nearest[b] = near[b].T

    def one_tile(b, carry):
        column = lax.broadcasted_iota(jnp.int32, (LANES, ROWS), 1)
        lhs = jnp.where(column < 24, nearest[b], 0.0).astype(BF16)
        for e in range(listed):
            rhs = far[bead_lists[b, e]].astype(BF16)
            dist[:, e * LANES : (e + 1) * LANES] = jnp.dot(lhs, rhs, preferred_element_type=F32)
        block = 32
        for i in range(0, LANES, block):
            at = slice(i, i + block)
            acc = [jnp.zeros((block, LANES), F32)] * 4
            here = jnp.broadcast_to(nearest[b, at, 24:25], (block, LANES))
            for e in range(listed):
                k = bead_lists[b, e]
                s = jnp.exp(dist[at, e * LANES : (e + 1) * LANES]) * (
                    EPS_COARSE - here * (EPS_COARSE * far[k, 27:28, :])
                )
                acc[3] = acc[3] + s
                for d in range(3):
                    acc[d] = acc[d] + s * far[k, 24 + d : 25 + d, :]
            for d in range(4):
                total[d, at, :] = acc[d]
        sums = [jnp.sum(total[d].T, axis=0, keepdims=True) for d in range(4)]
        for d in range(3):
            centre = own[pl.ds(base + d * groups + b, 1), :] - 0.5
            coarse[pl.ds(d * groups + b, 1), :] = centre * sums[3] - sums[d]
        return carry

    lax.fori_loop(0, groups, one_tile, 0)

    one_hot(label_ref, hot, tiles)
    label = label_ref[...]
    mass_sum = mass_sum_ref[...]
    scaled = coarse[...] / jnp.concatenate([mass_sum] * 3, axis=0)
    spread = gather_rows(scaled, label, hot[...], groups)
    forces = []
    for d in range(3):
        flat = jnp.concatenate(
            [atomic[d * tiles + t : d * tiles + t + 1, :] for t in range(tiles)], axis=1
        )
        forces.append(flat + mass[...] * spread[d])
        forces_out[d : d + 1, :] = forces[d]
    molecule = sum_rows(forces, label, hot[...], groups)
    table = jnp.concatenate(
        [own[base : base + 3 * groups, :], molecule, own_weight, mass_sum], axis=0
    )
    leavers = leave_ref.shape[1] // 2
    one_hot(leave_ref, leave_hot, leave_ref.shape[1] // LANES)
    picked = gather_rows(table, leave_ref[...], leave_hot[...], groups)
    for side, shift in ((0, -1.0), (1, 1.0)):
        for f in range(8):
            row = picked[f][:, side * leavers : (side + 1) * leavers]
            record_out[side, f : f + 1, :] = row + shift if f == 0 else row


def exchange(x, axis):
    n = lax.axis_size(axis)
    if n == 1:
        return [(x, 1), (x, -1)]
    if n == 2:
        other = lax.ppermute(x, axis, [(0, 1), (1, 0)])
        return [(other, 1), (other, -1)]
    if n % 2 == 0:
        inner = [(i, i ^ 1) for i in range(n)]
        outer = [(i, ((i + 1) ^ 1) - 1) for i in range(n)]
        outer = [(i, (j + n) % n) for i, j in outer]
        second = lax.ppermute(x, axis, outer)
        first = lax.ppermute(x, axis, inner)
        return [(first, 1), (second, -1)]
    up = [(i, (i + 1) % n) for i in range(n)]
    down = [(j, i) for i, j in up]
    return [(lax.ppermute(x, axis, down), 1), (lax.ppermute(x, axis, up), -1)]


def sign_of(axis):
    n = lax.axis_size(axis)
    if n > 2 and n % 2 == 0:
        return 1 - 2 * lax.rem(lax.axis_index(axis), 2)
    return jnp.int32(1)


def per_device(positions, charges, masses, weights, mapping, atom_lists, bead_lists, leaving):
    pos = positions[0, 0, 0]
    charge, mass = charges[0, 0], masses[0, 0]
    weight, label = weights[0, 0], mapping[0, 0]
    lists, beads_listed = atom_lists[0, 0, 0], bead_lists[0, 0, 0]
    atoms, beads = pos.shape[1], weight.shape[1]
    tiles, groups = atoms // LANES, beads // LANES
    height = 4 * (tiles + groups)
    limit = pltpu.CompilerParams(vmem_limit_bytes=48 * 2**20)
    signs = jnp.stack([sign_of("gx"), sign_of("gy"), sign_of("gz")]).astype(jnp.int32)

    own, mass_sum, near = pl.pallas_call(
        prepare_kernel,
        out_shape=(
            jax.ShapeDtypeStruct((height, LANES), F32),
            jax.ShapeDtypeStruct((groups, LANES), F32),
            jax.ShapeDtypeStruct((tiles, LANES, ROWS), BF16),
        ),
        in_specs=[VMEM] * 5,
        out_specs=(VMEM,) * 3,
        scratch_shapes=[
            pltpu.VMEM((LANES, atoms), BF16),
            pltpu.VMEM((tiles, ROWS, LANES), F32),
        ],
        compiler_params=limit,
    )(pos, charge, mass, weight, label)

    def pairs(entries, cells, before):
        count = len(entries)
        extra = [] if before is None else [before]
        args = [signs, lists, own, near, *cells, *extra]
        work = tiles * count * LANES * LANES
        return pl.pallas_call(
            functools.partial(pair_kernel, tiles, groups, entries, len(cells), before is None),
            out_shape=jax.ShapeDtypeStruct((3 * tiles, LANES), F32),
            in_specs=[SMEM, SMEM] + [VMEM] * (len(args) - 2),
            out_specs=VMEM,
            scratch_shapes=[
                pltpu.VMEM((count, tiles, ROWS, LANES), F32),
                pltpu.VMEM((LANES, count * LANES), F32),
                pltpu.VMEM((LANES, count * LANES), F32),
                pltpu.VMEM((4, LANES, LANES), F32),
            ],
            compiler_params=limit,
            cost_estimate=pl.CostEstimate(
                flops=60 * work, bytes_accessed=4 * height * LANES, transcendentals=work
            ),
        )(*args)

    with_y = exchange(own, "gy")
    force = pairs([(0, 0, (0, 0, 0))], [own], None)
    column = jnp.concatenate([own] + [block for block, _ in with_y], axis=0)
    y_steps = [0] + [step for _, step in with_y]
    with_x = exchange(column, "gx")
    force = pairs([(0, c, (0, y_steps[c], 0)) for c in (1, 2)], [column], force)
    if lax.axis_size("gx") <= 2:
        plane = jnp.concatenate([column, with_x[0][0]], axis=0)
        plane_cells = [(c, (0, y_steps[c])) for c in range(3)]
        plane_cells += [(3 + c, (x, y_steps[c])) for c in range(3) for x in (1, -1)]
    else:
        plane = jnp.concatenate([column] + [block for block, _ in with_x], axis=0)
        plane_cells = [(c, (0, y_steps[c])) for c in range(3)]
        plane_cells += [
            (3 + 3 * k + c, (with_x[k][1], y_steps[c])) for c in range(3) for k in range(2)
        ]
    with_z = exchange(plane, "gz")
    force = pairs([(0, c, (x, y, 0)) for c, (x, y) in plane_cells[3:]], [plane], force)
    for block, z in with_z:
        force = pairs([(0, c, (x, y, z)) for c, (x, y) in plane_cells], [block], force)

    sources = [plane] + [block for block, _ in with_z]
    z_steps = [0] + [step for _, step in with_z]
    entries = [(s, c, (x, y, z_steps[s])) for s in range(3) for c, (x, y) in plane_cells]
    listed = beads_listed.shape[1]
    leavers = leaving.shape[4]
    forces, record = pl.pallas_call(
        functools.partial(final_kernel, tiles, groups, entries, len(sources)),
        out_shape=(
            jax.ShapeDtypeStruct((3, atoms), F32),
            jax.ShapeDtypeStruct((2, 8, leavers), F32),
        ),
        in_specs=[SMEM, SMEM] + [VMEM] * (6 + len(sources)),
        out_specs=(VMEM, VMEM),
        scratch_shapes=[
            pltpu.VMEM((LANES, atoms), BF16),
            pltpu.VMEM((LANES, 2 * leavers), BF16),
            pltpu.VMEM((27 * groups, ROWS, LANES), F32),
            pltpu.VMEM((groups, ROWS, LANES), F32),
            pltpu.VMEM((groups, LANES, ROWS), F32),
            pltpu.VMEM((LANES, listed * LANES), F32),
            pltpu.VMEM((4, LANES, LANES), F32),
            pltpu.VMEM((3 * groups, LANES), F32),
        ],
        compiler_params=limit,
    )(
        signs, beads_listed, own, mass_sum, force, mass, label,
        leaving[0, 0, 0].reshape(1, 2 * leavers), *sources,
    )
    n = lax.axis_size("gx")
    if n == 2:
        arrivals = lax.ppermute(record, "gx", [(0, 1), (1, 0)])
    else:
        up = [(i, (i + 1) % n) for i in range(n)]
        down = [(j, i) for i, j in up]
        arrivals = jnp.stack(
            [lax.ppermute(record[0], "gx", up), lax.ppermute(record[1], "gx", down)]
        )
    return (forces[None, None, None], arrivals[None, None, None])


def solution(mesh):
    cell = ("gx", "gy", "gz")
    placed = (
        P(*cell, None, None),
        P(*cell, None),
        P(*cell, None),
        P(*cell, None),
        P(*cell, None),
        P(*cell, None, None),
        P(*cell, None, None),
        P(*cell, None, None),
    )
    return jax.shard_map(
        per_device,
        mesh=mesh,
        in_specs=placed,
        out_specs=(P(*cell, None, None), P(*cell, None, None, None)),
        check_vma=False,
    )
```

time: 111 us -> 55.5 us (0.50)
  other arithmetic: 34.4 us -> 0.08 us
  Pallas kernels: 0 us -> 31.7 us
  matrix products: 19.6 us -> 0 us
  local copies, waits for them, and re-layouts: 21.3 us -> 4.01 us
  starting transfers between devices: 18.7 us -> 10.4 us
  waiting for transfers between devices: 12.9 us -> 8.21 us
  loops' own time: 1.84 us -> 0 us
    pallas_call x0 -> x7, Pallas kernels: none -> 31.7 us  [the longest x5 26.6 us: pairs(): pl.pallas_call(functools.partial(pair_kernel, tiles, groups, entries, len...]
    reduce_sum x40 -> x0, other arithmetic: 24.5 us -> none  [the longest x16 11 us: atom_tile(): return jnp.sum(strength[None] * displace, axis=(2, 3))]
    dot_general x27 -> x0, matrix products: 19.6 us -> none  [the longest x20 9.2 us: one_tile(): jnp.dot(selector, near_flat, precision=exact, preferred_element_type=jnp....]
    eq x21 -> x0, local copies, waits for them, and re-layouts: 13.9 us -> none  [the longest x20 13.9 us: one_tile(): selector = (listed[:, None] == tile_ids[None, :]).astype(jnp.float32)]
    ppermute x14 -> x6, starting transfers between devices: 18.7 us -> 10.4 us  [the longest x2 4.11 us: exchange(): second = lax.ppermute(x, axis, outer)]
    mul x52 -> x0, other arithmetic: 7.83 us -> none  [the longest x16 6.37 us: atom_tile(): (own_rows[3] * own_rows[4])[:, None, None]]
    ppermute x14 -> x6, waiting for transfers between devices: 12.9 us -> 8.21 us  [the longest x1 3.39 us: exchange(): other = lax.ppermute(x, axis, [(0, 1), (1, 0)])]
    unnamed x17 -> x19, local copies, waits for them, and re-layouts: 1.76 us -> 3.99 us
  transfers between devices with their start and end apart: 14 -> 6, of which waited for: 8 -> 3; matrix products, arithmetic and copies ran while one was open for 14% -> 1% of each run, Pallas kernels for 0% -> 35%
where the time goes in v1:
time: 55.5 us; the launch traced here: 55.2 us
  Pallas kernels  31.7 us (57%)
  starting transfers between devices  10.4 us (19%)
  waiting for transfers between devices  8.21 us (15%)
  local copies, waits for them, and re-layouts  4.01 us (7%)
  between operations  0.79 us (1%)
    pallas_call x5, Pallas kernels, pairs(): pl.pallas_call(functools.partial(pair_kernel, tiles, groups, entries, len...  26.6 us
    pallas_call x1, Pallas kernels, per_device(): pl.pallas_call(functools.partial(final_kernel, tiles, groups, entries, le...  4.5 us
    ppermute x2, starting transfers between devices, exchange(): second = lax.ppermute(x, axis, outer)  4.11 us
    unnamed x19, local copies, waits for them, and re-layouts  3.99 us
    ppermute x1, waiting for transfers between devices, exchange(): other = lax.ppermute(x, axis, [(0, 1), (1, 0)])  3.39 us
    ppermute x2, waiting for transfers between devices, exchange(): second = lax.ppermute(x, axis, outer)  3.3 us
    ppermute x2, starting transfers between devices, exchange(): first = lax.ppermute(x, axis, inner)  3.16 us
    ppermute x1, starting transfers between devices, per_device(): arrivals = lax.ppermute(record, 'gx', [(0, 1), (1, 0)])  1.56 us
  transfers between devices with their start and end apart: 6, of which 3 were waited for; matrix products, arithmetic and copies ran while one was open for 1% of the time, Pallas kernels for 35%

profile of v1, /device:TPU:0, one launch (start us, length us, event | category | flops | bytes accessed | tf_op | source)
XLA Modules:
  0.0 55.2 jit_solution(14503302133732902057)
XLA Ops:
  0.6 0.0 copy-start.1
  0.6 0.0 copy-start.3
  0.7 0.8 %copy.13 = f32[1,1,1,3,2048]{4,3,2,1,0:T(4,128)S(1)} copy(f32[1,1,1,3,2048]{4,2,3,1,0:T(1,128)} %param.8) | data formatting | bytes 49152
  1.4 0.0 copy-start
  1.5 0.7 %copy-done = f32[1,1,1,2048]{3,2,1,0:T(1,128)S(1)} copy-done((f32[1,1,1,2048]{3,2,1,0:T(1,128)S(1)}, f32[1,1,1,2048]{3,2,1,0:T(1,128)}, u32[]{:S(2)}) %copy-start) | copy-done | bytes 8216
  2.1 0.6 %shard_map.95 = (f32[80,128]{1,0:T(8,128)S(1)}, f32[4,128]{1,0:T(4,128)S(1)}, bf16[16,128,32]{2,1,0:T(8,128)(2,1)S(1)}) custom-call(f32[3,2048]{1,0:T(4,128)S(1)} %bitcast.14, f32[1,2048]{1,0:T(1,128)S(1)} %bitcast.25, f32[1,2048]{1,0:T(1,128)S(1)} %bitcast.15, f32[1,512]{1,0:T(1,128)S(1)} %bitcast.27, s32[1,2048]{1,0:T(1,128)S(1)} %bitcast.17), custom_call_target="tpu_custom_call" | custom-call | tf_op jit(solution)/shard_map/pallas_call | solution.py:312
  2.7 3.1 %collective-permute-start = (f32[80,128]{1,0:T(8,128)S(1)}, f32[80,128]{1,0:T(8,128)S(1)}, u32[]{:S(2)}, u32[]{:S(2)}) collective-permute-start(f32[80,128]{1,0:T(8,128)S(1)} %get-tuple-element.7.refs_2_.refs_4_), channel_id=1, source_target_pairs={{0,4},{4,0},{8,12},{12,8},{1,5},{5,1},{9,13},{13,9},{2,6},{6,2},{1... | collective-permute-start | bytes 122888 | tf_op jit(solution)/shard_map/ppermute | solution.py:287
  5.8 2.5 %collective-permute-start.1 = (f32[80,128]{1,0:T(8,128)S(1)}, f32[80,128]{1,0:T(8,128)S(1)}, u32[]{:S(2)}, u32[]{:S(2)}) collective-permute-start(f32[80,128]{1,0:T(8,128)S(1)} %get-tuple-element.7.refs_2_.refs_4_), channel_id=1, source_target_pairs={{0,12},{4,8},{8,4},{12,0},{1,13},{5,9},{9,5},{13,1},{2,14},{6,10},... | collective-permute-start | bytes 122888 | tf_op jit(solution)/shard_map/ppermute | solution.py:286
  8.3 0.0 collective-permute-done
  8.3 3.3 %collective-permute-done.1 = f32[80,128]{1,0:T(8,128)S(1)} collective-permute-done((f32[80,128]{1,0:T(8,128)S(1)}, f32[80,128]{1,0:T(8,128)S(1)}, u32[]{:S(2)}, u32[]{:S(2)}) %collective-permute-start.1) | collective-permute-done | bytes 40992 | tf_op jit(solution)/shard_map/ppermute | solution.py:286
  11.6 1.6 %collective-permute-start.2 = (f32[240,128]{1,0:T(8,128)S(1)}, f32[240,128]{1,0:T(8,128)S(1)}, u32[]{:S(2)}, u32[]{:S(2)}) collective-permute-start(f32[240,128]{1,0:T(8,128)S(1)} %get-tuple-element.14.refs_4_), channel_id=1, source_target_pairs={{0,16},{16,0},{1,17},{17,1},{2,18},{18,2},{3,19},{19,3},{4,20},{20... | collective-permute-start | bytes 368648 | tf_op jit(solution)/shard_map/ppermute | solution.py:280
  13.2 3.4 %collective-permute-done.2 = f32[240,128]{1,0:T(8,128)S(1)} collective-permute-done((f32[240,128]{1,0:T(8,128)S(1)}, f32[240,128]{1,0:T(8,128)S(1)}, u32[]{:S(2)}, u32[]{:S(2)}) %collective-permute-start.2) | collective-permute-done | bytes 122912 | tf_op jit(solution)/shard_map/ppermute | solution.py:280
  16.6 0.1 collective-permute-start.4
  16.7 1.6 %collective-permute-start.3 = (f32[480,128]{1,0:T(8,128)S(1)}, f32[480,128]{1,0:T(8,128)S(1)}, u32[]{:S(2)}, u32[]{:S(2)}) collective-permute-start(f32[480,128]{1,0:T(8,128)S(1)} %constant_dynamic-update-slice_fusion.3.refs_4_.refs_8_), channel_id=1, source_target_pairs={{0,3},{1,2},{2,1},{3,0},{4,7},{5,6},{6,5},{7,4},{8,11},{9,10},{10,... | collective-permute-start | bytes 737288 | tf_op jit(solution)/shard_map/ppermute | solution.py:286
  18.3 0.1 pad_add_fusion.refs_0_
  18.4 0.6 %copy-done.2 = s32[1,1,1,16,27]{4,3,2,1,0:T(8,128)S(1)} copy-done((s32[1,1,1,16,27]{4,3,2,1,0:T(8,128)S(1)}, s32[1,1,1,16,27]{4,3,2,1,0:T(8,128)}, u32[]{:S(2)}) %copy-start.2) | copy-done | bytes 1752
  19.0 3.3 %shard_map.96.refs_5_ = f32[48,128]{1,0:T(8,128)S(1)} custom-call(s32[3]{0:T(128)S(1)} %pad_add_fusion.refs_0_, s32[16,27]{1,0:T(8,128)S(1)} %bitcast.20, f32[80,128]{1,0:T(8,128)S(1)} %get-tuple-element.7.refs_2_.refs_4_, bf16[16,128,32]{2,1,0:T(8,128)(2,1)S(1)} %get-tuple-element.9.refs_3_, f32[80,128]{1,0:T(8,128)S(1)} %get-tuple-element.7.refs_2_.refs_4_), custom_call_target="tpu_custom_call" | custom-call | flops 15728640 | bytes 40960 | tf_op jit(solution)/shard_map/pallas_call | solution.py:333
  22.3 3.6 %shard_map.97.refs_5_ = f32[48,128]{1,0:T(8,128)S(1)} custom-call(s32[3]{0:T(128)S(1)} %pad_add_fusion.refs_0_, s32[16,27]{1,0:T(8,128)S(1)} %bitcast.21, f32[80,128]{1,0:T(8,128)S(1)} %get-tuple-element.7.refs_2_.refs_4_, bf16[16,128,32]{2,1,0:T(8,128)(2,1)S(1)} %get-tuple-element.9.refs_3_, f32[240,128]{1,0:T(8,128)S(1)} %get-tuple-element.14.refs_4_, ...), custom_call_target="tpu_custom_call" | custom-call | flops 31457280 | bytes 40960 | tf_op jit(solution)/shard_map/pallas_call | solution.py:333
  25.9 5.3 %shard_map.98.refs_5_ = f32[48,128]{1,0:T(8,128)S(1)} custom-call(s32[3]{0:T(128)S(1)} %pad_add_fusion.refs_0_, s32[16,27]{1,0:T(8,128)S(1)} %bitcast.22, f32[80,128]{1,0:T(8,128)S(1)} %get-tuple-element.7.refs_2_.refs_4_, bf16[16,128,32]{2,1,0:T(8,128)(2,1)S(1)} %get-tuple-element.9.refs_3_, ...), custom_call_target="tpu_custom_call" | custom-call | flops 94371840 | bytes 40960 | tf_op jit(solution)/shard_map/pallas_call | solution.py:333
  31.2 0.0 collective-permute-done.4.refs_4_.refs_9_
  31.2 7.2 %shard_map.99.refs_5_ = f32[48,128]{1,0:T(8,128)S(1)} custom-call(s32[3]{0:T(128)S(1)} %pad_add_fusion.refs_0_, s32[16,27]{1,0:T(8,128)S(1)} %bitcast.23, f32[80,128]{1,0:T(8,128)S(1)} %get-tuple-element.7.refs_2_.refs_4_, bf16[16,128,32]{2,1,0:T(8,128)(2,1)S(1)} %get-tuple-element.9.refs_3_, f32[480,128]{1,0:T(8,128)S(1)} %collective-permute-done.4.refs_4_.refs_9_, ...), custom_call_target="tpu_custom_call" | custom-call | flops 141557760 | bytes 40960 | tf_op jit(solution)/shard_map/pallas_call | solution.py:333
  38.4 0.0 collective-permute-done.3.refs_4_.refs_10_
  38.5 7.2 %shard_map.100.refs_4_ = f32[48,128]{1,0:T(8,128)S(1)} custom-call(s32[3]{0:T(128)S(1)} %pad_add_fusion.refs_0_, s32[16,27]{1,0:T(8,128)S(1)} %bitcast.24, f32[80,128]{1,0:T(8,128)S(1)} %get-tuple-element.7.refs_2_.refs_4_, bf16[16,128,32]{2,1,0:T(8,128)(2,1)S(1)} %get-tuple-element.9.refs_3_, f32[480,128]{1,0:T(8,128)S(1)} %collective-permute-done.3.refs_4_.refs_10_, ...), custom_call_target="tpu_custom_call" | custom-call | flops 141557760 | bytes 40960 | tf_op jit(solution)/shard_map/pallas_call | solution.py:333
  45.7 0.0 copy-start.4
  45.7 0.0 copy-start.6
  45.7 0.7 %copy-done.4 = s32[1,1,1,4,12]{4,3,2,1,0:T(4,128)S(1)} copy-done((s32[1,1,1,4,12]{4,3,2,1,0:T(4,128)S(1)}, s32[1,1,1,4,12]{4,3,2,1,0:T(4,128)}, u32[]{:S(2)}) %copy-start.4) | copy-done | bytes 216
  46.4 0.0 copy-done.6
  46.4 4.5 %shard_map.101 = (f32[3,2048]{1,0:T(4,128)S(1)}, f32[2,8,128]{2,1,0:T(8,128)S(1)}) custom-call(s32[3]{0:T(128)S(1)} %pad_add_fusion.refs_0_, s32[4,12]{1,0:T(4,128)S(1)} %bitcast.26, f32[80,128]{1,0:T(8,128)S(1)} %get-tuple-element.7.refs_2_.refs_4_, f32[4,128]{1,0:T(4,128)S(1)} %get-tuple-element.8.refs_3_, f32[48,128]{1,0:T(8,128)S(1)} %shard_map.100.refs_4_, ...), custom_call_target="tpu_custom_call" | custom-call | tf_op jit(solution)/shard_map/pallas_call | solution.py:376
  50.9 1.6 %collective-permute-start.5 = (f32[2,8,128]{2,1,0:T(8,128)S(1)}, f32[2,8,128]{2,1,0:T(8,128)S(1)}, u32[]{:S(2)}, u32[]{:S(2)}) collective-permute-start(f32[2,8,128]{2,1,0:T(8,128)S(1)} %get-tuple-element.11), channel_id=1, source_target_pairs={{0,16},{16,0},{1,17},{17,1},{2,18},{18,2},{3,19},{19,3},{4,20},{20... | collective-permute-start | bytes 24584 | tf_op jit(solution)/shard_map/ppermute | solution.py:401
  52.5 0.6 %copy.10 = f32[1,1,1,3,2048]{4,2,3,1,0:T(1,128)} copy(f32[1,1,1,3,2048]{4,3,2,1,0:T(4,128)S(1)} %bitcast.19) | data formatting | bytes 49152
  53.1 1.5 %collective-permute-done.5 = f32[2,8,128]{2,1,0:T(8,128)S(1)} collective-permute-done((f32[2,8,128]{2,1,0:T(8,128)S(1)}, f32[2,8,128]{2,1,0:T(8,128)S(1)}, u32[]{:S(2)}, u32[]{:S(2)}) %collective-permute-start.5) | collective-permute-done | bytes 8224 | tf_op jit(solution)/shard_map/ppermute | solution.py:401
  54.6 0.6 %copy.20 = f32[1,1,1,2,8,128]{5,4,3,2,1,0:T(8,128)} copy(f32[1,1,1,2,8,128]{5,4,3,2,1,0:T(8,128)S(1)} %bitcast.29) | data formatting | bytes 16384
  (9 shorter events, 0.0 us)
Async XLA Ops:
  0.6 0.8 %copy-start.1 = (s32[1,1,1,2048]{3,2,1,0:T(1,128)S(1)}, s32[1,1,1,2048]{3,2,1,0:T(1,128)}, u32[]{:S(2)}) copy-start(s32[1,1,1,2048]{3,2,1,0:T(1,128)} %param.12) | copy-start | bytes 24580
  0.6 0.8 %copy-start.3 = (f32[1,1,1,2048]{3,2,1,0:T(1,128)S(1)}, f32[1,1,1,2048]{3,2,1,0:T(1,128)}, u32[]{:S(2)}) copy-start(f32[1,1,1,2048]{3,2,1,0:T(1,128)} %param.9) | copy-start | bytes 24580
  0.7 0.8 %copy-start.5 = (f32[1,1,1,512]{3,2,1,0:T(1,128)S(1)}, f32[1,1,1,512]{3,2,1,0:T(1,128)}, u32[]{:S(2)}) copy-start(f32[1,1,1,512]{3,2,1,0:T(1,128)} %param.11) | copy-start | bytes 6148
  1.4 0.7 %copy-start = (f32[1,1,1,2048]{3,2,1,0:T(1,128)S(1)}, f32[1,1,1,2048]{3,2,1,0:T(1,128)}, u32[]{:S(2)}) copy-start(f32[1,1,1,2048]{3,2,1,0:T(1,128)} %param.10) | copy-start | bytes 24580
  2.7 5.6 %collective-permute-start = (f32[80,128]{1,0:T(8,128)S(1)}, f32[80,128]{1,0:T(8,128)S(1)}, u32[]{:S(2)}, u32[]{:S(2)}) collective-permute-start(f32[80,128]{1,0:T(8,128)S(1)} %get-tuple-element.7.refs_2_.refs_4_), channel_id=1, source_target_pairs={{0,4},{4,0},{8,12},{12,8},{1,5},{5,1},{9,13},{13,9},{2,6},{6,2},{1... | collective-permute-start | bytes 122888 | tf_op jit(solution)/shard_map/ppermute | solution.py:287
  5.8 5.8 %collective-permute-start.1 = (f32[80,128]{1,0:T(8,128)S(1)}, f32[80,128]{1,0:T(8,128)S(1)}, u32[]{:S(2)}, u32[]{:S(2)}) collective-permute-start(f32[80,128]{1,0:T(8,128)S(1)} %get-tuple-element.7.refs_2_.refs_4_), channel_id=1, source_target_pairs={{0,12},{4,8},{8,4},{12,0},{1,13},{5,9},{9,5},{13,1},{2,14},{6,10},... | collective-permute-start | bytes 122888 | tf_op jit(solution)/shard_map/ppermute | solution.py:286
  11.6 4.9 %collective-permute-start.2 = (f32[240,128]{1,0:T(8,128)S(1)}, f32[240,128]{1,0:T(8,128)S(1)}, u32[]{:S(2)}, u32[]{:S(2)}) collective-permute-start(f32[240,128]{1,0:T(8,128)S(1)} %get-tuple-element.14.refs_4_), channel_id=1, source_target_pairs={{0,16},{16,0},{1,17},{17,1},{2,18},{18,2},{3,19},{19,3},{4,20},{20... | collective-permute-start | bytes 368648 | tf_op jit(solution)/shard_map/ppermute | solution.py:280
  16.6 14.6 %collective-permute-start.4 = (f32[480,128]{1,0:T(8,128)S(1)}, f32[480,128]{1,0:T(8,128)S(1)}, u32[]{:S(2)}, u32[]{:S(2)}) collective-permute-start(f32[480,128]{1,0:T(8,128)S(1)} %constant_dynamic-update-slice_fusion.3.refs_4_.refs_8_), channel_id=1, source_target_pairs={{0,1},{1,0},{2,3},{3,2},{4,5},{5,4},{6,7},{7,6},{8,9},{9,8},{10,11... | collective-permute-start | bytes 737288 | tf_op jit(solution)/shard_map/ppermute | solution.py:287
  16.7 21.8 %collective-permute-start.3 = (f32[480,128]{1,0:T(8,128)S(1)}, f32[480,128]{1,0:T(8,128)S(1)}, u32[]{:S(2)}, u32[]{:S(2)}) collective-permute-start(f32[480,128]{1,0:T(8,128)S(1)} %constant_dynamic-update-slice_fusion.3.refs_4_.refs_8_), channel_id=1, source_target_pairs={{0,3},{1,2},{2,1},{3,0},{4,7},{5,6},{6,5},{7,4},{8,11},{9,10},{10,... | collective-permute-start | bytes 737288 | tf_op jit(solution)/shard_map/ppermute | solution.py:286
  18.3 0.7 %copy-start.2 = (s32[1,1,1,16,27]{4,3,2,1,0:T(8,128)S(1)}, s32[1,1,1,16,27]{4,3,2,1,0:T(8,128)}, u32[]{:S(2)}) copy-start(s32[1,1,1,16,27]{4,3,2,1,0:T(8,128)} %param.13) | copy-start | bytes 5188
  45.7 0.7 %copy-start.4 = (s32[1,1,1,4,12]{4,3,2,1,0:T(4,128)S(1)}, s32[1,1,1,4,12]{4,3,2,1,0:T(4,128)}, u32[]{:S(2)}) copy-start(s32[1,1,1,4,12]{4,3,2,1,0:T(4,128)} %param.14) | copy-start | bytes 580
  45.7 0.7 %copy-start.6 = (s32[1,1,1,2,128]{4,3,2,1,0:T(2,128)S(1)}, s32[1,1,1,2,128]{4,3,2,1,0:T(2,128)}, u32[]{:S(2)}) copy-start(s32[1,1,1,2,128]{4,3,2,1,0:T(2,128)} %param.15) | copy-start | bytes 3076
  50.9 3.7 %collective-permute-start.5 = (f32[2,8,128]{2,1,0:T(8,128)S(1)}, f32[2,8,128]{2,1,0:T(8,128)S(1)}, u32[]{:S(2)}, u32[]{:S(2)}) collective-permute-start(f32[2,8,128]{2,1,0:T(8,128)S(1)} %get-tuple-element.11), channel_id=1, source_target_pairs={{0,16},{16,0},{1,17},{17,1},{2,18},{18,2},{3,19},{19,3},{4,20},{20... | collective-permute-start | bytes 24584 | tf_op jit(solution)/shard_map/ppermute | solution.py:401

commit v2 on v1

v2 whole, which is shorter than its diff:
```python
import functools
import math

import jax
import jax.numpy as jnp
from jax import lax
from jax.experimental import pallas as pl
from jax.experimental.pallas import tpu as pltpu
from jax.sharding import PartitionSpec as P

SOFT_CORE = 0.01
EPS_COARSE = 2.0
SIGMA_SQ = 0.25
LANES = 128
ROWS = 32
PARTS = 4
F32, BF16 = jnp.float32, jnp.bfloat16
VMEM = pl.BlockSpec(memory_space=pltpu.VMEM)
SMEM = pl.BlockSpec(memory_space=pltpu.SMEM)
CONTRACT_LANES = (((1,), (1,)), ((), ()))


def split3(v):
    high = v.astype(BF16).astype(F32)
    rest = v - high
    mid = rest.astype(BF16).astype(F32)
    return high, mid, rest - mid


def far_rows(coords, soft):
    parts = [split3(v) for v in coords]
    norm = coords[0] * coords[0] + coords[1] * coords[1] + (coords[2] * coords[2] + soft)
    nh, nm, nl = split3(norm)
    one = jnp.ones_like(norm)
    rows = [p[0] for p in parts] + [p[1] for p in parts] + [nh, nm]
    return rows + [p[2] for p in parts] + [nl, one, one, one, jnp.zeros_like(one)]


def near_rows(coords, scale):
    parts = [[-2.0 * scale * part for part in split3(v)] for v in coords]
    norm = scale * (coords[0] * coords[0] + coords[1] * coords[1] + coords[2] * coords[2])
    one, zero = jnp.full_like(norm, scale), jnp.zeros_like(norm)
    h, m, l = ([p[k] for p in parts] for k in range(3))
    rows = h + h + [one, one] + m + m + [zero, zero] + l + l + [zero, zero]
    return rows + h + [one] + list(split3(norm)) + [zero]


def picked_rows(far, k, stride):
    first = far[pl.ds(k, 8, stride=stride), :]
    last = far[pl.ds(k + 8 * stride, 8, stride=stride), :]
    return jnp.concatenate([first, first, first, last], axis=0).astype(BF16)


def one_hot(label_ref, out_ref, tiles):
    ids = lax.broadcasted_iota(jnp.int32, (LANES, LANES), 0)
    for t in range(tiles):
        at = slice(t * LANES, (t + 1) * LANES)
        low = lax.rem(label_ref[:, at], LANES)
        out_ref[:, at] = jnp.where(ids == low, 1.0, 0.0).astype(BF16)


def high_mask(label, groups, repeat):
    ids = lax.broadcasted_iota(jnp.int32, (groups, label.shape[1]), 0)
    hit = (ids == label // LANES).astype(F32)
    return jnp.concatenate([hit] * repeat, axis=0)


def stacked3(v):
    return jnp.concatenate(list(split3(v)), axis=0).astype(BF16)


def fold3(v):
    n = v.shape[0] // 3
    return v[:n] + v[n : 2 * n] + v[2 * n :]


def gather_rows(table, label, hot, groups):
    features = table.shape[0] // groups
    picked = fold3(jnp.dot(stacked3(table), hot, preferred_element_type=F32))
    picked = picked * high_mask(label, groups, features)
    return [
        jnp.sum(picked[f * groups : (f + 1) * groups], axis=0, keepdims=True)
        for f in range(features)
    ]


def sum_rows(values, label, hot, groups):
    spread = jnp.concatenate([jnp.broadcast_to(v, (groups, v.shape[1])) for v in values], axis=0)
    spread = spread * high_mask(label, groups, len(values))
    return fold3(
        lax.dot_general(stacked3(spread), hot, CONTRACT_LANES, preferred_element_type=F32)
    )


def flat_row(ref, first, tiles):
    return jnp.concatenate([ref[first + t : first + t + 1, :] for t in range(tiles)], axis=1)


def signs_here():
    return [sign_of(axis) for axis in ("gx", "gy", "gz")]


def column_of(step):
    return 9 * (step[0] + 1) + 3 * (step[1] + 1) + (step[2] + 1)


def as_float(step):
    return float(step) if isinstance(step, int) else step.astype(F32)


def pair_plan(tiles, count):
    held, ahead = (8, 6) if count == 1 else (8, 4) if count == 2 else (2, 1)
    unroll = max(held, 4)
    if tiles % unroll:
        held, unroll, ahead = 2, 2, 1
    return held, unroll, ahead


def prepare_kernel(
    label_ref, mass, pos, weight, charge, rows_out, mass_out, near_out, hot, near
):
    beads = weight.shape[1]
    tiles, groups = pos.shape[1] // LANES, beads // LANES
    one_hot(label_ref, hot, tiles)
    label = label_ref[...]
    m = mass[...]
    values = [m * pos[k : k + 1, :] for k in range(3)] + [m]
    sums = sum_rows(values, label, hot[...], groups)
    mass_sum = sums[3 * groups :]
    mass_out[...] = mass_sum
    table = jnp.concatenate(
        [weight[:, g * LANES : (g + 1) * LANES] for g in range(groups)], axis=0
    )
    charged = charge[...] * gather_rows(table, label, hot[...], groups)[0]
    for t in range(tiles):
        at = slice(t * LANES, (t + 1) * LANES)
        for k in range(3):
            rows_out[k * tiles + t : k * tiles + t + 1, :] = pos[k : k + 1, at]
        rows_out[3 * tiles + t : 3 * tiles + t + 1, :] = charged[:, at]
    base = 4 * tiles
    for k in range(3):
        rows_out[base + k * groups : base + (k + 1) * groups, :] = (
            sums[k * groups : (k + 1) * groups] / mass_sum
        )
    rows_out[base + 3 * groups : base + 4 * groups, :] = table
    coords = [rows_out[k * tiles : (k + 1) * tiles, :] - 0.5 for k in range(3)]
    for r, row in enumerate(near_rows(coords, 1.0)):
        near[r * tiles : (r + 1) * tiles, :] = row
    for t in range(tiles):
        block = near[pl.ds(t, ROWS, stride=tiles), :]
        near_out[t] = block.T.astype(BF16)


def pair_kernel(tiles, groups, entries, sources, first, last, passed, *refs):
    lists, own, near = refs[:3]
    cells = refs[3 : 3 + sources]
    rest = refs[3 + sources :]
    before = None if first else rest[0]
    rest = rest[0 if first else 1 :]
    for p in range(passed):
        rest[passed + 1 + p][...] = rest[p][...]
    rest = rest[passed : passed + 1] + rest[2 * passed + 1 :]
    out, far, held = rest[:3]
    total = rest[-1] if last else None
    count = len(entries)
    height = 4 * (tiles + groups)
    signs = signs_here()
    columns = []
    for e, (source, cell, steps) in enumerate(entries):
        step = [steps[k] * signs[k] if steps[k] else 0 for k in range(3)]
        columns.append(column_of(step))
        base = cell * height
        coords = [
            cells[source][base + k * tiles : base + (k + 1) * tiles, :]
            + (as_float(step[k]) - 0.5)
            for k in range(3)
        ]
        charged = cells[source][base + 3 * tiles : base + 4 * tiles, :]
        for r, row in enumerate(far_rows(coords, SOFT_CORE) + coords + [charged]):
            far[e, r * tiles : (r + 1) * tiles, :] = row

    def number(t, e):
        return lists[t, columns[e]] - tiles * columns[e]

    def distances(t, into, part=None):
        lhs = near[t]
        starts = list(range(0, count, 2))
        if part is not None:
            starts = starts[part::PARTS]
        for e in starts:
            members = range(e, min(e + 2, count))
            rhs = [
                picked_rows(far.at[m], number(t, m), tiles) for m in members
            ]
            rhs = jnp.concatenate(rhs, axis=1) if len(rhs) > 1 else rhs[0]
            inv = lax.rsqrt(jnp.dot(lhs, rhs, preferred_element_type=F32))
            charged = [far[m, pl.ds(19 * tiles + number(t, m), 1), :] for m in members]
            charged = jnp.concatenate(charged, axis=1) if len(charged) > 1 else charged[0]
            into[:, e * LANES : e * LANES + rhs.shape[1]] = inv * inv * inv * charged

    def strengths(t, dist, part):
        block = LANES // PARTS
        at = slice(part * block, (part + 1) * block)
        if True:
            if before is None:
                acc = [jnp.zeros((block, LANES), F32)] * 4
            else:
                acc = [before[t, d, at, :] for d in range(4)]
            for e in range(count):
                k = number(t, e)
                s = dist[at, e * LANES : (e + 1) * LANES]
                acc[3] = acc[3] + s
                for d in range(3):
                    acc[d] = acc[d] + s * far[e, pl.ds((16 + d) * tiles + k, 1), :]
            for d in range(4):
                if last:
                    total[d, at, :] = acc[d]
                else:
                    out[t, d, at, :] = acc[d]
        if not last or part < PARTS - 1:
            return
        sums = [jnp.sum(total[d].T, axis=0, keepdims=True) for d in range(4)]
        scale = own[pl.ds(3 * tiles + t, 1), :]
        for d in range(3):
            here = own[pl.ds(d * tiles + t, 1), :] - 0.5
            out[pl.ds(d * tiles + t, 1), :] = scale * (here * sums[3] - sums[d])

    buffered, unroll, ahead = pair_plan(tiles, count)
    buffers = [held.at[i] for i in range(buffered)]
    for i in range(ahead):
        distances(jnp.int32(i), buffers[i])

    def some_tiles(step, carry):
        for u in range(unroll):
            t = unroll * step + u
            for part in range(PARTS):
                distances(jnp.minimum(t + ahead, tiles - 1), buffers[(u + ahead) % buffered], part)
                strengths(t, buffers[u % buffered], part)

        return carry

    lax.fori_loop(0, tiles // unroll, some_tiles, 0)


def weight_rows(weight):
    h, m, l = split3(weight)
    return [h, h, h, m, m, l], [h, m, l, h, m, h]


def final_kernel(tiles, groups, entries, sources, *refs):
    lists, own, mass_sum_ref, atomic, mass, label_ref, leave_ref, hot = refs[:8]
    cells = refs[8 : 8 + sources]
    rest = refs[8 + sources :]
    forces_out, record_out, leave_hot, raw, far, near, nearest = rest[:7]
    buffers, (total, coarse) = (rest[7:9], rest[9:11]), rest[11:]
    listed = lists.shape[1]
    height = 4 * (tiles + groups)
    signs = signs_here()
    every = len(entries) * groups
    for source, cell, steps in entries:
        step = [steps[k] * signs[k] if steps[k] else 0 for k in range(3)]
        column = column_of(step)
        base = cell * height + 4 * tiles
        for k in range(4):
            block = cells[source][base + k * groups : base + (k + 1) * groups, :]
            if k < 3:
                block = block + (as_float(step[k]) - 0.5)
            raw[k, pl.ds(column * groups, groups), :] = block
    scale = math.sqrt(math.log2(math.e) / SIGMA_SQ)
    coords = [raw[k] for k in range(3)]
    one, zero = jnp.ones_like(coords[0]), jnp.zeros_like(coords[0])
    plain = coords + weight_rows(raw[3])[0] + [one, zero]
    for r, row in enumerate(far_rows([scale * v for v in coords], 0.0) + plain):
        far[r * every : (r + 1) * every, :] = row
    base = 4 * tiles
    coords = [own[base + k * groups : base + (k + 1) * groups, :] - 0.5 for k in range(3)]
    own_weight = own[base + 3 * groups : base + 4 * groups, :]
    zero = jnp.zeros_like(own_weight)
    factors = [-EPS_COARSE * row for row in weight_rows(own_weight)[1]]
    factors += [zero + EPS_COARSE, zero] + [zero] * 8
    for r, row in enumerate(near_rows([scale * v for v in coords], -1.0) + factors):
        near[r * groups : (r + 1) * groups, :] = row
    for b in range(groups):
        nearest[b] = near[pl.ds(b, ROWS + 16, stride=groups), :].T.astype(BF16)

    def products(b, dist, factor):
        lhs = nearest[b]
        for e in range(0, listed, 2):
            members = [lists[b, m] for m in range(e, min(e + 2, listed))]
            at = slice(e * LANES, (e + len(members)) * LANES)
            rhs = jnp.concatenate([picked_rows(far, k, every) for k in members], axis=1)
            dist[:, at] = jnp.dot(lhs[:, :ROWS], rhs, preferred_element_type=F32)
            rhs = [far[pl.ds(k + 19 * every, 8, stride=every), :] for k in members]
            rhs = jnp.concatenate([jnp.concatenate([r, r], axis=0) for r in rhs], axis=1)
            factor[:, at] = jnp.dot(lhs[:, ROWS:], rhs.astype(BF16), preferred_element_type=F32)

    def strengths(b, dist, factor):
        block = 32
        for i in range(0, LANES, block):
            at = slice(i, i + block)
            acc = [jnp.zeros((block, LANES), F32)] * 4
            for e in range(listed):
                k = lists[b, e]
                lanes = slice(e * LANES, (e + 1) * LANES)
                s = jnp.exp2(dist[at, lanes]) * factor[at, lanes]
                acc[3] = acc[3] + s
                for d in range(3):
                    acc[d] = acc[d] + s * far[pl.ds((16 + d) * every + k, 1), :]
            for d in range(4):
                total[d, at, :] = acc[d]
        sums = [jnp.sum(total[d].T, axis=0, keepdims=True) for d in range(4)]
        for d in range(3):
            centre = own[base + d * groups + b : base + d * groups + b + 1, :] - 0.5
            coarse[d * groups + b : d * groups + b + 1, :] = centre * sums[3] - sums[d]

    products(0, *buffers[0])
    for b in range(groups):
        if b + 1 < groups:
            products(b + 1, *buffers[(b + 1) % 2])
        strengths(b, *buffers[b % 2])

    label = label_ref[...]
    mass_sum = mass_sum_ref[...]
    scaled = coarse[...] / jnp.concatenate([mass_sum] * 3, axis=0)
    spread = gather_rows(scaled, label, hot[...], groups)
    forces = []
    for d in range(3):
        forces.append(flat_row(atomic, d * tiles, tiles) + mass[...] * spread[d])
        for t in range(tiles):
            at = slice(t * LANES, (t + 1) * LANES)
            forces_out[d * tiles + t : d * tiles + t + 1, :] = forces[d][:, at]
    molecule = sum_rows(forces, label, hot[...], groups)
    table = jnp.concatenate(
        [own[base : base + 3 * groups, :], molecule, own_weight, mass_sum], axis=0
    )
    leavers = leave_ref.shape[1] // 2
    one_hot(leave_ref, leave_hot, leave_ref.shape[1] // LANES)
    picked = gather_rows(table, leave_ref[...], leave_hot[...], groups)
    for side, shift in ((0, -1.0), (1, 1.0)):
        for f in range(8):
            row = picked[f][:, side * leavers : (side + 1) * leavers]
            record_out[side, f : f + 1, :] = row + shift if f == 0 else row


def exchange(x, axis):
    n = lax.axis_size(axis)
    if n == 1:
        return [(x, 1), (x, -1)]
    if n == 2:
        other = lax.ppermute(x, axis, [(0, 1), (1, 0)])
        return [(other, 1), (other, -1)]
    if n % 2 == 0:
        inner = [(i, i ^ 1) for i in range(n)]
        outer = [(i, ((i + 1) ^ 1) - 1) for i in range(n)]
        outer = [(i, (j + n) % n) for i, j in outer]
        second = lax.ppermute(x, axis, outer)
        first = lax.ppermute(x, axis, inner)
        return [(first, 1), (second, -1)]
    up = [(i, (i + 1) % n) for i in range(n)]
    down = [(j, i) for i, j in up]
    return [(lax.ppermute(x, axis, down), 1), (lax.ppermute(x, axis, up), -1)]


def sign_of(axis):
    n = lax.axis_size(axis)
    if n > 2 and n % 2 == 0:
        return 1 - 2 * lax.rem(lax.axis_index(axis), 2)
    return jnp.int32(1)


def per_device(positions, charges, masses, weights, mapping, atom_lists, bead_lists, leaving):
    atoms, beads = positions.shape[4], weights.shape[3]
    tiles, groups = atoms // LANES, beads // LANES
    pos = positions[0, 0, 0]
    charge, mass = charges[0, 0], masses[0, 0]
    weight, label = weights[0, 0], mapping[0, 0]
    leavers = leaving.shape[4]
    height = 4 * (tiles + groups)
    limit = pltpu.CompilerParams(vmem_limit_bytes=48 * 2**20)
    inputs = [label, mass, pos, weight, charge]
    lists = atom_lists[0, 0, 0]

    def like(x):
        return jax.ShapeDtypeStruct(x.shape, x.dtype)

    own, mass_sum, near, hot = pl.pallas_call(
        prepare_kernel,
        out_shape=(
            jax.ShapeDtypeStruct((height, LANES), F32),
            jax.ShapeDtypeStruct((groups, LANES), F32),
            jax.ShapeDtypeStruct((tiles, LANES, ROWS), BF16),
            jax.ShapeDtypeStruct((LANES, atoms), BF16),
        ),
        in_specs=[VMEM] * 5,
        out_specs=(VMEM,) * 4,
        scratch_shapes=[pltpu.VMEM((ROWS * tiles, LANES), F32)],
        compiler_params=limit,
    )(*inputs)

    def pairs(lists, entries, cells, before, last=False, passed=()):
        count = len(entries)
        args = [lists, own, near, *cells] + ([] if before is None else [before])
        place = len(args) - 1
        args += passed
        shape = (3 * tiles, LANES) if last else (tiles, 4, LANES, LANES)
        work = tiles * count * LANES * LANES
        return pl.pallas_call(
            functools.partial(
                pair_kernel, tiles, groups, entries, len(cells), before is None, last, len(passed)
            ),
            out_shape=(jax.ShapeDtypeStruct(shape, F32), *[like(x) for x in passed]),
            in_specs=[SMEM] + [VMEM] * (len(args) - 1),
            out_specs=(VMEM,) * (1 + len(passed)),
            scratch_shapes=[
                pltpu.VMEM((count, 20 * tiles, LANES), F32),
                pltpu.VMEM((pair_plan(tiles, count)[0], LANES, count * LANES), F32),
            ]
            + ([pltpu.VMEM((4, LANES, LANES), F32)] if last else []),
            input_output_aliases={} if last or before is None else {place: 0},
            compiler_params=limit,
            cost_estimate=pl.CostEstimate(
                flops=60 * work, bytes_accessed=4 * height * LANES, transcendentals=work
            ),
        )(*args)

    with_y = exchange(own, "gy")
    force, lists = pairs(lists, [(0, 0, (0, 0, 0))], [own], None, passed=[lists])
    column = jnp.concatenate([own] + [block for block, _ in with_y], axis=0)
    column, force = lax.optimization_barrier((column, force))
    y_steps = [0] + [step for _, step in with_y]
    with_x = exchange(column, "gx")
    small = [bead_lists[0, 0, 0], leaving.reshape(1, 2 * leavers)]
    entries = [(0, c, (0, y_steps[c], 0)) for c in (1, 2)]
    force, beads_listed, leaving = pairs(lists, entries, [column], force, passed=small)
    plane_cells = [(c, (0, y_steps[c])) for c in range(3)]
    if lax.axis_size("gx") <= 2:
        plane = jnp.concatenate([column, with_x[0][0]], axis=0)
        plane_cells += [(3 + c, (x, y_steps[c])) for c in range(3) for x in (1, -1)]
    else:
        plane = jnp.concatenate([column] + [block for block, _ in with_x], axis=0)
        plane_cells += [
            (3 + 3 * k + c, (with_x[k][1], y_steps[c])) for c in range(3) for k in range(2)
        ]
    plane, force = lax.optimization_barrier((plane, force))
    with_z = exchange(plane, "gz")
    entries = [(0, c, (x, y, 0)) for c, (x, y) in plane_cells[3:]]
    force = pairs(lists, entries, [plane], force)[0]
    for place, (block, z) in enumerate(with_z):
        entries = [(0, c, (x, y, z)) for c, (x, y) in plane_cells]
        force = pairs(lists, entries, [block], force, place == 1)[0]

    sources = [plane] + [block for block, _ in with_z]
    z_steps = [0] + [step for _, step in with_z]
    entries = [(s, c, (x, y, z_steps[s])) for s in range(3) for c, (x, y) in plane_cells]
    every, listed = len(entries) * groups, beads_listed.shape[1]
    forces, record = pl.pallas_call(
        functools.partial(final_kernel, tiles, groups, entries, len(sources)),
        out_shape=(
            jax.ShapeDtypeStruct((3 * tiles, LANES), F32),
            jax.ShapeDtypeStruct((2, 8, leavers), F32),
        ),
        in_specs=[SMEM] + [VMEM] * (7 + len(sources)),
        out_specs=(VMEM, VMEM),
        scratch_shapes=[
            pltpu.VMEM((LANES, 2 * leavers), BF16),
            pltpu.VMEM((4, every, LANES), F32),
            pltpu.VMEM((27 * every, LANES), F32),
            pltpu.VMEM(((ROWS + 16) * groups, LANES), F32),
            pltpu.VMEM((groups, LANES, ROWS + 16), BF16),
            *[pltpu.VMEM((LANES, listed * LANES), F32)] * 4,
            pltpu.VMEM((4, LANES, LANES), F32),
            pltpu.VMEM((3 * groups, LANES), F32),
        ],
        compiler_params=limit,
    )(beads_listed, own, mass_sum, force, mass, label, leaving, hot, *sources)
    n = lax.axis_size("gx")
    if n == 2:
        arrivals = lax.ppermute(record, "gx", [(0, 1), (1, 0)])
    else:
        up = [(i, (i + 1) % n) for i in range(n)]
        down = [(j, i) for i, j in up]
        arrivals = jnp.stack(
            [lax.ppermute(record[0], "gx", up), lax.ppermute(record[1], "gx", down)]
        )
    return (forces.reshape(1, 1, 1, 3, atoms), arrivals[None, None, None])


def solution(mesh):
    cell = ("gx", "gy", "gz")
    placed = (
        P(*cell, None, None),
        P(*cell, None),
        P(*cell, None),
        P(*cell, None),
        P(*cell, None),
        P(*cell, None, None),
        P(*cell, None, None),
        P(*cell, None, None),
    )
    return jax.shard_map(
        per_device,
        mesh=mesh,
        in_specs=placed,
        out_specs=(P(*cell, None, None), P(*cell, None, None, None)),
        check_vma=False,
    )
```

time: 55.5 us -> 44.8 us (0.81)
  Pallas kernels: 31.7 us -> 23.5 us
  waiting for transfers between devices: 8.21 us -> 4.31 us
  local copies, waits for them, and re-layouts: 4.01 us -> 6.17 us
  starting transfers between devices: 10.4 us -> 9.55 us
    pallas_call x5, Pallas kernels: 26.6 us -> 19.6 us  [pairs(): pl.pallas_call(functools.partial(pair_kernel, tiles, groups, entries, len...]
    ppermute x1, waiting for transfers between devices: 3.39 us -> 0.01 us  [exchange(): other = lax.ppermute(x, axis, [(0, 1), (1, 0)])]
    ppermute x2, waiting for transfers between devices: 3.3 us -> 0.01 us  [exchange(): second = lax.ppermute(x, axis, outer)]
    ppermute x2, starting transfers between devices: 3.16 us -> 0.07 us  [exchange(): first = lax.ppermute(x, axis, inner)]
    ppermute x2, starting transfers between devices: 4.11 us -> 6.75 us  [exchange(): second = lax.ppermute(x, axis, outer)]
    unnamed x19 -> x16, local copies, waits for them, and re-layouts: 3.99 us -> 6.17 us
    ppermute x2, waiting for transfers between devices: 0.01 us -> 1.82 us  [exchange(): first = lax.ppermute(x, axis, inner)]
    pallas_call x1, Pallas kernels: 4.5 us -> 3.47 us  [per_device(): pl.pallas_call(functools.partial(final_kernel, tiles, groups, entries, le...]
  transfers between devices with their start and end apart: 6 -> 6, of which waited for: 3 -> 2; matrix products, arithmetic and copies ran while one was open for 1% -> 0% of each run, Pallas kernels for 35% -> 31%
where the time goes in v2:
time: 44.8 us; the launch traced here: 44.3 us
  Pallas kernels  23.5 us (52%)
  starting transfers between devices  9.55 us (21%)
  local copies, waits for them, and re-layouts  6.17 us (14%)
  waiting for transfers between devices  4.31 us (10%)
  between operations  0.75 us (2%)
    pallas_call x5, Pallas kernels, pairs(): pl.pallas_call(functools.partial(pair_kernel, tiles, groups, entries, len...  19.6 us
    ppermute x2, starting transfers between devices, exchange(): second = lax.ppermute(x, axis, outer)  6.75 us
    unnamed x16, local copies, waits for them, and re-layouts  6.17 us
    pallas_call x1, Pallas kernels, per_device(): pl.pallas_call(functools.partial(final_kernel, tiles, groups, entries, le...  3.47 us
    ppermute x1, waiting for transfers between devices, per_device(): arrivals = lax.ppermute(record, 'gx', [(0, 1), (1, 0)])  2.48 us
    ppermute x2, waiting for transfers between devices, exchange(): first = lax.ppermute(x, axis, inner)  1.82 us
    ppermute x1, starting transfers between devices, exchange(): other = lax.ppermute(x, axis, [(0, 1), (1, 0)])  1.56 us
    ppermute x1, starting transfers between devices, per_device(): arrivals = lax.ppermute(record, 'gx', [(0, 1), (1, 0)])  1.17 us
  transfers between devices with their start and end apart: 6, of which 2 were waited for; matrix products, arithmetic and copies ran while one was open for 0% of the time, Pallas kernels for 31%

profile of v2, /device:TPU:0, one launch (start us, length us, event | category | flops | bytes accessed | tf_op | source)
XLA Modules:
  0.0 44.3 jit_solution(382456201981844478)
XLA Ops:
  0.6 0.8 %copy.17 = f32[1,1,1,3,2048]{4,3,2,1,0:T(4,128)S(1)} copy(f32[1,1,1,3,2048]{4,2,3,1,0:T(1,128)} %param.8) | data formatting | bytes 49152
  1.4 0.0 copy-start.1
  1.4 0.7 %copy-done.1 = s32[1,1,1,2048]{3,2,1,0:T(1,128)S(1)} copy-done((s32[1,1,1,2048]{3,2,1,0:T(1,128)S(1)}, s32[1,1,1,2048]{3,2,1,0:T(1,128)}, u32[]{:S(2)}) %copy-start.1) | copy-done | bytes 8216
  2.1 0.0 copy-start.2
  2.1 0.7 %copy-done.2 = f32[1,1,1,2048]{3,2,1,0:T(1,128)S(1)} copy-done((f32[1,1,1,2048]{3,2,1,0:T(1,128)S(1)}, f32[1,1,1,2048]{3,2,1,0:T(1,128)}, u32[]{:S(2)}) %copy-start.2) | copy-done | bytes 8216
  2.8 0.0 copy-start.3
  2.8 0.7 %copy-done.3 = f32[1,1,1,2048]{3,2,1,0:T(1,128)S(1)} copy-done((f32[1,1,1,2048]{3,2,1,0:T(1,128)S(1)}, f32[1,1,1,2048]{3,2,1,0:T(1,128)}, u32[]{:S(2)}) %copy-start.3) | copy-done | bytes 8216
  3.5 0.0 copy-start.5
  3.5 0.7 %copy-done.5 = f32[1,1,1,512]{3,2,1,0:T(1,128)S(1)} copy-done((f32[1,1,1,512]{3,2,1,0:T(1,128)S(1)}, f32[1,1,1,512]{3,2,1,0:T(1,128)}, u32[]{:S(2)}) %copy-start.5) | copy-done | bytes 2072
  4.2 0.5 %shard_map.95 = (f32[80,128]{1,0:T(8,128)S(1)}, f32[4,128]{1,0:T(4,128)S(1)}, bf16[16,128,32]{2,1,0:T(8,128)(2,1)S(1)}, bf16[128,2048]{1,0:T(8,128)(2,1)S(1)}) custom-call(s32[1,2048]{1,0:T(1,128)S(1)} %bitcast.15, f32[1,2048]{1,0:T(1,128)S(1)} %bitcast.17, f32[3,2048]{1,0:T(4,128)S(1)} %bitcast.12, f32[1,512]{1,0:T(1,128)S(1)} %bitcast.21, ...), custom_call_target="tpu_custom_call" | custom-call | tf_op jit(solution)/shard_map/pallas_call | solution.py:386
  4.6 5.1 %collective-permute-start.1 = (f32[80,128]{1,0:T(8,128)S(1)}, f32[80,128]{1,0:T(8,128)S(1)}, u32[]{:S(2)}, u32[]{:S(2)}) collective-permute-start(f32[80,128]{1,0:T(8,128)S(1)} %get-tuple-element.17.refs_1_.refs_3_), channel_id=1, source_target_pairs={{0,12},{4,8},{8,4},{12,0},{1,13},{5,9},{9,5},{13,1},{2,14},{6,10},... | collective-permute-start | bytes 122888 | tf_op jit(solution)/shard_map/ppermute | solution.py:356
  9.8 0.0 collective-permute-start
  9.8 0.7 %copy-done = s32[1,1,1,16,27]{4,3,2,1,0:T(8,128)S(1)} copy-done((s32[1,1,1,16,27]{4,3,2,1,0:T(8,128)S(1)}, s32[1,1,1,16,27]{4,3,2,1,0:T(8,128)}, u32[]{:S(2)}) %copy-start) | copy-done | bytes 1752
  10.5 1.5 %shard_map.96 = (f32[16,4,128,128]{3,2,1,0:T(8,128)S(1)}, s32[16,27]{1,0:T(8,128)S(1)}) custom-call(s32[16,27]{1,0:T(8,128)S(1)} %bitcast.13, f32[80,128]{1,0:T(8,128)S(1)} %get-tuple-element.17.refs_1_.refs_3_, bf16[16,128,32]{2,1,0:T(8,128)(2,1)S(1)} %get-tuple-element.18.refs_2_, f32[80,128]{1,0:T(8,128)S(1)} %get-tuple-element.17.refs_1_.refs_3_, ...), custom_call_target="tpu_custom_call" | custom-call | flops 15728640 | bytes 40960 | tf_op jit(solution)/shard_map/pallas_call | solution.py:407
  11.9 0.0 collective-permute-done.1
  11.9 1.8 %collective-permute-done = f32[80,128]{1,0:T(8,128)S(1)} collective-permute-done((f32[80,128]{1,0:T(8,128)S(1)}, f32[80,128]{1,0:T(8,128)S(1)}, u32[]{:S(2)}, u32[]{:S(2)}) %collective-permute-start) | collective-permute-done | bytes 40992 | tf_op jit(solution)/shard_map/ppermute | solution.py:357
  13.8 1.6 %collective-permute-start.2 = (f32[240,128]{1,0:T(8,128)S(1)}, f32[240,128]{1,0:T(8,128)S(1)}, u32[]{:S(2)}, u32[]{:S(2)}) collective-permute-start(f32[240,128]{1,0:T(8,128)S(1)} %pad_maximum_fusion.1.refs_3_), channel_id=1, source_target_pairs={{0,16},{16,0},{1,17},{17,1},{2,18},{18,2},{3,19},{19,3},{4,20},{20... | collective-permute-start | bytes 368648 | tf_op jit(solution)/shard_map/ppermute | solution.py:350
  15.3 0.7 %copy-done.4 = s32[1,1,1,4,12]{4,3,2,1,0:T(4,128)S(1)} copy-done((s32[1,1,1,4,12]{4,3,2,1,0:T(4,128)S(1)}, s32[1,1,1,4,12]{4,3,2,1,0:T(4,128)}, u32[]{:S(2)}) %copy-start.4) | copy-done | bytes 216
  16.0 0.7 %copy-done.6 = s32[1,1,1,2,128]{4,3,2,1,0:T(2,128)S(1)} copy-done((s32[1,1,1,2,128]{4,3,2,1,0:T(2,128)S(1)}, s32[1,1,1,2,128]{4,3,2,1,0:T(2,128)}, u32[]{:S(2)}) %copy-start.6) | copy-done | bytes 1048
  16.7 2.3 %shard_map.97 = (f32[16,4,128,128]{3,2,1,0:T(8,128)S(1)}, s32[4,12]{1,0:T(4,128)S(1)}, s32[1,256]{1,0:T(1,128)S(1)}) custom-call(s32[16,27]{1,0:T(8,128)S(1)} %get-tuple-element.19.refs_0_, f32[80,128]{1,0:T(8,128)S(1)} %get-tuple-element.17.refs_1_.refs_3_, bf16[16,128,32]{2,1,0:T(8,128)(2,1)S(1)} %get-tuple-element.18.refs_2_, ...), custom_call_target="tpu_custom_call", output_to_operand_aliasing={{0}: (4, {})} | custom-call | flops 31457280 | bytes 40960 | tf_op jit(solution)/shard_map/pallas_call | solution.py:407
  19.0 0.0 collective-permute-done.2
  19.0 0.1 collective-permute-start.4
  19.1 1.6 %collective-permute-start.3 = (f32[480,128]{1,0:T(8,128)S(1)}, f32[480,128]{1,0:T(8,128)S(1)}, u32[]{:S(2)}, u32[]{:S(2)}) collective-permute-start(f32[480,128]{1,0:T(8,128)S(1)} %pad_maximum_fusion.refs_3_.refs_8_), channel_id=1, source_target_pairs={{0,3},{1,2},{2,1},{3,0},{4,7},{5,6},{6,5},{7,4},{8,11},{9,10},{10,... | collective-permute-start | bytes 737288 | tf_op jit(solution)/shard_map/ppermute | solution.py:356
  20.7 4.2 %shard_map.98.refs_4_ = f32[16,4,128,128]{3,2,1,0:T(8,128)S(1)} custom-call(s32[16,27]{1,0:T(8,128)S(1)} %get-tuple-element.19.refs_0_, f32[80,128]{1,0:T(8,128)S(1)} %get-tuple-element.17.refs_1_.refs_3_, bf16[16,128,32]{2,1,0:T(8,128)(2,1)S(1)} %get-tuple-element.18.refs_2_, ...), custom_call_target="tpu_custom_call", output_to_operand_aliasing={{}: (4, {})} | custom-call | flops 94371840 | bytes 40960 | tf_op jit(solution)/shard_map/pallas_call | solution.py:407
  25.0 0.0 collective-permute-done.4.refs_3_.refs_9_
  25.0 5.7 %shard_map.99.refs_4_ = f32[16,4,128,128]{3,2,1,0:T(8,128)S(1)} custom-call(s32[16,27]{1,0:T(8,128)S(1)} %get-tuple-element.19.refs_0_, f32[80,128]{1,0:T(8,128)S(1)} %get-tuple-element.17.refs_1_.refs_3_, bf16[16,128,32]{2,1,0:T(8,128)(2,1)S(1)} %get-tuple-element.18.refs_2_, ...), custom_call_target="tpu_custom_call", output_to_operand_aliasing={{}: (4, {})} | custom-call | flops 141557760 | bytes 40960 | tf_op jit(solution)/shard_map/pallas_call | solution.py:407
  30.7 0.0 collective-permute-done.3.refs_3_.refs_10_
  30.7 5.9 %shard_map.100.refs_3_ = f32[48,128]{1,0:T(8,128)S(1)} custom-call(s32[16,27]{1,0:T(8,128)S(1)} %get-tuple-element.19.refs_0_, f32[80,128]{1,0:T(8,128)S(1)} %get-tuple-element.17.refs_1_.refs_3_, bf16[16,128,32]{2,1,0:T(8,128)(2,1)S(1)} %get-tuple-element.18.refs_2_, f32[480,128]{1,0:T(8,128)S(1)} %collective-permute-done.3.refs_3_.refs_10_, ...), custom_call_target="tpu_custom_call" | custom-call | flops 141557760 | bytes 40960 | tf_op jit(solution)/shard_map/pallas_call | solution.py:407
  36.6 3.5 %shard_map.101 = (f32[48,128]{1,0:T(8,128)}, f32[2,8,128]{2,1,0:T(8,128)S(1)}) custom-call(s32[4,12]{1,0:T(4,128)S(1)} %get-tuple-element.23.refs_0_, f32[80,128]{1,0:T(8,128)S(1)} %get-tuple-element.17.refs_1_.refs_3_, f32[4,128]{1,0:T(4,128)S(1)} %get-tuple-element.24.refs_2_, f32[48,128]{1,0:T(8,128)S(1)} %shard_map.100.refs_3_, f32[1,2048]{1,0:T(1,128)S(1)} %bitcast.18, ...), custom_call_target="tpu_custom_call" | custom-call | tf_op jit(solution)/shard_map/pallas_call | solution.py:456
  40.1 1.2 %collective-permute-start.5 = (f32[2,8,128]{2,1,0:T(8,128)S(1)}, f32[2,8,128]{2,1,0:T(8,128)S(1)}, u32[]{:S(2)}, u32[]{:S(2)}) collective-permute-start(f32[2,8,128]{2,1,0:T(8,128)S(1)} %get-tuple-element.31), channel_id=1, source_target_pairs={{0,16},{16,0},{1,17},{17,1},{2,18},{18,2},{3,19},{19,3},{4,20},{20... | collective-permute-start | bytes 24584 | tf_op jit(solution)/shard_map/ppermute | solution.py:478
  41.2 2.5 %collective-permute-done.5 = f32[2,8,128]{2,1,0:T(8,128)S(1)} collective-permute-done((f32[2,8,128]{2,1,0:T(8,128)S(1)}, f32[2,8,128]{2,1,0:T(8,128)S(1)}, u32[]{:S(2)}, u32[]{:S(2)}) %collective-permute-start.5) | collective-permute-done | bytes 8224 | tf_op jit(solution)/shard_map/ppermute | solution.py:478
  43.7 0.6 %copy.22 = f32[1,1,1,2,8,128]{5,4,3,2,1,0:T(8,128)} copy(f32[1,1,1,2,8,128]{5,4,3,2,1,0:T(8,128)S(1)} %bitcast.23) | data formatting | bytes 16384
  (5 shorter events, 0.0 us)
Async XLA Ops:
  1.4 0.7 %copy-start.1 = (s32[1,1,1,2048]{3,2,1,0:T(1,128)S(1)}, s32[1,1,1,2048]{3,2,1,0:T(1,128)}, u32[]{:S(2)}) copy-start(s32[1,1,1,2048]{3,2,1,0:T(1,128)} %param.12) | copy-start | bytes 24580
  2.1 0.7 %copy-start.2 = (f32[1,1,1,2048]{3,2,1,0:T(1,128)S(1)}, f32[1,1,1,2048]{3,2,1,0:T(1,128)}, u32[]{:S(2)}) copy-start(f32[1,1,1,2048]{3,2,1,0:T(1,128)} %param.10) | copy-start | bytes 24580
  2.8 0.7 %copy-start.3 = (f32[1,1,1,2048]{3,2,1,0:T(1,128)S(1)}, f32[1,1,1,2048]{3,2,1,0:T(1,128)}, u32[]{:S(2)}) copy-start(f32[1,1,1,2048]{3,2,1,0:T(1,128)} %param.9) | copy-start | bytes 24580
  3.5 0.7 %copy-start.5 = (f32[1,1,1,512]{3,2,1,0:T(1,128)S(1)}, f32[1,1,1,512]{3,2,1,0:T(1,128)}, u32[]{:S(2)}) copy-start(f32[1,1,1,512]{3,2,1,0:T(1,128)} %param.11) | copy-start | bytes 6148
  4.6 7.3 %collective-permute-start.1 = (f32[80,128]{1,0:T(8,128)S(1)}, f32[80,128]{1,0:T(8,128)S(1)}, u32[]{:S(2)}, u32[]{:S(2)}) collective-permute-start(f32[80,128]{1,0:T(8,128)S(1)} %get-tuple-element.17.refs_1_.refs_3_), channel_id=1, source_target_pairs={{0,12},{4,8},{8,4},{12,0},{1,13},{5,9},{9,5},{13,1},{2,14},{6,10},... | collective-permute-start | bytes 122888 | tf_op jit(solution)/shard_map/ppermute | solution.py:356
  9.8 4.0 %collective-permute-start = (f32[80,128]{1,0:T(8,128)S(1)}, f32[80,128]{1,0:T(8,128)S(1)}, u32[]{:S(2)}, u32[]{:S(2)}) collective-permute-start(f32[80,128]{1,0:T(8,128)S(1)} %get-tuple-element.17.refs_1_.refs_3_), channel_id=1, source_target_pairs={{0,4},{4,0},{8,12},{12,8},{1,5},{5,1},{9,13},{13,9},{2,6},{6,2},{1... | collective-permute-start | bytes 122888 | tf_op jit(solution)/shard_map/ppermute | solution.py:357
  9.8 0.7 %copy-start = (s32[1,1,1,16,27]{4,3,2,1,0:T(8,128)S(1)}, s32[1,1,1,16,27]{4,3,2,1,0:T(8,128)}, u32[]{:S(2)}) copy-start(s32[1,1,1,16,27]{4,3,2,1,0:T(8,128)} %param.13) | copy-start | bytes 5188
  13.8 5.2 %collective-permute-start.2 = (f32[240,128]{1,0:T(8,128)S(1)}, f32[240,128]{1,0:T(8,128)S(1)}, u32[]{:S(2)}, u32[]{:S(2)}) collective-permute-start(f32[240,128]{1,0:T(8,128)S(1)} %pad_maximum_fusion.1.refs_3_), channel_id=1, source_target_pairs={{0,16},{16,0},{1,17},{17,1},{2,18},{18,2},{3,19},{19,3},{4,20},{20... | collective-permute-start | bytes 368648 | tf_op jit(solution)/shard_map/ppermute | solution.py:350
  15.3 0.7 %copy-start.4 = (s32[1,1,1,4,12]{4,3,2,1,0:T(4,128)S(1)}, s32[1,1,1,4,12]{4,3,2,1,0:T(4,128)}, u32[]{:S(2)}) copy-start(s32[1,1,1,4,12]{4,3,2,1,0:T(4,128)} %param.14) | copy-start | bytes 580
  16.0 0.7 %copy-start.6 = (s32[1,1,1,2,128]{4,3,2,1,0:T(2,128)S(1)}, s32[1,1,1,2,128]{4,3,2,1,0:T(2,128)}, u32[]{:S(2)}) copy-start(s32[1,1,1,2,128]{4,3,2,1,0:T(2,128)} %param.15) | copy-start | bytes 3076
  19.0 6.0 %collective-permute-start.4 = (f32[480,128]{1,0:T(8,128)S(1)}, f32[480,128]{1,0:T(8,128)S(1)}, u32[]{:S(2)}, u32[]{:S(2)}) collective-permute-start(f32[480,128]{1,0:T(8,128)S(1)} %pad_maximum_fusion.refs_3_.refs_8_), channel_id=1, source_target_pairs={{0,1},{1,0},{2,3},{3,2},{4,5},{5,4},{6,7},{7,6},{8,9},{9,8},{10,11... | collective-permute-start | bytes 737288 | tf_op jit(solution)/shard_map/ppermute | solution.py:357
  19.1 11.6 %collective-permute-start.3 = (f32[480,128]{1,0:T(8,128)S(1)}, f32[480,128]{1,0:T(8,128)S(1)}, u32[]{:S(2)}, u32[]{:S(2)}) collective-permute-start(f32[480,128]{1,0:T(8,128)S(1)} %pad_maximum_fusion.refs_3_.refs_8_), channel_id=1, source_target_pairs={{0,3},{1,2},{2,1},{3,0},{4,7},{5,6},{6,5},{7,4},{8,11},{9,10},{10,... | collective-permute-start | bytes 737288 | tf_op jit(solution)/shard_map/ppermute | solution.py:356
  40.1 3.7 %collective-permute-start.5 = (f32[2,8,128]{2,1,0:T(8,128)S(1)}, f32[2,8,128]{2,1,0:T(8,128)S(1)}, u32[]{:S(2)}, u32[]{:S(2)}) collective-permute-start(f32[2,8,128]{2,1,0:T(8,128)S(1)} %get-tuple-element.31), channel_id=1, source_target_pairs={{0,16},{16,0},{1,17},{17,1},{2,18},{18,2},{3,19},{19,3},{4,20},{20... | collective-permute-start | bytes 24584 | tf_op jit(solution)/shard_map/ppermute | solution.py:478

commit v3 on v2

--- a/solution.py
+++ b/solution.py
@@ -1,4 +1,5 @@
 import functools
+import itertools
 import math
 
 import jax
@@ -16,7 +17,7 @@
 PARTS = 4
 F32, BF16 = jnp.float32, jnp.bfloat16
 VMEM = pl.BlockSpec(memory_space=pltpu.VMEM)
-SMEM = pl.BlockSpec(memory_space=pltpu.SMEM)
+HBM = pl.BlockSpec(memory_space=pltpu.HBM)
 CONTRACT_LANES = (((1,), (1,)), ((), ()))
 
 
@@ -104,6 +105,34 @@
     return 9 * (step[0] + 1) + 3 * (step[1] + 1) + (step[2] + 1)
 
 
+def number_plan(tiles):
+    bits = max((tiles - 1).bit_length(), 1)
+    return bits, min(31 // bits, 9)
+
+
+def place_of(step, tiles):
+    bits, share = number_plan(tiles)
+    order = 3 * (step[0] + 1) + (step[1] + 1)
+    return -(-9 // share) * (step[2] + 1) + order // share, bits * (order % share)
+
+
+def packed_numbers(lists, tiles):
+    numbers = lists - tiles * lax.broadcasted_iota(jnp.int32, lists.shape, 1)
+    for sign, width in zip(signs_here(), (9, 3, 1)):
+        pieces = []
+        for start in range(0, 27, 3 * width):
+            for k in (2, 1, 0):
+                pieces.append(numbers[:, start + k * width : start + (k + 1) * width])
+        numbers = jnp.where(sign < 0, jnp.concatenate(pieces, axis=1), numbers)
+    words = {}
+    for x, y, z in itertools.product((-1, 0, 1), repeat=3):
+        word, shift = place_of((x, y, z), tiles)
+        column = column_of((x, y, z))
+        piece = lax.shift_left(numbers[:, column : column + 1], jnp.int32(shift))
+        words[word] = words[word] + piece if word in words else piece
+    return jnp.concatenate([words[word] for word in sorted(words)], axis=1)
+
+
 def as_float(step):
     return float(step) if isinstance(step, int) else step.astype(F32)
 
@@ -117,25 +146,39 @@
 
 
 def prepare_kernel(
-    label_ref, mass, pos, weight, charge, rows_out, mass_out, near_out, hot, near
+    label_in, mass_in, pos_in, weight_in, charge_in, lists_in, bead_lists_in, leaving_in,
+    rows_out, mass_out, near_out, hot, label_ref, mass, lists_out, bead_lists_out, leaving_out,
+    pos, weight, charge, near, sem,
 ):
+    moves = [
+        (label_in, label_ref), (mass_in, mass), (pos_in, pos), (weight_in, weight),
+        (charge_in, charge), (lists_in, lists_out), (bead_lists_in, bead_lists_out),
+        (leaving_in, leaving_out),
+    ]
+    copies = [pltpu.make_async_copy(a, b, sem.at[i]) for i, (a, b) in enumerate(moves)]
+    for copy in copies:
+        copy.start()
     beads = weight.shape[1]
-    tiles, groups = pos.shape[1] // LANES, beads // LANES
+    tiles, groups = pos.shape[0] // 3, beads // LANES
+    copies[0].wait()
     one_hot(label_ref, hot, tiles)
     label = label_ref[...]
+    copies[1].wait()
+    copies[2].wait()
     m = mass[...]
-    values = [m * pos[k : k + 1, :] for k in range(3)] + [m]
+    values = [m * flat_row(pos, k * tiles, tiles) for k in range(3)] + [m]
     sums = sum_rows(values, label, hot[...], groups)
     mass_sum = sums[3 * groups :]
     mass_out[...] = mass_sum
+    for copy in copies[3:]:
+        copy.wait()
     table = jnp.concatenate(
         [weight[:, g * LANES : (g + 1) * LANES] for g in range(groups)], axis=0
     )
     charged = charge[...] * gather_rows(table, label, hot[...], groups)[0]
+    rows_out[: 3 * tiles, :] = pos[...]
     for t in range(tiles):
         at = slice(t * LANES, (t + 1) * LANES)
-        for k in range(3):
-            rows_out[k * tiles + t : k * tiles + t + 1, :] = pos[k : k + 1, at]
         rows_out[3 * tiles + t : 3 * tiles + t + 1, :] = charged[:, at]
     base = 4 * tiles
     for k in range(3):
@@ -152,7 +195,7 @@
 
 
 def pair_kernel(tiles, groups, entries, sources, first, last, passed, *refs):
-    lists, own, near = refs[:3]
+    numbers, own, near = refs[:3]
     cells = refs[3 : 3 + sources]
     rest = refs[3 + sources :]
     before = None if first else rest[0]
@@ -160,15 +203,18 @@
     for p in range(passed):
         rest[passed + 1 + p][...] = rest[p][...]
     rest = rest[passed : passed + 1] + rest[2 * passed + 1 :]
+    if first:
+        rest[1][...] = packed_numbers(numbers[...], tiles)
+        numbers, rest = rest[1], rest[:1] + rest[2:]
     out, far, held = rest[:3]
     total = rest[-1] if last else None
     count = len(entries)
     height = 4 * (tiles + groups)
     signs = signs_here()
-    columns = []
+    places = []
     for e, (source, cell, steps) in enumerate(entries):
         step = [steps[k] * signs[k] if steps[k] else 0 for k in range(3)]
-        columns.append(column_of(step))
+        places.append(place_of(steps, tiles))
         base = cell * height
         coords = [
             cells[source][base + k * tiles : base + (k + 1) * tiles, :]
@@ -179,10 +225,24 @@
         for r, row in enumerate(far_rows(coords, SOFT_CORE) + coords + [charged]):
             far[e, r * tiles : (r + 1) * tiles, :] = row
 
-    def number(t, e):
-        return lists[t, columns[e]] - tiles * columns[e]
-
-    def distances(t, into, part=None):
+    bits = number_plan(tiles)[0]
+
+    used = sorted({word for word, _ in places})
+
+    def words_of(t):
+        row = numbers[pl.ds(t, 1), :]
+        return tuple(row[0, word] for word in used)
+
+    def numbers_of(words):
+        words = dict(zip(used, words))
+        return [
+            lax.bitwise_and(
+                lax.shift_right_logical(words[word], jnp.int32(shift)), jnp.int32((1 << bits) - 1)
+            )
+            for word, shift in places
+        ]
+
+    def distances(t, into, ks, part=None):
         lhs = near[t]
         starts = list(range(0, count, 2))
         if part is not None:
@@ -190,15 +250,15 @@
         for e in starts:
             members = range(e, min(e + 2, count))
             rhs = [
-                picked_rows(far.at[m], number(t, m), tiles) for m in members
+                picked_rows(far.at[m], ks[m], tiles) for m in members
             ]
             rhs = jnp.concatenate(rhs, axis=1) if len(rhs) > 1 else rhs[0]
             inv = lax.rsqrt(jnp.dot(lhs, rhs, preferred_element_type=F32))
-            charged = [far[m, pl.ds(19 * tiles + number(t, m), 1), :] for m in members]
+            charged = [far[m, pl.ds(19 * tiles + ks[m], 1), :] for m in members]
             charged = jnp.concatenate(charged, axis=1) if len(charged) > 1 else charged[0]
             into[:, e * LANES : e * LANES + rhs.shape[1]] = inv * inv * inv * charged
 
-    def strengths(t, dist, part):
+    def strengths(t, dist, ks, part):
         block = LANES // PARTS
         at = slice(part * block, (part + 1) * block)
         if True:
@@ -207,7 +267,7 @@
             else:
                 acc = [before[t, d, at, :] for d in range(4)]
             for e in range(count):
-                k = number(t, e)
+                k = ks[e]
                 s = dist[at, e * LANES : (e + 1) * LANES]
                 acc[3] = acc[3] + s
                 for d in range(3):
@@ -227,19 +287,24 @@
 
     buffered, unroll, ahead = pair_plan(tiles, count)
     buffers = [held.at[i] for i in range(buffered)]
+    words = [words_of(min(i, tiles - 1)) for i in range(unroll + ahead)]
     for i in range(ahead):
-        distances(jnp.int32(i), buffers[i])
-
-    def some_tiles(step, carry):
+        distances(i, buffers[i], numbers_of(words[i]))
+
+    def some_tiles(step, words):
+        following = [
+            words_of(jnp.minimum(unroll * (step + 1) + ahead + u, tiles - 1)) for u in range(unroll)
+        ]
         for u in range(unroll):
             t = unroll * step + u
+            later = jnp.minimum(t + ahead, tiles - 1)
+            ks, ks_later = numbers_of(words[u]), numbers_of(words[u + ahead])
             for part in range(PARTS):
-                distances(jnp.minimum(t + ahead, tiles - 1), buffers[(u + ahead) % buffered], part)
-                strengths(t, buffers[u % buffered], part)
-
-        return carry
-
-    lax.fori_loop(0, tiles // unroll, some_tiles, 0)
+                distances(later, buffers[(u + ahead) % buffered], ks_later, part)
+                strengths(t, buffers[u % buffered], ks, part)
+        return tuple(words[unroll:]) + tuple(following)
+
+    lax.fori_loop(0, tiles // unroll, some_tiles, tuple(words))
 
 
 def weight_rows(weight):
@@ -248,12 +313,12 @@
 
 
 def final_kernel(tiles, groups, entries, sources, *refs):
-    lists, own, mass_sum_ref, atomic, mass, label_ref, leave_ref, hot = refs[:8]
+    lists_ref, own, mass_sum_ref, atomic, mass, label_ref, leave_ref, hot = refs[:8]
     cells = refs[8 : 8 + sources]
     rest = refs[8 + sources :]
     forces_out, record_out, leave_hot, raw, far, near, nearest = rest[:7]
     buffers, (total, coarse) = (rest[7:9], rest[9:11]), rest[11:]
-    listed = lists.shape[1]
+    lists, listed = lists_ref[...], lists_ref.shape[1]
     height = 4 * (tiles + groups)
     signs = signs_here()
     every = len(entries) * groups
@@ -371,46 +436,57 @@
 def per_device(positions, charges, masses, weights, mapping, atom_lists, bead_lists, leaving):
     atoms, beads = positions.shape[4], weights.shape[3]
     tiles, groups = atoms // LANES, beads // LANES
-    pos = positions[0, 0, 0]
+    pos = positions.reshape(3 * tiles, LANES)
     charge, mass = charges[0, 0], masses[0, 0]
     weight, label = weights[0, 0], mapping[0, 0]
     leavers = leaving.shape[4]
     height = 4 * (tiles + groups)
     limit = pltpu.CompilerParams(vmem_limit_bytes=48 * 2**20)
-    inputs = [label, mass, pos, weight, charge]
-    lists = atom_lists[0, 0, 0]
+    inputs = [
+        label, mass, pos, weight, charge,
+        atom_lists[0, 0, 0], bead_lists[0, 0, 0], leaving.reshape(1, 2 * leavers),
+    ]
 
     def like(x):
         return jax.ShapeDtypeStruct(x.shape, x.dtype)
 
-    own, mass_sum, near, hot = pl.pallas_call(
+    own, mass_sum, near, hot, label, mass, lists, *small = pl.pallas_call(
         prepare_kernel,
         out_shape=(
             jax.ShapeDtypeStruct((height, LANES), F32),
             jax.ShapeDtypeStruct((groups, LANES), F32),
             jax.ShapeDtypeStruct((tiles, LANES, ROWS), BF16),
             jax.ShapeDtypeStruct((LANES, atoms), BF16),
+            like(label),
+            like(mass),
+            *[like(x) for x in inputs[5:]],
         ),
-        in_specs=[VMEM] * 5,
-        out_specs=(VMEM,) * 4,
-        scratch_shapes=[pltpu.VMEM((ROWS * tiles, LANES), F32)],
-        compiler_params=limit,
-    )(*inputs)
+        in_specs=[HBM] * 8,
+        out_specs=(VMEM,) * 9,
+        scratch_shapes=[
+            *[pltpu.VMEM(x.shape, x.dtype) for x in inputs[2:5]],
+            pltpu.VMEM((ROWS * tiles, LANES), F32),
+            pltpu.SemaphoreType.DMA((8,)),
+        ],
+        compiler_params=pltpu.CompilerParams(vmem_limit_bytes=48 * 2**20),
+    )(*[pltpu.with_memory_space_constraint(x, pltpu.HBM) for x in inputs])
 
     def pairs(lists, entries, cells, before, last=False, passed=()):
         count = len(entries)
         args = [lists, own, near, *cells] + ([] if before is None else [before])
         place = len(args) - 1
         args += passed
+        words = jax.ShapeDtypeStruct((tiles, 3 * -(-9 // number_plan(tiles)[1])), jnp.int32)
+        extra = [*passed, words] if before is None else passed
         shape = (3 * tiles, LANES) if last else (tiles, 4, LANES, LANES)
         work = tiles * count * LANES * LANES
         return pl.pallas_call(
             functools.partial(
                 pair_kernel, tiles, groups, entries, len(cells), before is None, last, len(passed)
             ),
-            out_shape=(jax.ShapeDtypeStruct(shape, F32), *[like(x) for x in passed]),
-            in_specs=[SMEM] + [VMEM] * (len(args) - 1),
-            out_specs=(VMEM,) * (1 + len(passed)),
+            out_shape=(jax.ShapeDtypeStruct(shape, F32), *[like(x) for x in extra]),
+            in_specs=[VMEM] * len(args),
+            out_specs=(VMEM,) * (1 + len(extra)),
             scratch_shapes=[
                 pltpu.VMEM((count, 20 * tiles, LANES), F32),
                 pltpu.VMEM((pair_plan(tiles, count)[0], LANES, count * LANES), F32),
@@ -424,12 +500,11 @@
         )(*args)
 
     with_y = exchange(own, "gy")
-    force, lists = pairs(lists, [(0, 0, (0, 0, 0))], [own], None, passed=[lists])
+    force, lists = pairs(lists, [(0, 0, (0, 0, 0))], [own], None)
     column = jnp.concatenate([own] + [block for block, _ in with_y], axis=0)
     column, force = lax.optimization_barrier((column, force))
     y_steps = [0] + [step for _, step in with_y]
     with_x = exchange(column, "gx")
-    small = [bead_lists[0, 0, 0], leaving.reshape(1, 2 * leavers)]
     entries = [(0, c, (0, y_steps[c], 0)) for c in (1, 2)]
     force, beads_listed, leaving = pairs(lists, entries, [column], force, passed=small)
     plane_cells = [(c, (0, y_steps[c])) for c in range(3)]
@@ -459,7 +534,7 @@
             jax.ShapeDtypeStruct((3 * tiles, LANES), F32),
             jax.ShapeDtypeStruct((2, 8, leavers), F32),
         ),
-        in_specs=[SMEM] + [VMEM] * (7 + len(sources)),
+        in_specs=[VMEM] * (8 + len(sources)),
         out_specs=(VMEM, VMEM),
         scratch_shapes=[
             pltpu.VMEM((LANES, 2 * leavers), BF16),

time: 44.8 us -> 39.2 us (0.88)
  local copies, waits for them, and re-layouts: 6.17 us -> 0.6 us
  Pallas kernels: 23.5 us -> 21.2 us
  waiting for transfers between devices: 4.31 us -> 6.59 us
    unnamed x16 -> x1, local copies, waits for them, and re-layouts: 6.17 us -> 0.6 us
    pallas_call x5, Pallas kernels: 19.6 us -> 16.7 us  [pairs(): pl.pallas_call(functools.partial(pair_kernel, tiles, groups, entries, len...]
    ppermute x1, waiting for transfers between devices: 0.01 us -> 1.78 us  [exchange(): other = lax.ppermute(x, axis, [(0, 1), (1, 0)])]
    pallas_call x1, Pallas kernels: 0.48 us -> 1.57 us  [per_device(): pl.pallas_call(prepare_kernel, out_shape=(jax.ShapeDtypeStruct((height, L...]
    ppermute x2, waiting for transfers between devices: 0.01 us -> 0.64 us  [exchange(): second = lax.ppermute(x, axis, outer)]
    pallas_call x1, Pallas kernels: 3.47 us -> 2.87 us  [per_device(): pl.pallas_call(functools.partial(final_kernel, tiles, groups, entries, le...]
  transfers between devices with their start and end apart: 6 -> 6, of which waited for: 2 -> 4; matrix products, arithmetic and copies ran while one was open for 0% -> 0% of each run, Pallas kernels for 31% -> 30%
where the time goes in v3:
time: 39.2 us; the launch traced here: 39 us
  Pallas kernels  21.2 us (54%)
  starting transfers between devices  9.86 us (25%)
  waiting for transfers between devices  6.59 us (17%)
  between operations  0.71 us (2%)
  local copies, waits for them, and re-layouts  0.6 us (2%)
    pallas_call x5, Pallas kernels, pairs(): pl.pallas_call(functools.partial(pair_kernel, tiles, groups, entries, len...  16.7 us
    ppermute x2, starting transfers between devices, exchange(): second = lax.ppermute(x, axis, outer)  6.75 us
    pallas_call x1, Pallas kernels, per_device(): pl.pallas_call(functools.partial(final_kernel, tiles, groups, entries, le...  2.87 us
    ppermute x1, waiting for transfers between devices, per_device(): arrivals = lax.ppermute(record, 'gx', [(0, 1), (1, 0)])  2.17 us
    ppermute x2, waiting for transfers between devices, exchange(): first = lax.ppermute(x, axis, inner)  2 us
    ppermute x1, waiting for transfers between devices, exchange(): other = lax.ppermute(x, axis, [(0, 1), (1, 0)])  1.78 us
    pallas_call x1, Pallas kernels, per_device(): pl.pallas_call(prepare_kernel, out_shape=(jax.ShapeDtypeStruct((height, L...  1.57 us
    ppermute x1, starting transfers between devices, exchange(): other = lax.ppermute(x, axis, [(0, 1), (1, 0)])  1.56 us
  transfers between devices with their start and end apart: 6, of which 4 were waited for; matrix products, arithmetic and copies ran while one was open for 0% of the time, Pallas kernels for 30%

profile of v3, /device:TPU:0, one launch (start us, length us, event | category | flops | bytes accessed | tf_op | source)
XLA Modules:
  0.0 39.0 jit_solution(1127088264103920891)
XLA Ops:
  0.6 1.6 %shard_map.95 = (f32[80,128]{1,0:T(8,128)S(1)}, f32[4,128]{1,0:T(4,128)S(1)}, bf16[16,128,32]{2,1,0:T(8,128)(2,1)S(1)}, bf16[128,2048]{1,0:T(8,128)(2,1)S(1)}, s...) custom-call(s32[1,2048]{1,0:T(1,128)} %bitcast.11, ...), custom_call_target="tpu_custom_call" | custom-call | tf_op jit(solution)/shard_map/pallas_call | solution.py:453
  2.2 5.1 %collective-permute-start.1 = (f32[80,128]{1,0:T(8,128)S(1)}, f32[80,128]{1,0:T(8,128)S(1)}, u32[]{:S(2)}, u32[]{:S(2)}) collective-permute-start(f32[80,128]{1,0:T(8,128)S(1)} %get-tuple-element.23.refs_1_.refs_3_), channel_id=1, source_target_pairs={{0,12},{4,8},{8,4},{12,0},{1,13},{5,9},{9,5},{13,1},{2,14},{6,10},... | collective-permute-start | bytes 122888 | tf_op jit(solution)/shard_map/ppermute | solution.py:421
  7.3 0.0 collective-permute-start
  7.3 1.4 %shard_map.96 = (f32[16,4,128,128]{3,2,1,0:T(8,128)S(1)}, s32[16,6]{1,0:T(8,128)S(1)}) custom-call(s32[16,27]{1,0:T(8,128)S(1)} %get-tuple-element.22.refs_0_, f32[80,128]{1,0:T(8,128)S(1)} %get-tuple-element.23.refs_1_.refs_3_, bf16[16,128,32]{2,1,0:T(8,128)(2,1)S(1)} %get-tuple-element.24.refs_2_, f32[80,128]{1,0:T(8,128)S(1)} %get-tuple-element.23.refs_1_.refs_3_), custom_call_target="tpu_custom_call" | custom-call | flops 15728640 | bytes 40960 | tf_op jit(solution)/shard_map/pallas_call | solution.py:483
  8.7 0.6 %collective-permute-done.1 = f32[80,128]{1,0:T(8,128)S(1)} collective-permute-done((f32[80,128]{1,0:T(8,128)S(1)}, f32[80,128]{1,0:T(8,128)S(1)}, u32[]{:S(2)}, u32[]{:S(2)}) %collective-permute-start.1) | collective-permute-done | bytes 40992 | tf_op jit(solution)/shard_map/ppermute | solution.py:421
  9.3 2.0 %collective-permute-done = f32[80,128]{1,0:T(8,128)S(1)} collective-permute-done((f32[80,128]{1,0:T(8,128)S(1)}, f32[80,128]{1,0:T(8,128)S(1)}, u32[]{:S(2)}, u32[]{:S(2)}) %collective-permute-start) | collective-permute-done | bytes 40992 | tf_op jit(solution)/shard_map/ppermute | solution.py:422
  11.3 1.6 %collective-permute-start.2 = (f32[240,128]{1,0:T(8,128)S(1)}, f32[240,128]{1,0:T(8,128)S(1)}, u32[]{:S(2)}, u32[]{:S(2)}) collective-permute-start(f32[240,128]{1,0:T(8,128)S(1)} %pad_maximum_fusion.1.refs_3_), channel_id=1, source_target_pairs={{0,16},{16,0},{1,17},{17,1},{2,18},{18,2},{3,19},{19,3},{4,20},{20... | collective-permute-start | bytes 368648 | tf_op jit(solution)/shard_map/ppermute | solution.py:415
  12.9 1.6 %shard_map.97 = (f32[16,4,128,128]{3,2,1,0:T(8,128)S(1)}, s32[4,12]{1,0:T(4,128)S(1)}, s32[1,256]{1,0:T(1,128)S(1)}) custom-call(s32[16,6]{1,0:T(8,128)S(1)} %get-tuple-element.25.refs_0_, f32[80,128]{1,0:T(8,128)S(1)} %get-tuple-element.23.refs_1_.refs_3_, bf16[16,128,32]{2,1,0:T(8,128)(2,1)S(1)} %get-tuple-element.24.refs_2_, ...), custom_call_target="tpu_custom_call", output_to_operand_aliasing={{0}: (4, {})} | custom-call | flops 31457280 | bytes 40960 | tf_op jit(solution)/shard_map/pallas_call | solution.py:483
  14.5 1.8 %collective-permute-done.2 = f32[240,128]{1,0:T(8,128)S(1)} collective-permute-done((f32[240,128]{1,0:T(8,128)S(1)}, f32[240,128]{1,0:T(8,128)S(1)}, u32[]{:S(2)}, u32[]{:S(2)}) %collective-permute-start.2) | collective-permute-done | bytes 122912 | tf_op jit(solution)/shard_map/ppermute | solution.py:415
  16.3 0.1 collective-permute-start.4
  16.4 1.6 %collective-permute-start.3 = (f32[480,128]{1,0:T(8,128)S(1)}, f32[480,128]{1,0:T(8,128)S(1)}, u32[]{:S(2)}, u32[]{:S(2)}) collective-permute-start(f32[480,128]{1,0:T(8,128)S(1)} %pad_maximum_fusion.refs_3_.refs_8_), channel_id=1, source_target_pairs={{0,3},{1,2},{2,1},{3,0},{4,7},{5,6},{6,5},{7,4},{8,11},{9,10},{10,... | collective-permute-start | bytes 737288 | tf_op jit(solution)/shard_map/ppermute | solution.py:421
  18.0 3.6 %shard_map.98.refs_4_ = f32[16,4,128,128]{3,2,1,0:T(8,128)S(1)} custom-call(s32[16,6]{1,0:T(8,128)S(1)} %get-tuple-element.25.refs_0_, f32[80,128]{1,0:T(8,128)S(1)} %get-tuple-element.23.refs_1_.refs_3_, bf16[16,128,32]{2,1,0:T(8,128)(2,1)S(1)} %get-tuple-element.24.refs_2_, ...), custom_call_target="tpu_custom_call", output_to_operand_aliasing={{}: (4, {})} | custom-call | flops 94371840 | bytes 40960 | tf_op jit(solution)/shard_map/pallas_call | solution.py:483
  21.6 0.0 collective-permute-done.4.refs_3_.refs_9_
  21.6 5.0 %shard_map.99.refs_4_ = f32[16,4,128,128]{3,2,1,0:T(8,128)S(1)} custom-call(s32[16,6]{1,0:T(8,128)S(1)} %get-tuple-element.25.refs_0_, f32[80,128]{1,0:T(8,128)S(1)} %get-tuple-element.23.refs_1_.refs_3_, bf16[16,128,32]{2,1,0:T(8,128)(2,1)S(1)} %get-tuple-element.24.refs_2_, ...), custom_call_target="tpu_custom_call", output_to_operand_aliasing={{}: (4, {})} | custom-call | flops 141557760 | bytes 40960 | tf_op jit(solution)/shard_map/pallas_call | solution.py:483
  26.7 0.0 collective-permute-done.3.refs_3_.refs_10_
  26.7 5.1 %shard_map.100.refs_3_ = f32[48,128]{1,0:T(8,128)S(1)} custom-call(s32[16,6]{1,0:T(8,128)S(1)} %get-tuple-element.25.refs_0_, f32[80,128]{1,0:T(8,128)S(1)} %get-tuple-element.23.refs_1_.refs_3_, bf16[16,128,32]{2,1,0:T(8,128)(2,1)S(1)} %get-tuple-element.24.refs_2_, f32[480,128]{1,0:T(8,128)S(1)} %collective-permute-done.3.refs_3_.refs_10_, ...), custom_call_target="tpu_custom_call" | custom-call | flops 141557760 | bytes 40960 | tf_op jit(solution)/shard_map/pallas_call | solution.py:483
  31.8 2.9 %shard_map.101 = (f32[48,128]{1,0:T(8,128)}, f32[2,8,128]{2,1,0:T(8,128)S(1)}) custom-call(s32[4,12]{1,0:T(4,128)S(1)} %get-tuple-element.31.refs_0_, f32[80,128]{1,0:T(8,128)S(1)} %get-tuple-element.23.refs_1_.refs_3_, f32[4,128]{1,0:T(4,128)S(1)} %get-tuple-element.32.refs_2_, f32[48,128]{1,0:T(8,128)S(1)} %shard_map.100.refs_3_, ...), custom_call_target="tpu_custom_call" | custom-call | tf_op jit(solution)/shard_map/pallas_call | solution.py:531
  34.7 1.5 %collective-permute-start.5 = (f32[2,8,128]{2,1,0:T(8,128)S(1)}, f32[2,8,128]{2,1,0:T(8,128)S(1)}, u32[]{:S(2)}, u32[]{:S(2)}) collective-permute-start(f32[2,8,128]{2,1,0:T(8,128)S(1)} %get-tuple-element.41), channel_id=1, source_target_pairs={{0,16},{16,0},{1,17},{17,1},{2,18},{18,2},{3,19},{19,3},{4,20},{20... | collective-permute-start | bytes 24584 | tf_op jit(solution)/shard_map/ppermute | solution.py:553
  36.2 2.2 %collective-permute-done.5 = f32[2,8,128]{2,1,0:T(8,128)S(1)} collective-permute-done((f32[2,8,128]{2,1,0:T(8,128)S(1)}, f32[2,8,128]{2,1,0:T(8,128)S(1)}, u32[]{:S(2)}, u32[]{:S(2)}) %collective-permute-start.5) | collective-permute-done | bytes 8224 | tf_op jit(solution)/shard_map/ppermute | solution.py:553
  38.4 0.6 %copy.19 = f32[1,1,1,2,8,128]{5,4,3,2,1,0:T(8,128)} copy(f32[1,1,1,2,8,128]{5,4,3,2,1,0:T(8,128)S(1)} %bitcast.15) | data formatting | bytes 16384
  (2 shorter events, 0.0 us)
Async XLA Ops:
  2.2 7.1 %collective-permute-start.1 = (f32[80,128]{1,0:T(8,128)S(1)}, f32[80,128]{1,0:T(8,128)S(1)}, u32[]{:S(2)}, u32[]{:S(2)}) collective-permute-start(f32[80,128]{1,0:T(8,128)S(1)} %get-tuple-element.23.refs_1_.refs_3_), channel_id=1, source_target_pairs={{0,12},{4,8},{8,4},{12,0},{1,13},{5,9},{9,5},{13,1},{2,14},{6,10},... | collective-permute-start | bytes 122888 | tf_op jit(solution)/shard_map/ppermute | solution.py:421
  7.3 4.0 %collective-permute-start = (f32[80,128]{1,0:T(8,128)S(1)}, f32[80,128]{1,0:T(8,128)S(1)}, u32[]{:S(2)}, u32[]{:S(2)}) collective-permute-start(f32[80,128]{1,0:T(8,128)S(1)} %get-tuple-element.23.refs_1_.refs_3_), channel_id=1, source_target_pairs={{0,4},{4,0},{8,12},{12,8},{1,5},{5,1},{9,13},{13,9},{2,6},{6,2},{1... | collective-permute-start | bytes 122888 | tf_op jit(solution)/shard_map/ppermute | solution.py:422
  11.3 4.9 %collective-permute-start.2 = (f32[240,128]{1,0:T(8,128)S(1)}, f32[240,128]{1,0:T(8,128)S(1)}, u32[]{:S(2)}, u32[]{:S(2)}) collective-permute-start(f32[240,128]{1,0:T(8,128)S(1)} %pad_maximum_fusion.1.refs_3_), channel_id=1, source_target_pairs={{0,16},{16,0},{1,17},{17,1},{2,18},{18,2},{3,19},{19,3},{4,20},{20... | collective-permute-start | bytes 368648 | tf_op jit(solution)/shard_map/ppermute | solution.py:415
  16.3 5.3 %collective-permute-start.4 = (f32[480,128]{1,0:T(8,128)S(1)}, f32[480,128]{1,0:T(8,128)S(1)}, u32[]{:S(2)}, u32[]{:S(2)}) collective-permute-start(f32[480,128]{1,0:T(8,128)S(1)} %pad_maximum_fusion.refs_3_.refs_8_), channel_id=1, source_target_pairs={{0,1},{1,0},{2,3},{3,2},{4,5},{5,4},{6,7},{7,6},{8,9},{9,8},{10,11... | collective-permute-start | bytes 737288 | tf_op jit(solution)/shard_map/ppermute | solution.py:422
  16.4 10.3 %collective-permute-start.3 = (f32[480,128]{1,0:T(8,128)S(1)}, f32[480,128]{1,0:T(8,128)S(1)}, u32[]{:S(2)}, u32[]{:S(2)}) collective-permute-start(f32[480,128]{1,0:T(8,128)S(1)} %pad_maximum_fusion.refs_3_.refs_8_), channel_id=1, source_target_pairs={{0,3},{1,2},{2,1},{3,0},{4,7},{5,6},{6,5},{7,4},{8,11},{9,10},{10,... | collective-permute-start | bytes 737288 | tf_op jit(solution)/shard_map/ppermute | solution.py:421
  34.7 3.7 %collective-permute-start.5 = (f32[2,8,128]{2,1,0:T(8,128)S(1)}, f32[2,8,128]{2,1,0:T(8,128)S(1)}, u32[]{:S(2)}, u32[]{:S(2)}) collective-permute-start(f32[2,8,128]{2,1,0:T(8,128)S(1)} %get-tuple-element.41), channel_id=1, source_target_pairs={{0,16},{16,0},{1,17},{17,1},{2,18},{18,2},{3,19},{19,3},{4,20},{20... | collective-permute-start | bytes 24584 | tf_op jit(solution)/shard_map/ppermute | solution.py:553

commit v4 on v3

--- a/solution.py
+++ b/solution.py
@@ -147,8 +147,8 @@
 
 def prepare_kernel(
     label_in, mass_in, pos_in, weight_in, charge_in, lists_in, bead_lists_in, leaving_in,
-    rows_out, mass_out, near_out, hot, label_ref, mass, lists_out, bead_lists_out, leaving_out,
-    pos, weight, charge, near, sem,
+    rows_out, mass_out, hot, label_ref, mass, lists_out, bead_lists_out, leaving_out,
+    pos, weight, charge, sem,
 ):
     moves = [
         (label_in, label_ref), (mass_in, mass), (pos_in, pos), (weight_in, weight),
@@ -186,26 +186,24 @@
             sums[k * groups : (k + 1) * groups] / mass_sum
         )
     rows_out[base + 3 * groups : base + 4 * groups, :] = table
-    coords = [rows_out[k * tiles : (k + 1) * tiles, :] - 0.5 for k in range(3)]
-    for r, row in enumerate(near_rows(coords, 1.0)):
-        near[r * tiles : (r + 1) * tiles, :] = row
-    for t in range(tiles):
-        block = near[pl.ds(t, ROWS, stride=tiles), :]
-        near_out[t] = block.T.astype(BF16)
-
-
-def pair_kernel(tiles, groups, entries, sources, first, last, passed, *refs):
-    numbers, own, near = refs[:3]
-    cells = refs[3 : 3 + sources]
-    rest = refs[3 + sources :]
+
+
+def pair_kernel(tiles, groups, entries, sources, first, last, *refs):
+    numbers, own = refs[:2]
+    near = None if first else refs[2]
+    refs = refs[2 if first else 3 :]
+    cells = refs[:sources]
+    rest = refs[sources:]
     before = None if first else rest[0]
     rest = rest[0 if first else 1 :]
-    for p in range(passed):
-        rest[passed + 1 + p][...] = rest[p][...]
-    rest = rest[passed : passed + 1] + rest[2 * passed + 1 :]
     if first:
         rest[1][...] = packed_numbers(numbers[...], tiles)
-        numbers, rest = rest[1], rest[:1] + rest[2:]
+        numbers, near, rest = rest[1], rest[2], rest[:1] + rest[3:]
+        coords = [own[k * tiles : (k + 1) * tiles, :] - 0.5 for k in range(3)]
+        for r, row in enumerate(near_rows(coords, 1.0)):
+            rest[-1][r * tiles : (r + 1) * tiles, :] = row
+        for t in range(tiles):
+            near[t] = rest[-1][pl.ds(t, ROWS, stride=tiles), :].T.astype(BF16)
     out, far, held = rest[:3]
     total = rest[-1] if last else None
     count = len(entries)
@@ -317,7 +315,7 @@
     cells = refs[8 : 8 + sources]
     rest = refs[8 + sources :]
     forces_out, record_out, leave_hot, raw, far, near, nearest = rest[:7]
-    buffers, (total, coarse) = (rest[7:9], rest[9:11]), rest[11:]
+    buffers, (total, coarse) = rest[7:9], rest[9:]
     lists, listed = lists_ref[...], lists_ref.shape[1]
     height = 4 * (tiles + groups)
     signs = signs_here()
@@ -348,26 +346,25 @@
     for b in range(groups):
         nearest[b] = near[pl.ds(b, ROWS + 16, stride=groups), :].T.astype(BF16)
 
-    def products(b, dist, factor):
+    def products(b, into):
         lhs = nearest[b]
         for e in range(0, listed, 2):
             members = [lists[b, m] for m in range(e, min(e + 2, listed))]
-            at = slice(e * LANES, (e + len(members)) * LANES)
             rhs = jnp.concatenate([picked_rows(far, k, every) for k in members], axis=1)
-            dist[:, at] = jnp.dot(lhs[:, :ROWS], rhs, preferred_element_type=F32)
+            dist = jnp.dot(lhs[:, :ROWS], rhs, preferred_element_type=F32)
             rhs = [far[pl.ds(k + 19 * every, 8, stride=every), :] for k in members]
             rhs = jnp.concatenate([jnp.concatenate([r, r], axis=0) for r in rhs], axis=1)
-            factor[:, at] = jnp.dot(lhs[:, ROWS:], rhs.astype(BF16), preferred_element_type=F32)
-
-    def strengths(b, dist, factor):
-        block = 32
-        for i in range(0, LANES, block):
-            at = slice(i, i + block)
+            factor = jnp.dot(lhs[:, ROWS:], rhs.astype(BF16), preferred_element_type=F32)
+            into[:, e * LANES : (e + len(members)) * LANES] = jnp.exp2(dist) * factor
+
+    def strengths(b, held):
+        block = LANES // PARTS
+        for part in range(PARTS):
+            at = slice(part * block, (part + 1) * block)
             acc = [jnp.zeros((block, LANES), F32)] * 4
             for e in range(listed):
                 k = lists[b, e]
-                lanes = slice(e * LANES, (e + 1) * LANES)
-                s = jnp.exp2(dist[at, lanes]) * factor[at, lanes]
+                s = held[at, e * LANES : (e + 1) * LANES]
                 acc[3] = acc[3] + s
                 for d in range(3):
                     acc[d] = acc[d] + s * far[pl.ds((16 + d) * every + k, 1), :]
@@ -378,11 +375,11 @@
             centre = own[base + d * groups + b : base + d * groups + b + 1, :] - 0.5
             coarse[d * groups + b : d * groups + b + 1, :] = centre * sums[3] - sums[d]
 
-    products(0, *buffers[0])
+    products(0, buffers[0])
     for b in range(groups):
         if b + 1 < groups:
-            products(b + 1, *buffers[(b + 1) % 2])
-        strengths(b, *buffers[b % 2])
+            products(b + 1, buffers[(b + 1) % 2])
+        strengths(b, buffers[b % 2])
 
     label = label_ref[...]
     mass_sum = mass_sum_ref[...]
@@ -407,23 +404,39 @@
             record_out[side, f : f + 1, :] = row + shift if f == 0 else row
 
 
+def moves(axis):
+    n = lax.axis_size(axis)
+    if n <= 2:
+        return [([n - 1 - i for i in range(n)], (1, -1))]
+    if n % 2 == 0:
+        inner = [i ^ 1 for i in range(n)]
+        return [([(((i + 1) ^ 1) - 1) % n for i in range(n)], (-1,)), (inner, (1,))]
+    return [([(i + 1) % n for i in range(n)], (-1,)), ([(i - 1) % n for i in range(n)], (1,))]
+
+
 def exchange(x, axis):
-    n = lax.axis_size(axis)
-    if n == 1:
-        return [(x, 1), (x, -1)]
-    if n == 2:
-        other = lax.ppermute(x, axis, [(0, 1), (1, 0)])
-        return [(other, 1), (other, -1)]
-    if n % 2 == 0:
-        inner = [(i, i ^ 1) for i in range(n)]
-        outer = [(i, ((i + 1) ^ 1) - 1) for i in range(n)]
-        outer = [(i, (j + n) % n) for i, j in outer]
-        second = lax.ppermute(x, axis, outer)
-        first = lax.ppermute(x, axis, inner)
-        return [(first, 1), (second, -1)]
-    up = [(i, (i + 1) % n) for i in range(n)]
-    down = [(j, i) for i, j in up]
-    return [(lax.ppermute(x, axis, down), 1), (lax.ppermute(x, axis, up), -1)]
+    return [
+        (lax.ppermute(x, axis, list(enumerate(receivers))), steps)
+        for receivers, steps in moves(axis)
+    ]
+
+
+def exchange_plane(x, first, second):
+    sizes = lax.axis_size(first), lax.axis_size(second)
+    still = [(list(range(n)), (0,)) for n in sizes]
+    blocks = []
+    for to_b, steps_b in moves(second) + [still[1]]:
+        for to_a, steps_a in [still[0]] + moves(first):
+            steps = [(p, q) for p in steps_a for q in steps_b]
+            if steps == [(0, 0)]:
+                continue
+            pairs = [
+                (a * sizes[1] + b, to_a[a] * sizes[1] + to_b[b])
+                for a in range(sizes[0])
+                for b in range(sizes[1])
+            ]
+            blocks.append((lax.ppermute(x, (first, second), pairs), steps))
+    return blocks
 
 
 def sign_of(axis):
@@ -450,48 +463,48 @@
     def like(x):
         return jax.ShapeDtypeStruct(x.shape, x.dtype)
 
-    own, mass_sum, near, hot, label, mass, lists, *small = pl.pallas_call(
+    own, mass_sum, hot, label, mass, lists, *small = pl.pallas_call(
         prepare_kernel,
         out_shape=(
             jax.ShapeDtypeStruct((height, LANES), F32),
             jax.ShapeDtypeStruct((groups, LANES), F32),
-            jax.ShapeDtypeStruct((tiles, LANES, ROWS), BF16),
             jax.ShapeDtypeStruct((LANES, atoms), BF16),
             like(label),
             like(mass),
             *[like(x) for x in inputs[5:]],
         ),
         in_specs=[HBM] * 8,
-        out_specs=(VMEM,) * 9,
+        out_specs=(VMEM,) * 8,
         scratch_shapes=[
             *[pltpu.VMEM(x.shape, x.dtype) for x in inputs[2:5]],
-            pltpu.VMEM((ROWS * tiles, LANES), F32),
             pltpu.SemaphoreType.DMA((8,)),
         ],
         compiler_params=pltpu.CompilerParams(vmem_limit_bytes=48 * 2**20),
     )(*[pltpu.with_memory_space_constraint(x, pltpu.HBM) for x in inputs])
 
-    def pairs(lists, entries, cells, before, last=False, passed=()):
+    def pairs(lists, near, entries, cells, before, last=False):
         count = len(entries)
-        args = [lists, own, near, *cells] + ([] if before is None else [before])
+        first = before is None
+        args = [lists, own, *cells] if first else [lists, own, near, *cells, before]
         place = len(args) - 1
-        args += passed
         words = jax.ShapeDtypeStruct((tiles, 3 * -(-9 // number_plan(tiles)[1])), jnp.int32)
-        extra = [*passed, words] if before is None else passed
+        points = jax.ShapeDtypeStruct((tiles, LANES, ROWS), BF16)
+        extra = [words, points] if first else []
         shape = (3 * tiles, LANES) if last else (tiles, 4, LANES, LANES)
         work = tiles * count * LANES * LANES
         return pl.pallas_call(
             functools.partial(
-                pair_kernel, tiles, groups, entries, len(cells), before is None, last, len(passed)
+                pair_kernel, tiles, groups, entries, len(cells), before is None, last
             ),
-            out_shape=(jax.ShapeDtypeStruct(shape, F32), *[like(x) for x in extra]),
+            out_shape=(jax.ShapeDtypeStruct(shape, F32), *extra),
             in_specs=[VMEM] * len(args),
             out_specs=(VMEM,) * (1 + len(extra)),
             scratch_shapes=[
                 pltpu.VMEM((count, 20 * tiles, LANES), F32),
                 pltpu.VMEM((pair_plan(tiles, count)[0], LANES, count * LANES), F32),
             ]
-            + ([pltpu.VMEM((4, LANES, LANES), F32)] if last else []),
+            + ([pltpu.VMEM((4, LANES, LANES), F32)] if last else [])
+            + ([pltpu.VMEM((ROWS * tiles, LANES), F32)] if first else []),
             input_output_aliases={} if last or before is None else {place: 0},
             compiler_params=limit,
             cost_estimate=pl.CostEstimate(
@@ -499,35 +512,40 @@
             ),
         )(*args)
 
-    with_y = exchange(own, "gy")
-    force, lists = pairs(lists, [(0, 0, (0, 0, 0))], [own], None)
-    column = jnp.concatenate([own] + [block for block, _ in with_y], axis=0)
+    with_x = exchange(own, "gx")
+    force, lists, near = pairs(lists, None, [(0, 0, (0, 0, 0))], [own], None)
+    column = jnp.concatenate([own] + [block for block, _ in with_x], axis=0)
     column, force = lax.optimization_barrier((column, force))
-    y_steps = [0] + [step for _, step in with_y]
-    with_x = exchange(column, "gx")
-    entries = [(0, c, (0, y_steps[c], 0)) for c in (1, 2)]
-    force, beads_listed, leaving = pairs(lists, entries, [column], force, passed=small)
-    plane_cells = [(c, (0, y_steps[c])) for c in range(3)]
-    if lax.axis_size("gx") <= 2:
-        plane = jnp.concatenate([column, with_x[0][0]], axis=0)
-        plane_cells += [(3 + c, (x, y_steps[c])) for c in range(3) for x in (1, -1)]
-    else:
-        plane = jnp.concatenate([column] + [block for block, _ in with_x], axis=0)
-        plane_cells += [
-            (3 + 3 * k + c, (with_x[k][1], y_steps[c])) for c in range(3) for k in range(2)
-        ]
+    cells = [(0, 0)] + [(c + 1, x) for c, (_, steps) in enumerate(with_x) for x in steps]
+    with_y = exchange(column, "gy")[::-1]
+    entries = [(0, c, (x, 0, 0)) for c, x in cells[1:]]
+    force = pairs(lists, near, entries, [column], force)[0]
+    near_y, far_y = with_y[:1], with_y[1:]
+    if far_y:
+        entries = [(0, c, (x, y, 0)) for y in near_y[0][1] for c, x in cells]
+        force = pairs(lists, near, entries, [near_y[0][0]], force)[0]
+    plane = jnp.concatenate([column] + [block for block, _ in with_y], axis=0)
     plane, force = lax.optimization_barrier((plane, force))
-    with_z = exchange(plane, "gz")
-    entries = [(0, c, (x, y, 0)) for c, (x, y) in plane_cells[3:]]
-    force = pairs(lists, entries, [plane], force)[0]
+    held = 1 + len(with_x)
+    plane_cells = [(c, (x, 0)) for c, x in cells]
+    plane_cells += [
+        (held * (k + 1) + c, (x, y))
+        for k, (_, steps) in enumerate(with_y)
+        for y in steps
+        for c, x in cells
+    ]
+    with_z = [(block, z) for block, steps in exchange(plane, "gz") for z in steps][::-1]
+    left = far_y[0][1] if far_y else near_y[0][1]
+    entries = [(0, c, (x, y, 0)) for c, (x, y) in plane_cells if y in left]
+    force = pairs(lists, near, entries, [plane], force)[0]
     for place, (block, z) in enumerate(with_z):
         entries = [(0, c, (x, y, z)) for c, (x, y) in plane_cells]
-        force = pairs(lists, entries, [block], force, place == 1)[0]
+        force = pairs(lists, near, entries, [block], force, place == 1)[0]
 
     sources = [plane] + [block for block, _ in with_z]
     z_steps = [0] + [step for _, step in with_z]
     entries = [(s, c, (x, y, z_steps[s])) for s in range(3) for c, (x, y) in plane_cells]
-    every, listed = len(entries) * groups, beads_listed.shape[1]
+    every, listed = len(entries) * groups, small[0].shape[1]
     forces, record = pl.pallas_call(
         functools.partial(final_kernel, tiles, groups, entries, len(sources)),
         out_shape=(
@@ -542,12 +560,12 @@
             pltpu.VMEM((27 * every, LANES), F32),
             pltpu.VMEM(((ROWS + 16) * groups, LANES), F32),
             pltpu.VMEM((groups, LANES, ROWS + 16), BF16),
-            *[pltpu.VMEM((LANES, listed * LANES), F32)] * 4,
+            *[pltpu.VMEM((LANES, listed * LANES), F32)] * 2,
             pltpu.VMEM((4, LANES, LANES), F32),
             pltpu.VMEM((3 * groups, LANES), F32),
         ],
         compiler_params=limit,
-    )(beads_listed, own, mass_sum, force, mass, label, leaving, hot, *sources)
+    )(small[0], own, mass_sum, force, mass, label, small[1], hot, *sources)
     n = lax.axis_size("gx")
     if n == 2:
         arrivals = lax.ppermute(record, "gx", [(0, 1), (1, 0)])

time: 39.2 us -> 36.9 us (0.941)
  waiting for transfers between devices: 6.59 us -> 2.84 us
  starting transfers between devices: 9.86 us -> 10.8 us
  Pallas kernels: 21.2 us -> 21.7 us
    ppermute x5, waiting for transfers between devices: 4.42 us -> 0.67 us  [exchange(): lax.ppermute(x, axis, list(enumerate(receivers)))]
    ppermute x5, starting transfers between devices: 8.38 us -> 9.29 us  [exchange(): lax.ppermute(x, axis, list(enumerate(receivers)))]
    pallas_call x5 -> x6, Pallas kernels: 16.7 us -> 17.3 us  [pairs(): pl.pallas_call(functools.partial(pair_kernel, tiles, groups, entries, len...]
  transfers between devices with their start and end apart: 6 -> 6, of which waited for: 4 -> 2; matrix products, arithmetic and copies ran while one was open for 0% -> 0% of each run, Pallas kernels for 30% -> 33%
where the time goes in v4:
time: 36.9 us; the launch traced here: 36.6 us
  Pallas kernels  21.7 us (59%)
  starting transfers between devices  10.8 us (29%)
  waiting for transfers between devices  2.84 us (8%)
  between operations  0.72 us (2%)
  local copies, waits for them, and re-layouts  0.6 us (2%)
    pallas_call x6, Pallas kernels, pairs(): pl.pallas_call(functools.partial(pair_kernel, tiles, groups, entries, len...  17.3 us
    ppermute x5, starting transfers between devices, exchange(): lax.ppermute(x, axis, list(enumerate(receivers)))  9.29 us
    pallas_call x1, Pallas kernels, per_device(): pl.pallas_call(functools.partial(final_kernel, tiles, groups, entries, le...  2.88 us
    ppermute x1, waiting for transfers between devices, per_device(): arrivals = lax.ppermute(record, 'gx', [(0, 1), (1, 0)])  2.17 us
    pallas_call x1, Pallas kernels, per_device(): pl.pallas_call(prepare_kernel, out_shape=(jax.ShapeDtypeStruct((height, L...  1.55 us
    ppermute x1, starting transfers between devices, per_device(): arrivals = lax.ppermute(record, 'gx', [(0, 1), (1, 0)])  1.48 us
  transfers between devices with their start and end apart: 6, of which 2 were waited for; matrix products, arithmetic and copies ran while one was open for 0% of the time, Pallas kernels for 33%

profile of v4, /device:TPU:0, one launch (start us, length us, event | category | flops | bytes accessed | tf_op | source)
XLA Modules:
  0.0 36.6 jit_solution(436983729976089062)
XLA Ops:
  0.6 1.5 %shard_map.95 = (f32[80,128]{1,0:T(8,128)S(1)}, f32[4,128]{1,0:T(4,128)S(1)}, bf16[128,2048]{1,0:T(8,128)(2,1)S(1)}, s32[1,2048]{1,0:T(1,128)S(1)}, f32[1,2048]{...) custom-call(s32[1,2048]{1,0:T(1,128)} %bitcast.11, f32[1,2048]{1,0:T(1,128)} %bitcast.12, ...), custom_call_target="tpu_custom_call" | custom-call | tf_op jit(solution)/shard_map/pallas_call | solution.py:466
  2.2 3.0 %collective-permute-start = (f32[80,128]{1,0:T(8,128)S(1)}, f32[80,128]{1,0:T(8,128)S(1)}, u32[]{:S(2)}, u32[]{:S(2)}) collective-permute-start(f32[80,128]{1,0:T(8,128)S(1)} %get-tuple-element.20.refs_1_.refs_2_), channel_id=1, source_target_pairs={{0,16},{16,0},{1,17},{17,1},{2,18},{18,2},{3,19},{19,3},{4,20},{20... | collective-permute-start | bytes 122888 | tf_op jit(solution)/shard_map/ppermute | solution.py:419
  5.2 1.4 %shard_map.96 = (f32[16,4,128,128]{3,2,1,0:T(8,128)S(1)}, s32[16,6]{1,0:T(8,128)S(1)}, bf16[16,128,32]{2,1,0:T(8,128)(2,1)S(1)}) custom-call(s32[16,27]{1,0:T(8,128)S(1)} %get-tuple-element.22.refs_0_, f32[80,128]{1,0:T(8,128)S(1)} %get-tuple-element.20.refs_1_.refs_2_, f32[80,128]{1,0:T(8,128)S(1)} %get-tuple-element.20.refs_1_.refs_2_), custom_call_target="tpu_custom_call" | custom-call | flops 15728640 | bytes 40960 | tf_op jit(solution)/shard_map/pallas_call | solution.py:495
  6.6 0.6 %collective-permute-done = f32[80,128]{1,0:T(8,128)S(1)} collective-permute-done((f32[80,128]{1,0:T(8,128)S(1)}, f32[80,128]{1,0:T(8,128)S(1)}, u32[]{:S(2)}, u32[]{:S(2)}) %collective-permute-start) | collective-permute-done | bytes 40992 | tf_op jit(solution)/shard_map/ppermute | solution.py:419
  7.2 2.1 %collective-permute-start.1 = (f32[160,128]{1,0:T(8,128)S(1)}, f32[160,128]{1,0:T(8,128)S(1)}, u32[]{:S(2)}, u32[]{:S(2)}) collective-permute-start(f32[160,128]{1,0:T(8,128)S(1)} %pad_maximum_fusion.1.refs_3_), channel_id=1, source_target_pairs={{0,4},{4,0},{8,12},{12,8},{1,5},{5,1},{9,13},{13,9},{2,6},{6,2},{1... | collective-permute-start | bytes 245768 | tf_op jit(solution)/shard_map/ppermute | solution.py:419
  9.3 2.5 %collective-permute-start.2 = (f32[160,128]{1,0:T(8,128)S(1)}, f32[160,128]{1,0:T(8,128)S(1)}, u32[]{:S(2)}, u32[]{:S(2)}) collective-permute-start(f32[160,128]{1,0:T(8,128)S(1)} %pad_maximum_fusion.1.refs_3_), channel_id=1, source_target_pairs={{0,12},{4,8},{8,4},{12,0},{1,13},{5,9},{9,5},{13,1},{2,14},{6,10},... | collective-permute-start | bytes 245768 | tf_op jit(solution)/shard_map/ppermute | solution.py:419
  11.8 1.6 %shard_map.97.refs_4_ = f32[16,4,128,128]{3,2,1,0:T(8,128)S(1)} custom-call(s32[16,6]{1,0:T(8,128)S(1)} %get-tuple-element.23.refs_0_, f32[80,128]{1,0:T(8,128)S(1)} %get-tuple-element.20.refs_1_.refs_2_, bf16[16,128,32]{2,1,0:T(8,128)(2,1)S(1)} %get-tuple-element.24.refs_2_, ...), custom_call_target="tpu_custom_call", output_to_operand_aliasing={{}: (4, {})} | custom-call | flops 31457280 | bytes 40960 | tf_op jit(solution)/shard_map/pallas_call | solution.py:495
  13.4 0.0 collective-permute-done.1.refs_3_
  13.4 2.1 %shard_map.98.refs_4_ = f32[16,4,128,128]{3,2,1,0:T(8,128)S(1)} custom-call(s32[16,6]{1,0:T(8,128)S(1)} %get-tuple-element.23.refs_0_, f32[80,128]{1,0:T(8,128)S(1)} %get-tuple-element.20.refs_1_.refs_2_, bf16[16,128,32]{2,1,0:T(8,128)(2,1)S(1)} %get-tuple-element.24.refs_2_, ...), custom_call_target="tpu_custom_call", output_to_operand_aliasing={{}: (4, {})} | custom-call | flops 47185920 | bytes 40960 | tf_op jit(solution)/shard_map/pallas_call | solution.py:495
  15.5 0.0 collective-permute-done.2
  15.5 0.1 collective-permute-start.4
  15.6 1.6 %collective-permute-start.3 = (f32[480,128]{1,0:T(8,128)S(1)}, f32[480,128]{1,0:T(8,128)S(1)}, u32[]{:S(2)}, u32[]{:S(2)}) collective-permute-start(f32[480,128]{1,0:T(8,128)S(1)} %pad_maximum_fusion.refs_3_.refs_8_), channel_id=1, source_target_pairs={{0,3},{1,2},{2,1},{3,0},{4,7},{5,6},{6,5},{7,4},{8,11},{9,10},{10,... | collective-permute-start | bytes 737288 | tf_op jit(solution)/shard_map/ppermute | solution.py:419
  17.3 2.1 %shard_map.99.refs_4_ = f32[16,4,128,128]{3,2,1,0:T(8,128)S(1)} custom-call(s32[16,6]{1,0:T(8,128)S(1)} %get-tuple-element.23.refs_0_, f32[80,128]{1,0:T(8,128)S(1)} %get-tuple-element.20.refs_1_.refs_2_, bf16[16,128,32]{2,1,0:T(8,128)(2,1)S(1)} %get-tuple-element.24.refs_2_, ...), custom_call_target="tpu_custom_call", output_to_operand_aliasing={{}: (4, {})} | custom-call | flops 47185920 | bytes 40960 | tf_op jit(solution)/shard_map/pallas_call | solution.py:495
  19.4 0.0 collective-permute-done.4.refs_3_.refs_9_
  19.4 5.1 %shard_map.100.refs_4_ = f32[16,4,128,128]{3,2,1,0:T(8,128)S(1)} custom-call(s32[16,6]{1,0:T(8,128)S(1)} %get-tuple-element.23.refs_0_, f32[80,128]{1,0:T(8,128)S(1)} %get-tuple-element.20.refs_1_.refs_2_, bf16[16,128,32]{2,1,0:T(8,128)(2,1)S(1)} %get-tuple-element.24.refs_2_, ...), custom_call_target="tpu_custom_call", output_to_operand_aliasing={{}: (4, {})} | custom-call | flops 141557760 | bytes 40960 | tf_op jit(solution)/shard_map/pallas_call | solution.py:495
  24.4 0.0 collective-permute-done.3.refs_3_.refs_10_
  24.4 5.1 %shard_map.101.refs_3_ = f32[48,128]{1,0:T(8,128)S(1)} custom-call(s32[16,6]{1,0:T(8,128)S(1)} %get-tuple-element.23.refs_0_, f32[80,128]{1,0:T(8,128)S(1)} %get-tuple-element.20.refs_1_.refs_2_, bf16[16,128,32]{2,1,0:T(8,128)(2,1)S(1)} %get-tuple-element.24.refs_2_, f32[480,128]{1,0:T(8,128)S(1)} %collective-permute-done.3.refs_3_.refs_10_, ...), custom_call_target="tpu_custom_call" | custom-call | flops 141557760 | bytes 40960 | tf_op jit(solution)/shard_map/pallas_call | solution.py:495
  29.5 2.9 %shard_map.102 = (f32[48,128]{1,0:T(8,128)}, f32[2,8,128]{2,1,0:T(8,128)S(1)}) custom-call(s32[4,12]{1,0:T(4,128)S(1)} %get-tuple-element.19.refs_0_, f32[80,128]{1,0:T(8,128)S(1)} %get-tuple-element.20.refs_1_.refs_2_, f32[4,128]{1,0:T(4,128)S(1)} %get-tuple-element.21.refs_2_, f32[48,128]{1,0:T(8,128)S(1)} %shard_map.101.refs_3_, ...), custom_call_target="tpu_custom_call" | custom-call | tf_op jit(solution)/shard_map/pallas_call | solution.py:549
  32.4 1.5 %collective-permute-start.5 = (f32[2,8,128]{2,1,0:T(8,128)S(1)}, f32[2,8,128]{2,1,0:T(8,128)S(1)}, u32[]{:S(2)}, u32[]{:S(2)}) collective-permute-start(f32[2,8,128]{2,1,0:T(8,128)S(1)} %get-tuple-element.35), channel_id=1, source_target_pairs={{0,16},{16,0},{1,17},{17,1},{2,18},{18,2},{3,19},{19,3},{4,20},{20... | collective-permute-start | bytes 24584 | tf_op jit(solution)/shard_map/ppermute | solution.py:571
  33.9 2.2 %collective-permute-done.5 = f32[2,8,128]{2,1,0:T(8,128)S(1)} collective-permute-done((f32[2,8,128]{2,1,0:T(8,128)S(1)}, f32[2,8,128]{2,1,0:T(8,128)S(1)}, u32[]{:S(2)}, u32[]{:S(2)}) %collective-permute-start.5) | collective-permute-done | bytes 8224 | tf_op jit(solution)/shard_map/ppermute | solution.py:571
  36.0 0.6 %copy.21 = f32[1,1,1,2,8,128]{5,4,3,2,1,0:T(8,128)} copy(f32[1,1,1,2,8,128]{5,4,3,2,1,0:T(8,128)S(1)} %bitcast.15) | data formatting | bytes 16384
  (2 shorter events, 0.0 us)
Async XLA Ops:
  2.2 5.0 %collective-permute-start = (f32[80,128]{1,0:T(8,128)S(1)}, f32[80,128]{1,0:T(8,128)S(1)}, u32[]{:S(2)}, u32[]{:S(2)}) collective-permute-start(f32[80,128]{1,0:T(8,128)S(1)} %get-tuple-element.20.refs_1_.refs_2_), channel_id=1, source_target_pairs={{0,16},{16,0},{1,17},{17,1},{2,18},{18,2},{3,19},{19,3},{4,20},{20... | collective-permute-start | bytes 122888 | tf_op jit(solution)/shard_map/ppermute | solution.py:419
  7.2 6.2 %collective-permute-start.1 = (f32[160,128]{1,0:T(8,128)S(1)}, f32[160,128]{1,0:T(8,128)S(1)}, u32[]{:S(2)}, u32[]{:S(2)}) collective-permute-start(f32[160,128]{1,0:T(8,128)S(1)} %pad_maximum_fusion.1.refs_3_), channel_id=1, source_target_pairs={{0,4},{4,0},{8,12},{12,8},{1,5},{5,1},{9,13},{13,9},{2,6},{6,2},{1... | collective-permute-start | bytes 245768 | tf_op jit(solution)/shard_map/ppermute | solution.py:419
  9.3 6.2 %collective-permute-start.2 = (f32[160,128]{1,0:T(8,128)S(1)}, f32[160,128]{1,0:T(8,128)S(1)}, u32[]{:S(2)}, u32[]{:S(2)}) collective-permute-start(f32[160,128]{1,0:T(8,128)S(1)} %pad_maximum_fusion.1.refs_3_), channel_id=1, source_target_pairs={{0,12},{4,8},{8,4},{12,0},{1,13},{5,9},{9,5},{13,1},{2,14},{6,10},... | collective-permute-start | bytes 245768 | tf_op jit(solution)/shard_map/ppermute | solution.py:419
  15.5 3.8 %collective-permute-start.4 = (f32[480,128]{1,0:T(8,128)S(1)}, f32[480,128]{1,0:T(8,128)S(1)}, u32[]{:S(2)}, u32[]{:S(2)}) collective-permute-start(f32[480,128]{1,0:T(8,128)S(1)} %pad_maximum_fusion.refs_3_.refs_8_), channel_id=1, source_target_pairs={{0,1},{1,0},{2,3},{3,2},{4,5},{5,4},{6,7},{7,6},{8,9},{9,8},{10,11... | collective-permute-start | bytes 737288 | tf_op jit(solution)/shard_map/ppermute | solution.py:419
  15.6 8.8 %collective-permute-start.3 = (f32[480,128]{1,0:T(8,128)S(1)}, f32[480,128]{1,0:T(8,128)S(1)}, u32[]{:S(2)}, u32[]{:S(2)}) collective-permute-start(f32[480,128]{1,0:T(8,128)S(1)} %pad_maximum_fusion.refs_3_.refs_8_), channel_id=1, source_target_pairs={{0,3},{1,2},{2,1},{3,0},{4,7},{5,6},{6,5},{7,4},{8,11},{9,10},{10,... | collective-permute-start | bytes 737288 | tf_op jit(solution)/shard_map/ppermute | solution.py:419
  32.4 3.7 %collective-permute-start.5 = (f32[2,8,128]{2,1,0:T(8,128)S(1)}, f32[2,8,128]{2,1,0:T(8,128)S(1)}, u32[]{:S(2)}, u32[]{:S(2)}) collective-permute-start(f32[2,8,128]{2,1,0:T(8,128)S(1)} %get-tuple-element.35), channel_id=1, source_target_pairs={{0,16},{16,0},{1,17},{17,1},{2,18},{18,2},{3,19},{19,3},{4,20},{20... | collective-permute-start | bytes 24584 | tf_op jit(solution)/shard_map/ppermute | solution.py:571

commit v5 on v4

--- a/solution.py
+++ b/solution.py
@@ -139,7 +139,7 @@
 
 def pair_plan(tiles, count):
     held, ahead = (8, 6) if count == 1 else (8, 4) if count == 2 else (2, 1)
-    unroll = max(held, 4)
+    unroll = 8 if count < 6 else 4
     if tiles % unroll:
         held, unroll, ahead = 2, 2, 1
     return held, unroll, ahead
@@ -549,7 +549,7 @@
     forces, record = pl.pallas_call(
         functools.partial(final_kernel, tiles, groups, entries, len(sources)),
         out_shape=(
-            jax.ShapeDtypeStruct((3 * tiles, LANES), F32),
+            pltpu.VMEM((3 * tiles, LANES), F32),
             jax.ShapeDtypeStruct((2, 8, leavers), F32),
         ),
         in_specs=[VMEM] * (8 + len(sources)),

time: 36.9 us -> 36.4 us (0.986)
  local copies, waits for them, and re-layouts: 0.6 us -> 1.21 us
  Pallas kernels: 21.7 us -> 21.1 us
  waiting for transfers between devices: 2.84 us -> 2.33 us
    unnamed x1 -> x2, local copies, waits for them, and re-layouts: 0.6 us -> 1.21 us
    ppermute x1, waiting for transfers between devices: 2.17 us -> 1.57 us  [per_device(): arrivals = lax.ppermute(record, 'gx', [(0, 1), (1, 0)])]
    pallas_call x1, Pallas kernels: 2.88 us -> 2.48 us  [per_device(): pl.pallas_call(functools.partial(final_kernel, tiles, groups, entries, le...]
  transfers between devices with their start and end apart: 6 -> 6, of which waited for: 2 -> 3; matrix products, arithmetic and copies ran while one was open for 0% -> 2% of each run, Pallas kernels for 33% -> 33%
where the time goes in v5:
time: 36.4 us; the launch traced here: 36.2 us
  Pallas kernels  21.1 us (58%)
  starting transfers between devices  10.8 us (30%)
  waiting for transfers between devices  2.33 us (6%)
  local copies, waits for them, and re-layouts  1.21 us (3%)
  between operations  0.73 us (2%)
    pallas_call x6, Pallas kernels, pairs(): pl.pallas_call(functools.partial(pair_kernel, tiles, groups, entries, len...  17.1 us
    ppermute x5, starting transfers between devices, exchange(): lax.ppermute(x, axis, list(enumerate(receivers)))  9.29 us
    pallas_call x1, Pallas kernels, per_device(): pl.pallas_call(functools.partial(final_kernel, tiles, groups, entries, le...  2.48 us
    ppermute x1, waiting for transfers between devices, per_device(): arrivals = lax.ppermute(record, 'gx', [(0, 1), (1, 0)])  1.57 us
    pallas_call x1, Pallas kernels, per_device(): pl.pallas_call(prepare_kernel, out_shape=(jax.ShapeDtypeStruct((height, L...  1.55 us
    ppermute x1, starting transfers between devices, per_device(): arrivals = lax.ppermute(record, 'gx', [(0, 1), (1, 0)])  1.54 us
    unnamed x2, local copies, waits for them, and re-layouts  1.21 us
    ppermute x5, waiting for transfers between devices, exchange(): lax.ppermute(x, axis, list(enumerate(receivers)))  0.76 us
  transfers between devices with their start and end apart: 6, of which 3 were waited for; matrix products, arithmetic and copies ran while one was open for 2% of the time, Pallas kernels for 33%

profile of v5, /device:TPU:0, one launch (start us, length us, event | category | flops | bytes accessed | tf_op | source)
XLA Modules:
  0.0 36.2 jit_solution(7252581582304070721)
XLA Ops:
  0.6 1.5 %shard_map.95 = (f32[80,128]{1,0:T(8,128)S(1)}, f32[4,128]{1,0:T(4,128)S(1)}, bf16[128,2048]{1,0:T(8,128)(2,1)S(1)}, s32[1,2048]{1,0:T(1,128)S(1)}, f32[1,2048]{...) custom-call(s32[1,2048]{1,0:T(1,128)} %bitcast.12, f32[1,2048]{1,0:T(1,128)} %bitcast.13, ...), custom_call_target="tpu_custom_call" | custom-call | tf_op jit(solution)/shard_map/pallas_call | solution.py:466
  2.2 3.0 %collective-permute-start = (f32[80,128]{1,0:T(8,128)S(1)}, f32[80,128]{1,0:T(8,128)S(1)}, u32[]{:S(2)}, u32[]{:S(2)}) collective-permute-start(f32[80,128]{1,0:T(8,128)S(1)} %get-tuple-element.20.refs_1_.refs_2_), channel_id=1, source_target_pairs={{0,16},{16,0},{1,17},{17,1},{2,18},{18,2},{3,19},{19,3},{4,20},{20... | collective-permute-start | bytes 122888 | tf_op jit(solution)/shard_map/ppermute | solution.py:419
  5.2 1.4 %shard_map.96 = (f32[16,4,128,128]{3,2,1,0:T(8,128)S(1)}, s32[16,6]{1,0:T(8,128)S(1)}, bf16[16,128,32]{2,1,0:T(8,128)(2,1)S(1)}) custom-call(s32[16,27]{1,0:T(8,128)S(1)} %get-tuple-element.22.refs_0_, f32[80,128]{1,0:T(8,128)S(1)} %get-tuple-element.20.refs_1_.refs_2_, f32[80,128]{1,0:T(8,128)S(1)} %get-tuple-element.20.refs_1_.refs_2_), custom_call_target="tpu_custom_call" | custom-call | flops 15728640 | bytes 40960 | tf_op jit(solution)/shard_map/pallas_call | solution.py:495
  6.6 0.6 %collective-permute-done = f32[80,128]{1,0:T(8,128)S(1)} collective-permute-done((f32[80,128]{1,0:T(8,128)S(1)}, f32[80,128]{1,0:T(8,128)S(1)}, u32[]{:S(2)}, u32[]{:S(2)}) %collective-permute-start) | collective-permute-done | bytes 40992 | tf_op jit(solution)/shard_map/ppermute | solution.py:419
  7.2 2.1 %collective-permute-start.1 = (f32[160,128]{1,0:T(8,128)S(1)}, f32[160,128]{1,0:T(8,128)S(1)}, u32[]{:S(2)}, u32[]{:S(2)}) collective-permute-start(f32[160,128]{1,0:T(8,128)S(1)} %pad_maximum_fusion.1.refs_3_), channel_id=1, source_target_pairs={{0,4},{4,0},{8,12},{12,8},{1,5},{5,1},{9,13},{13,9},{2,6},{6,2},{1... | collective-permute-start | bytes 245768 | tf_op jit(solution)/shard_map/ppermute | solution.py:419
  9.3 2.5 %collective-permute-start.2 = (f32[160,128]{1,0:T(8,128)S(1)}, f32[160,128]{1,0:T(8,128)S(1)}, u32[]{:S(2)}, u32[]{:S(2)}) collective-permute-start(f32[160,128]{1,0:T(8,128)S(1)} %pad_maximum_fusion.1.refs_3_), channel_id=1, source_target_pairs={{0,12},{4,8},{8,4},{12,0},{1,13},{5,9},{9,5},{13,1},{2,14},{6,10},... | collective-permute-start | bytes 245768 | tf_op jit(solution)/shard_map/ppermute | solution.py:419
  11.8 1.6 %shard_map.97.refs_4_ = f32[16,4,128,128]{3,2,1,0:T(8,128)S(1)} custom-call(s32[16,6]{1,0:T(8,128)S(1)} %get-tuple-element.23.refs_0_, f32[80,128]{1,0:T(8,128)S(1)} %get-tuple-element.20.refs_1_.refs_2_, bf16[16,128,32]{2,1,0:T(8,128)(2,1)S(1)} %get-tuple-element.24.refs_2_, ...), custom_call_target="tpu_custom_call", output_to_operand_aliasing={{}: (4, {})} | custom-call | flops 31457280 | bytes 40960 | tf_op jit(solution)/shard_map/pallas_call | solution.py:495
  13.4 0.0 collective-permute-done.1.refs_3_
  13.4 2.0 %shard_map.98.refs_4_ = f32[16,4,128,128]{3,2,1,0:T(8,128)S(1)} custom-call(s32[16,6]{1,0:T(8,128)S(1)} %get-tuple-element.23.refs_0_, f32[80,128]{1,0:T(8,128)S(1)} %get-tuple-element.20.refs_1_.refs_2_, bf16[16,128,32]{2,1,0:T(8,128)(2,1)S(1)} %get-tuple-element.24.refs_2_, ...), custom_call_target="tpu_custom_call", output_to_operand_aliasing={{}: (4, {})} | custom-call | flops 47185920 | bytes 40960 | tf_op jit(solution)/shard_map/pallas_call | solution.py:495
  15.4 0.1 collective-permute-done.2
  15.5 0.1 collective-permute-start.4
  15.6 1.6 %collective-permute-start.3 = (f32[480,128]{1,0:T(8,128)S(1)}, f32[480,128]{1,0:T(8,128)S(1)}, u32[]{:S(2)}, u32[]{:S(2)}) collective-permute-start(f32[480,128]{1,0:T(8,128)S(1)} %pad_maximum_fusion.refs_3_.refs_8_), channel_id=1, source_target_pairs={{0,3},{1,2},{2,1},{3,0},{4,7},{5,6},{6,5},{7,4},{8,11},{9,10},{10,... | collective-permute-start | bytes 737288 | tf_op jit(solution)/shard_map/ppermute | solution.py:419
  17.3 2.0 %shard_map.99.refs_4_ = f32[16,4,128,128]{3,2,1,0:T(8,128)S(1)} custom-call(s32[16,6]{1,0:T(8,128)S(1)} %get-tuple-element.23.refs_0_, f32[80,128]{1,0:T(8,128)S(1)} %get-tuple-element.20.refs_1_.refs_2_, bf16[16,128,32]{2,1,0:T(8,128)(2,1)S(1)} %get-tuple-element.24.refs_2_, ...), custom_call_target="tpu_custom_call", output_to_operand_aliasing={{}: (4, {})} | custom-call | flops 47185920 | bytes 40960 | tf_op jit(solution)/shard_map/pallas_call | solution.py:495
  19.2 0.0 collective-permute-done.4.refs_3_.refs_9_
  19.2 5.1 %shard_map.100.refs_4_ = f32[16,4,128,128]{3,2,1,0:T(8,128)S(1)} custom-call(s32[16,6]{1,0:T(8,128)S(1)} %get-tuple-element.23.refs_0_, f32[80,128]{1,0:T(8,128)S(1)} %get-tuple-element.20.refs_1_.refs_2_, bf16[16,128,32]{2,1,0:T(8,128)(2,1)S(1)} %get-tuple-element.24.refs_2_, ...), custom_call_target="tpu_custom_call", output_to_operand_aliasing={{}: (4, {})} | custom-call | flops 141557760 | bytes 40960 | tf_op jit(solution)/shard_map/pallas_call | solution.py:495
  24.3 0.0 collective-permute-done.3.refs_3_.refs_10_
  24.3 5.1 %shard_map.101.refs_3_ = f32[48,128]{1,0:T(8,128)S(1)} custom-call(s32[16,6]{1,0:T(8,128)S(1)} %get-tuple-element.23.refs_0_, f32[80,128]{1,0:T(8,128)S(1)} %get-tuple-element.20.refs_1_.refs_2_, bf16[16,128,32]{2,1,0:T(8,128)(2,1)S(1)} %get-tuple-element.24.refs_2_, f32[480,128]{1,0:T(8,128)S(1)} %collective-permute-done.3.refs_3_.refs_10_, ...), custom_call_target="tpu_custom_call" | custom-call | flops 141557760 | bytes 40960 | tf_op jit(solution)/shard_map/pallas_call | solution.py:495
  29.4 2.5 %shard_map.102 = (f32[48,128]{1,0:T(8,128)S(1)}, f32[2,8,128]{2,1,0:T(8,128)S(1)}) custom-call(s32[4,12]{1,0:T(4,128)S(1)} %get-tuple-element.19.refs_0_, f32[80,128]{1,0:T(8,128)S(1)} %get-tuple-element.20.refs_1_.refs_2_, f32[4,128]{1,0:T(4,128)S(1)} %get-tuple-element.21.refs_2_, f32[48,128]{1,0:T(8,128)S(1)} %shard_map.101.refs_3_, ...), custom_call_target="tpu_custom_call" | custom-call | tf_op jit(solution)/shard_map/pallas_call | solution.py:549
  31.9 1.5 %collective-permute-start.5 = (f32[2,8,128]{2,1,0:T(8,128)S(1)}, f32[2,8,128]{2,1,0:T(8,128)S(1)}, u32[]{:S(2)}, u32[]{:S(2)}) collective-permute-start(f32[2,8,128]{2,1,0:T(8,128)S(1)} %get-tuple-element.35), channel_id=1, source_target_pairs={{0,16},{16,0},{1,17},{17,1},{2,18},{18,2},{3,19},{19,3},{4,20},{20... | collective-permute-start | bytes 24584 | tf_op jit(solution)/shard_map/ppermute | solution.py:571
  33.4 0.6 %copy.21 = f32[1,1,1,3,2048]{4,2,3,1,0:T(1,128)} copy(f32[1,1,1,3,2048]{4,2,3,1,0:T(1,128)S(1)} %bitcast.10) | data formatting | bytes 49152
  34.0 1.6 %collective-permute-done.5 = f32[2,8,128]{2,1,0:T(8,128)S(1)} collective-permute-done((f32[2,8,128]{2,1,0:T(8,128)S(1)}, f32[2,8,128]{2,1,0:T(8,128)S(1)}, u32[]{:S(2)}, u32[]{:S(2)}) %collective-permute-start.5) | collective-permute-done | bytes 8224 | tf_op jit(solution)/shard_map/ppermute | solution.py:571
  35.6 0.6 %copy.22 = f32[1,1,1,2,8,128]{5,4,3,2,1,0:T(8,128)} copy(f32[1,1,1,2,8,128]{5,4,3,2,1,0:T(8,128)S(1)} %bitcast.16) | data formatting | bytes 16384
  (2 shorter events, 0.0 us)
Async XLA Ops:
  2.2 5.0 %collective-permute-start = (f32[80,128]{1,0:T(8,128)S(1)}, f32[80,128]{1,0:T(8,128)S(1)}, u32[]{:S(2)}, u32[]{:S(2)}) collective-permute-start(f32[80,128]{1,0:T(8,128)S(1)} %get-tuple-element.20.refs_1_.refs_2_), channel_id=1, source_target_pairs={{0,16},{16,0},{1,17},{17,1},{2,18},{18,2},{3,19},{19,3},{4,20},{20... | collective-permute-start | bytes 122888 | tf_op jit(solution)/shard_map/ppermute | solution.py:419
  7.2 6.2 %collective-permute-start.1 = (f32[160,128]{1,0:T(8,128)S(1)}, f32[160,128]{1,0:T(8,128)S(1)}, u32[]{:S(2)}, u32[]{:S(2)}) collective-permute-start(f32[160,128]{1,0:T(8,128)S(1)} %pad_maximum_fusion.1.refs_3_), channel_id=1, source_target_pairs={{0,4},{4,0},{8,12},{12,8},{1,5},{5,1},{9,13},{13,9},{2,6},{6,2},{1... | collective-permute-start | bytes 245768 | tf_op jit(solution)/shard_map/ppermute | solution.py:419
  9.3 6.2 %collective-permute-start.2 = (f32[160,128]{1,0:T(8,128)S(1)}, f32[160,128]{1,0:T(8,128)S(1)}, u32[]{:S(2)}, u32[]{:S(2)}) collective-permute-start(f32[160,128]{1,0:T(8,128)S(1)} %pad_maximum_fusion.1.refs_3_), channel_id=1, source_target_pairs={{0,12},{4,8},{8,4},{12,0},{1,13},{5,9},{9,5},{13,1},{2,14},{6,10},... | collective-permute-start | bytes 245768 | tf_op jit(solution)/shard_map/ppermute | solution.py:419
  15.5 3.7 %collective-permute-start.4 = (f32[480,128]{1,0:T(8,128)S(1)}, f32[480,128]{1,0:T(8,128)S(1)}, u32[]{:S(2)}, u32[]{:S(2)}) collective-permute-start(f32[480,128]{1,0:T(8,128)S(1)} %pad_maximum_fusion.refs_3_.refs_8_), channel_id=1, source_target_pairs={{0,1},{1,0},{2,3},{3,2},{4,5},{5,4},{6,7},{7,6},{8,9},{9,8},{10,11... | collective-permute-start | bytes 737288 | tf_op jit(solution)/shard_map/ppermute | solution.py:419
  15.6 8.7 %collective-permute-start.3 = (f32[480,128]{1,0:T(8,128)S(1)}, f32[480,128]{1,0:T(8,128)S(1)}, u32[]{:S(2)}, u32[]{:S(2)}) collective-permute-start(f32[480,128]{1,0:T(8,128)S(1)} %pad_maximum_fusion.refs_3_.refs_8_), channel_id=1, source_target_pairs={{0,3},{1,2},{2,1},{3,0},{4,7},{5,6},{6,5},{7,4},{8,11},{9,10},{10,... | collective-permute-start | bytes 737288 | tf_op jit(solution)/shard_map/ppermute | solution.py:419
  31.9 3.7 %collective-permute-start.5 = (f32[2,8,128]{2,1,0:T(8,128)S(1)}, f32[2,8,128]{2,1,0:T(8,128)S(1)}, u32[]{:S(2)}, u32[]{:S(2)}) collective-permute-start(f32[2,8,128]{2,1,0:T(8,128)S(1)} %get-tuple-element.35), channel_id=1, source_target_pairs={{0,16},{16,0},{1,17},{17,1},{2,18},{18,2},{3,19},{19,3},{4,20},{20... | collective-permute-start | bytes 24584 | tf_op jit(solution)/shard_map/ppermute | solution.py:571

commit v6 on v5

--- a/solution.py
+++ b/solution.py
@@ -310,11 +310,20 @@
     return [h, h, h, m, m, l], [h, m, l, h, m, h]
 
 
-def final_kernel(tiles, groups, entries, sources, *refs):
-    lists_ref, own, mass_sum_ref, atomic, mass, label_ref, leave_ref, hot = refs[:8]
-    cells = refs[8 : 8 + sources]
-    rest = refs[8 + sources :]
-    forces_out, record_out, leave_hot, raw, far, near, nearest = rest[:7]
+def force_kernel(tiles, groups, scaled, atomic, mass, label_ref, hot, forces_out):
+    spread = gather_rows(scaled[...], label_ref[...], hot[...], groups)
+    for d in range(3):
+        added = mass[...] * spread[d]
+        for t in range(tiles):
+            row = slice(d * tiles + t, d * tiles + t + 1)
+            forces_out[row, :] = atomic[row, :] + added[:, t * LANES : (t + 1) * LANES]
+
+
+def record_kernel(tiles, groups, entries, sources, *refs):
+    lists_ref, own, mass_sum_ref, atomic, label_ref, leave_ref, hot = refs[:7]
+    cells = refs[7 : 7 + sources]
+    rest = refs[7 + sources :]
+    scaled_out, record_out, leave_hot, raw, far, near, nearest = rest[:7]
     buffers, (total, coarse) = rest[7:9], rest[9:]
     lists, listed = lists_ref[...], lists_ref.shape[1]
     height = 4 * (tiles + groups)
@@ -381,17 +390,11 @@
             products(b + 1, buffers[(b + 1) % 2])
         strengths(b, buffers[b % 2])
 
-    label = label_ref[...]
     mass_sum = mass_sum_ref[...]
-    scaled = coarse[...] / jnp.concatenate([mass_sum] * 3, axis=0)
-    spread = gather_rows(scaled, label, hot[...], groups)
-    forces = []
-    for d in range(3):
-        forces.append(flat_row(atomic, d * tiles, tiles) + mass[...] * spread[d])
-        for t in range(tiles):
-            at = slice(t * LANES, (t + 1) * LANES)
-            forces_out[d * tiles + t : d * tiles + t + 1, :] = forces[d][:, at]
-    molecule = sum_rows(forces, label, hot[...], groups)
+    flat = [flat_row(atomic, d * tiles, tiles) for d in range(3)]
+    summed = sum_rows(flat, label_ref[...], hot[...], groups)
+    scaled_out[...] = coarse[...] / jnp.concatenate([mass_sum] * 3, axis=0)
+    molecule = summed + coarse[...]
     table = jnp.concatenate(
         [own[base : base + 3 * groups, :], molecule, own_weight, mass_sum], axis=0
     )
@@ -546,13 +549,13 @@
     z_steps = [0] + [step for _, step in with_z]
     entries = [(s, c, (x, y, z_steps[s])) for s in range(3) for c, (x, y) in plane_cells]
     every, listed = len(entries) * groups, small[0].shape[1]
-    forces, record = pl.pallas_call(
-        functools.partial(final_kernel, tiles, groups, entries, len(sources)),
+    scaled, record = pl.pallas_call(
+        functools.partial(record_kernel, tiles, groups, entries, len(sources)),
         out_shape=(
-            pltpu.VMEM((3 * tiles, LANES), F32),
+            jax.ShapeDtypeStruct((3 * groups, LANES), F32),
             jax.ShapeDtypeStruct((2, 8, leavers), F32),
         ),
-        in_specs=[VMEM] * (8 + len(sources)),
+        in_specs=[VMEM] * (7 + len(sources)),
         out_specs=(VMEM, VMEM),
         scratch_shapes=[
             pltpu.VMEM((LANES, 2 * leavers), BF16),
@@ -565,7 +568,14 @@
             pltpu.VMEM((3 * groups, LANES), F32),
         ],
         compiler_params=limit,
-    )(small[0], own, mass_sum, force, mass, label, small[1], hot, *sources)
+    )(small[0], own, mass_sum, force, label, small[1], hot, *sources)
+    forces = pl.pallas_call(
+        functools.partial(force_kernel, tiles, groups),
+        out_shape=jax.ShapeDtypeStruct((3 * tiles, LANES), F32),
+        in_specs=[VMEM] * 5,
+        out_specs=VMEM,
+        compiler_params=limit,
+    )(scaled, force, mass, label, hot)
     n = lax.axis_size("gx")
     if n == 2:
         arrivals = lax.ppermute(record, "gx", [(0, 1), (1, 0)])

time: 36.4 us -> 36 us (0.989)
  local copies, waits for them, and re-layouts: 1.21 us -> 0.6 us
  Pallas kernels: 21.1 us -> 21.5 us
    unnamed x2 -> x1, local copies, waits for them, and re-layouts: 1.21 us -> 0.6 us
    pallas_call x1 -> x2, Pallas kernels: 2.48 us -> 2.89 us  [the longest x1 2.02 us: per_device(): pl.pallas_call(functools.partial(record_kernel, tiles, groups, entries, l...]
  transfers between devices with their start and end apart: 6 -> 6, of which waited for: 3 -> 3; matrix products, arithmetic and copies ran while one was open for 2% -> 0% of each run, Pallas kernels for 33% -> 36%
where the time goes in v6:
time: 36 us; the launch traced here: 35.8 us
  Pallas kernels  21.5 us (60%)
  starting transfers between devices  10.8 us (30%)
  waiting for transfers between devices  2.08 us (6%)
  between operations  0.73 us (2%)
  local copies, waits for them, and re-layouts  0.6 us (2%)
    pallas_call x6, Pallas kernels, pairs(): pl.pallas_call(functools.partial(pair_kernel, tiles, groups, entries, len...  17.1 us
    ppermute x5, starting transfers between devices, exchange(): lax.ppermute(x, axis, list(enumerate(receivers)))  9.29 us
    pallas_call x1, Pallas kernels, per_device(): pl.pallas_call(functools.partial(record_kernel, tiles, groups, entries, l...  2.02 us
    pallas_call x1, Pallas kernels, per_device(): pl.pallas_call(prepare_kernel, out_shape=(jax.ShapeDtypeStruct((height, L...  1.55 us
    ppermute x1, starting transfers between devices, per_device(): arrivals = lax.ppermute(record, 'gx', [(0, 1), (1, 0)])  1.53 us
    ppermute x1, waiting for transfers between devices, per_device(): arrivals = lax.ppermute(record, 'gx', [(0, 1), (1, 0)])  1.32 us
    pallas_call x1, Pallas kernels, per_device(): pl.pallas_call(functools.partial(force_kernel, tiles, groups), out_shape=...  0.87 us
    ppermute x5, waiting for transfers between devices, exchange(): lax.ppermute(x, axis, list(enumerate(receivers)))  0.76 us
  transfers between devices with their start and end apart: 6, of which 3 were waited for; matrix products, arithmetic and copies ran while one was open for 0% of the time, Pallas kernels for 36%

profile of v6, /device:TPU:0, one launch (start us, length us, event | category | flops | bytes accessed | tf_op | source)
XLA Modules:
  0.0 35.8 jit_solution(15525571047047454432)
XLA Ops:
  0.6 1.5 %shard_map.95 = (f32[80,128]{1,0:T(8,128)S(1)}, f32[4,128]{1,0:T(4,128)S(1)}, bf16[128,2048]{1,0:T(8,128)(2,1)S(1)}, s32[1,2048]{1,0:T(1,128)S(1)}, f32[1,2048]{...) custom-call(s32[1,2048]{1,0:T(1,128)} %bitcast.12, f32[1,2048]{1,0:T(1,128)} %bitcast.13, ...), custom_call_target="tpu_custom_call" | custom-call | tf_op jit(solution)/shard_map/pallas_call | solution.py:469
  2.2 3.0 %collective-permute-start = (f32[80,128]{1,0:T(8,128)S(1)}, f32[80,128]{1,0:T(8,128)S(1)}, u32[]{:S(2)}, u32[]{:S(2)}) collective-permute-start(f32[80,128]{1,0:T(8,128)S(1)} %get-tuple-element.20.refs_1_.refs_2_), channel_id=1, source_target_pairs={{0,16},{16,0},{1,17},{17,1},{2,18},{18,2},{3,19},{19,3},{4,20},{20... | collective-permute-start | bytes 122888 | tf_op jit(solution)/shard_map/ppermute | solution.py:422
  5.2 1.4 %shard_map.96 = (f32[16,4,128,128]{3,2,1,0:T(8,128)S(1)}, s32[16,6]{1,0:T(8,128)S(1)}, bf16[16,128,32]{2,1,0:T(8,128)(2,1)S(1)}) custom-call(s32[16,27]{1,0:T(8,128)S(1)} %get-tuple-element.22.refs_0_, f32[80,128]{1,0:T(8,128)S(1)} %get-tuple-element.20.refs_1_.refs_2_, f32[80,128]{1,0:T(8,128)S(1)} %get-tuple-element.20.refs_1_.refs_2_), custom_call_target="tpu_custom_call" | custom-call | flops 15728640 | bytes 40960 | tf_op jit(solution)/shard_map/pallas_call | solution.py:498
  6.6 0.6 %collective-permute-done = f32[80,128]{1,0:T(8,128)S(1)} collective-permute-done((f32[80,128]{1,0:T(8,128)S(1)}, f32[80,128]{1,0:T(8,128)S(1)}, u32[]{:S(2)}, u32[]{:S(2)}) %collective-permute-start) | collective-permute-done | bytes 40992 | tf_op jit(solution)/shard_map/ppermute | solution.py:422
  7.2 2.1 %collective-permute-start.1 = (f32[160,128]{1,0:T(8,128)S(1)}, f32[160,128]{1,0:T(8,128)S(1)}, u32[]{:S(2)}, u32[]{:S(2)}) collective-permute-start(f32[160,128]{1,0:T(8,128)S(1)} %pad_maximum_fusion.1.refs_3_), channel_id=1, source_target_pairs={{0,4},{4,0},{8,12},{12,8},{1,5},{5,1},{9,13},{13,9},{2,6},{6,2},{1... | collective-permute-start | bytes 245768 | tf_op jit(solution)/shard_map/ppermute | solution.py:422
  9.3 2.5 %collective-permute-start.2 = (f32[160,128]{1,0:T(8,128)S(1)}, f32[160,128]{1,0:T(8,128)S(1)}, u32[]{:S(2)}, u32[]{:S(2)}) collective-permute-start(f32[160,128]{1,0:T(8,128)S(1)} %pad_maximum_fusion.1.refs_3_), channel_id=1, source_target_pairs={{0,12},{4,8},{8,4},{12,0},{1,13},{5,9},{9,5},{13,1},{2,14},{6,10},... | collective-permute-start | bytes 245768 | tf_op jit(solution)/shard_map/ppermute | solution.py:422
  11.8 1.6 %shard_map.97.refs_4_ = f32[16,4,128,128]{3,2,1,0:T(8,128)S(1)} custom-call(s32[16,6]{1,0:T(8,128)S(1)} %get-tuple-element.23.refs_0_, f32[80,128]{1,0:T(8,128)S(1)} %get-tuple-element.20.refs_1_.refs_2_, bf16[16,128,32]{2,1,0:T(8,128)(2,1)S(1)} %get-tuple-element.24.refs_2_, ...), custom_call_target="tpu_custom_call", output_to_operand_aliasing={{}: (4, {})} | custom-call | flops 31457280 | bytes 40960 | tf_op jit(solution)/shard_map/pallas_call | solution.py:498
  13.4 0.0 collective-permute-done.1.refs_3_
  13.4 2.0 %shard_map.98.refs_4_ = f32[16,4,128,128]{3,2,1,0:T(8,128)S(1)} custom-call(s32[16,6]{1,0:T(8,128)S(1)} %get-tuple-element.23.refs_0_, f32[80,128]{1,0:T(8,128)S(1)} %get-tuple-element.20.refs_1_.refs_2_, bf16[16,128,32]{2,1,0:T(8,128)(2,1)S(1)} %get-tuple-element.24.refs_2_, ...), custom_call_target="tpu_custom_call", output_to_operand_aliasing={{}: (4, {})} | custom-call | flops 47185920 | bytes 40960 | tf_op jit(solution)/shard_map/pallas_call | solution.py:498
  15.4 0.1 collective-permute-done.2
  15.5 0.1 collective-permute-start.4
  15.6 1.6 %collective-permute-start.3 = (f32[480,128]{1,0:T(8,128)S(1)}, f32[480,128]{1,0:T(8,128)S(1)}, u32[]{:S(2)}, u32[]{:S(2)}) collective-permute-start(f32[480,128]{1,0:T(8,128)S(1)} %pad_maximum_fusion.refs_3_.refs_7_), channel_id=1, source_target_pairs={{0,3},{1,2},{2,1},{3,0},{4,7},{5,6},{6,5},{7,4},{8,11},{9,10},{10,... | collective-permute-start | bytes 737288 | tf_op jit(solution)/shard_map/ppermute | solution.py:422
  17.3 2.0 %shard_map.99.refs_4_ = f32[16,4,128,128]{3,2,1,0:T(8,128)S(1)} custom-call(s32[16,6]{1,0:T(8,128)S(1)} %get-tuple-element.23.refs_0_, f32[80,128]{1,0:T(8,128)S(1)} %get-tuple-element.20.refs_1_.refs_2_, bf16[16,128,32]{2,1,0:T(8,128)(2,1)S(1)} %get-tuple-element.24.refs_2_, ...), custom_call_target="tpu_custom_call", output_to_operand_aliasing={{}: (4, {})} | custom-call | flops 47185920 | bytes 40960 | tf_op jit(solution)/shard_map/pallas_call | solution.py:498
  19.2 0.0 collective-permute-done.4.refs_3_.refs_8_
  19.3 5.0 %shard_map.100.refs_4_ = f32[16,4,128,128]{3,2,1,0:T(8,128)S(1)} custom-call(s32[16,6]{1,0:T(8,128)S(1)} %get-tuple-element.23.refs_0_, f32[80,128]{1,0:T(8,128)S(1)} %get-tuple-element.20.refs_1_.refs_2_, bf16[16,128,32]{2,1,0:T(8,128)(2,1)S(1)} %get-tuple-element.24.refs_2_, ...), custom_call_target="tpu_custom_call", output_to_operand_aliasing={{}: (4, {})} | custom-call | flops 141557760 | bytes 40960 | tf_op jit(solution)/shard_map/pallas_call | solution.py:498
  24.3 0.0 collective-permute-done.3.refs_3_.refs_9_
  24.3 5.1 %shard_map.101.refs_3_.atomic = f32[48,128]{1,0:T(8,128)S(1)} custom-call(s32[16,6]{1,0:T(8,128)S(1)} %get-tuple-element.23.refs_0_, f32[80,128]{1,0:T(8,128)S(1)} %get-tuple-element.20.refs_1_.refs_2_, bf16[16,128,32]{2,1,0:T(8,128)(2,1)S(1)} %get-tuple-element.24.refs_2_, f32[480,128]{1,0:T(8,128)S(1)} %collective-permute-done.3.refs_3_.refs_9_, ...), custom_call_target="tpu_custom_call" | custom-call | flops 141557760 | bytes 40960 | tf_op jit(solution)/shard_map/pallas_call | solution.py:498
  29.4 2.0 %shard_map.102 = (f32[12,128]{1,0:T(8,128)S(1)}, f32[2,8,128]{2,1,0:T(8,128)S(1)}) custom-call(s32[4,12]{1,0:T(4,128)S(1)} %get-tuple-element.19.refs_0_, f32[80,128]{1,0:T(8,128)S(1)} %get-tuple-element.20.refs_1_.refs_2_, f32[4,128]{1,0:T(4,128)S(1)} %get-tuple-element.21.refs_2_, f32[48,128]{1,0:T(8,128)S(1)} %shard_map.101.refs_3_.atomic, ...), custom_call_target="tpu_custom_call" | custom-call | tf_op jit(solution)/shard_map/pallas_call | solution.py:552
  31.4 1.5 %collective-permute-start.5 = (f32[2,8,128]{2,1,0:T(8,128)S(1)}, f32[2,8,128]{2,1,0:T(8,128)S(1)}, u32[]{:S(2)}, u32[]{:S(2)}) collective-permute-start(f32[2,8,128]{2,1,0:T(8,128)S(1)} %get-tuple-element.35), channel_id=1, source_target_pairs={{0,16},{16,0},{1,17},{17,1},{2,18},{18,2},{3,19},{19,3},{4,20},{20... | collective-permute-start | bytes 24584 | tf_op jit(solution)/shard_map/ppermute | solution.py:581
  33.0 0.9 %shard_map.103 = f32[48,128]{1,0:T(8,128)} custom-call(f32[12,128]{1,0:T(8,128)S(1)} %get-tuple-element.33.scaled, f32[48,128]{1,0:T(8,128)S(1)} %shard_map.101.refs_3_.atomic, f32[1,2048]{1,0:T(1,128)S(1)} %get-tuple-element.34.mass, s32[1,2048]{1,0:T(1,128)S(1)} %get-tuple-element.30.refs_4_.label_ref, bf16[128,2048]{1,0:T(8,128)(2,1)S(1)} %get-tuple-element.32.refs_6_.hot), custom_call_target="tpu_custom_call" | custom-call | tf_op jit(solution)/shard_map/pallas_call | solution.py:572
  33.8 1.3 %collective-permute-done.5 = f32[2,8,128]{2,1,0:T(8,128)S(1)} collective-permute-done((f32[2,8,128]{2,1,0:T(8,128)S(1)}, f32[2,8,128]{2,1,0:T(8,128)S(1)}, u32[]{:S(2)}, u32[]{:S(2)}) %collective-permute-start.5) | collective-permute-done | bytes 8224 | tf_op jit(solution)/shard_map/ppermute | solution.py:581
  35.2 0.6 %copy.21 = f32[1,1,1,2,8,128]{5,4,3,2,1,0:T(8,128)} copy(f32[1,1,1,2,8,128]{5,4,3,2,1,0:T(8,128)S(1)} %bitcast.16) | data formatting | bytes 16384
  (2 shorter events, 0.0 us)
Async XLA Ops:
  2.2 5.0 %collective-permute-start = (f32[80,128]{1,0:T(8,128)S(1)}, f32[80,128]{1,0:T(8,128)S(1)}, u32[]{:S(2)}, u32[]{:S(2)}) collective-permute-start(f32[80,128]{1,0:T(8,128)S(1)} %get-tuple-element.20.refs_1_.refs_2_), channel_id=1, source_target_pairs={{0,16},{16,0},{1,17},{17,1},{2,18},{18,2},{3,19},{19,3},{4,20},{20... | collective-permute-start | bytes 122888 | tf_op jit(solution)/shard_map/ppermute | solution.py:422
  7.2 6.2 %collective-permute-start.1 = (f32[160,128]{1,0:T(8,128)S(1)}, f32[160,128]{1,0:T(8,128)S(1)}, u32[]{:S(2)}, u32[]{:S(2)}) collective-permute-start(f32[160,128]{1,0:T(8,128)S(1)} %pad_maximum_fusion.1.refs_3_), channel_id=1, source_target_pairs={{0,4},{4,0},{8,12},{12,8},{1,5},{5,1},{9,13},{13,9},{2,6},{6,2},{1... | collective-permute-start | bytes 245768 | tf_op jit(solution)/shard_map/ppermute | solution.py:422
  9.3 6.2 %collective-permute-start.2 = (f32[160,128]{1,0:T(8,128)S(1)}, f32[160,128]{1,0:T(8,128)S(1)}, u32[]{:S(2)}, u32[]{:S(2)}) collective-permute-start(f32[160,128]{1,0:T(8,128)S(1)} %pad_maximum_fusion.1.refs_3_), channel_id=1, source_target_pairs={{0,12},{4,8},{8,4},{12,0},{1,13},{5,9},{9,5},{13,1},{2,14},{6,10},... | collective-permute-start | bytes 245768 | tf_op jit(solution)/shard_map/ppermute | solution.py:422
  15.5 3.7 %collective-permute-start.4 = (f32[480,128]{1,0:T(8,128)S(1)}, f32[480,128]{1,0:T(8,128)S(1)}, u32[]{:S(2)}, u32[]{:S(2)}) collective-permute-start(f32[480,128]{1,0:T(8,128)S(1)} %pad_maximum_fusion.refs_3_.refs_7_), channel_id=1, source_target_pairs={{0,1},{1,0},{2,3},{3,2},{4,5},{5,4},{6,7},{7,6},{8,9},{9,8},{10,11... | collective-permute-start | bytes 737288 | tf_op jit(solution)/shard_map/ppermute | solution.py:422
  15.6 8.7 %collective-permute-start.3 = (f32[480,128]{1,0:T(8,128)S(1)}, f32[480,128]{1,0:T(8,128)S(1)}, u32[]{:S(2)}, u32[]{:S(2)}) collective-permute-start(f32[480,128]{1,0:T(8,128)S(1)} %pad_maximum_fusion.refs_3_.refs_7_), channel_id=1, source_target_pairs={{0,3},{1,2},{2,1},{3,0},{4,7},{5,6},{6,5},{7,4},{8,11},{9,10},{10,... | collective-permute-start | bytes 737288 | tf_op jit(solution)/shard_map/ppermute | solution.py:422
  31.4 3.7 %collective-permute-start.5 = (f32[2,8,128]{2,1,0:T(8,128)S(1)}, f32[2,8,128]{2,1,0:T(8,128)S(1)}, u32[]{:S(2)}, u32[]{:S(2)}) collective-permute-start(f32[2,8,128]{2,1,0:T(8,128)S(1)} %get-tuple-element.35), channel_id=1, source_target_pairs={{0,16},{16,0},{1,17},{17,1},{2,18},{18,2},{3,19},{19,3},{4,20},{20... | collective-permute-start | bytes 24584 | tf_op jit(solution)/shard_map/ppermute | solution.py:581

commit v7 on v6

--- a/solution.py
+++ b/solution.py
@@ -14,7 +14,7 @@
 SIGMA_SQ = 0.25
 LANES = 128
 ROWS = 32
-PARTS = 4
+PARTS = 2
 F32, BF16 = jnp.float32, jnp.bfloat16
 VMEM = pl.BlockSpec(memory_space=pltpu.VMEM)
 HBM = pl.BlockSpec(memory_space=pltpu.HBM)

time: 36 us -> 35.7 us (level)
  Pallas kernels: 21.5 us -> 21.1 us
    pallas_call x6, Pallas kernels: 17.1 us -> 16.7 us  [pairs(): pl.pallas_call(functools.partial(pair_kernel, tiles, groups, entries, len...]
where the time goes in v7:
time: 35.7 us; the launch traced here: 35.5 us
  Pallas kernels  21.1 us (59%)
  starting transfers between devices  10.8 us (30%)
  waiting for transfers between devices  2.14 us (6%)
  between operations  0.73 us (2%)
  local copies, waits for them, and re-layouts  0.6 us (2%)
    pallas_call x6, Pallas kernels, pairs(): pl.pallas_call(functools.partial(pair_kernel, tiles, groups, entries, len...  16.7 us
    ppermute x5, starting transfers between devices, exchange(): lax.ppermute(x, axis, list(enumerate(receivers)))  9.29 us
    pallas_call x1, Pallas kernels, per_device(): pl.pallas_call(functools.partial(record_kernel, tiles, groups, entries, l...  2.02 us
    pallas_call x1, Pallas kernels, per_device(): pl.pallas_call(prepare_kernel, out_shape=(jax.ShapeDtypeStruct((height, L...  1.55 us
    ppermute x1, starting transfers between devices, per_device(): arrivals = lax.ppermute(record, 'gx', [(0, 1), (1, 0)])  1.53 us
    ppermute x1, waiting for transfers between devices, per_device(): arrivals = lax.ppermute(record, 'gx', [(0, 1), (1, 0)])  1.32 us
    pallas_call x1, Pallas kernels, per_device(): pl.pallas_call(functools.partial(force_kernel, tiles, groups), out_shape=...  0.86 us
    ppermute x5, waiting for transfers between devices, exchange(): lax.ppermute(x, axis, list(enumerate(receivers)))  0.82 us
  transfers between devices with their start and end apart: 6, of which 3 were waited for; matrix products, arithmetic and copies ran while one was open for 0% of the time, Pallas kernels for 36%

profile of v7, /device:TPU:0, one launch (start us, length us, event | category | flops | bytes accessed | tf_op | source)
XLA Modules:
  0.0 35.5 jit_solution(7453304780268936114)
XLA Ops:
  0.6 1.5 %shard_map.95 = (f32[80,128]{1,0:T(8,128)S(1)}, f32[4,128]{1,0:T(4,128)S(1)}, bf16[128,2048]{1,0:T(8,128)(2,1)S(1)}, s32[1,2048]{1,0:T(1,128)S(1)}, f32[1,2048]{...) custom-call(s32[1,2048]{1,0:T(1,128)} %bitcast.12, f32[1,2048]{1,0:T(1,128)} %bitcast.13, ...), custom_call_target="tpu_custom_call" | custom-call | tf_op jit(solution)/shard_map/pallas_call | solution.py:469
  2.2 3.0 %collective-permute-start = (f32[80,128]{1,0:T(8,128)S(1)}, f32[80,128]{1,0:T(8,128)S(1)}, u32[]{:S(2)}, u32[]{:S(2)}) collective-permute-start(f32[80,128]{1,0:T(8,128)S(1)} %get-tuple-element.20.refs_1_.refs_2_), channel_id=1, source_target_pairs={{0,16},{16,0},{1,17},{17,1},{2,18},{18,2},{3,19},{19,3},{4,20},{20... | collective-permute-start | bytes 122888 | tf_op jit(solution)/shard_map/ppermute | solution.py:422
  5.2 1.4 %shard_map.96 = (f32[16,4,128,128]{3,2,1,0:T(8,128)S(1)}, s32[16,6]{1,0:T(8,128)S(1)}, bf16[16,128,32]{2,1,0:T(8,128)(2,1)S(1)}) custom-call(s32[16,27]{1,0:T(8,128)S(1)} %get-tuple-element.22.refs_0_, f32[80,128]{1,0:T(8,128)S(1)} %get-tuple-element.20.refs_1_.refs_2_, f32[80,128]{1,0:T(8,128)S(1)} %get-tuple-element.20.refs_1_.refs_2_), custom_call_target="tpu_custom_call" | custom-call | flops 15728640 | bytes 40960 | tf_op jit(solution)/shard_map/pallas_call | solution.py:498
  6.6 0.6 %collective-permute-done = f32[80,128]{1,0:T(8,128)S(1)} collective-permute-done((f32[80,128]{1,0:T(8,128)S(1)}, f32[80,128]{1,0:T(8,128)S(1)}, u32[]{:S(2)}, u32[]{:S(2)}) %collective-permute-start) | collective-permute-done | bytes 40992 | tf_op jit(solution)/shard_map/ppermute | solution.py:422
  7.2 2.1 %collective-permute-start.1 = (f32[160,128]{1,0:T(8,128)S(1)}, f32[160,128]{1,0:T(8,128)S(1)}, u32[]{:S(2)}, u32[]{:S(2)}) collective-permute-start(f32[160,128]{1,0:T(8,128)S(1)} %pad_maximum_fusion.1.refs_3_), channel_id=1, source_target_pairs={{0,4},{4,0},{8,12},{12,8},{1,5},{5,1},{9,13},{13,9},{2,6},{6,2},{1... | collective-permute-start | bytes 245768 | tf_op jit(solution)/shard_map/ppermute | solution.py:422
  9.3 2.5 %collective-permute-start.2 = (f32[160,128]{1,0:T(8,128)S(1)}, f32[160,128]{1,0:T(8,128)S(1)}, u32[]{:S(2)}, u32[]{:S(2)}) collective-permute-start(f32[160,128]{1,0:T(8,128)S(1)} %pad_maximum_fusion.1.refs_3_), channel_id=1, source_target_pairs={{0,12},{4,8},{8,4},{12,0},{1,13},{5,9},{9,5},{13,1},{2,14},{6,10},... | collective-permute-start | bytes 245768 | tf_op jit(solution)/shard_map/ppermute | solution.py:422
  11.8 1.6 %shard_map.97.refs_4_ = f32[16,4,128,128]{3,2,1,0:T(8,128)S(1)} custom-call(s32[16,6]{1,0:T(8,128)S(1)} %get-tuple-element.23.refs_0_, f32[80,128]{1,0:T(8,128)S(1)} %get-tuple-element.20.refs_1_.refs_2_, bf16[16,128,32]{2,1,0:T(8,128)(2,1)S(1)} %get-tuple-element.24.refs_2_, ...), custom_call_target="tpu_custom_call", output_to_operand_aliasing={{}: (4, {})} | custom-call | flops 31457280 | bytes 40960 | tf_op jit(solution)/shard_map/pallas_call | solution.py:498
  13.4 0.0 collective-permute-done.1.refs_3_
  13.4 1.9 %shard_map.98.refs_4_ = f32[16,4,128,128]{3,2,1,0:T(8,128)S(1)} custom-call(s32[16,6]{1,0:T(8,128)S(1)} %get-tuple-element.23.refs_0_, f32[80,128]{1,0:T(8,128)S(1)} %get-tuple-element.20.refs_1_.refs_2_, bf16[16,128,32]{2,1,0:T(8,128)(2,1)S(1)} %get-tuple-element.24.refs_2_, ...), custom_call_target="tpu_custom_call", output_to_operand_aliasing={{}: (4, {})} | custom-call | flops 47185920 | bytes 40960 | tf_op jit(solution)/shard_map/pallas_call | solution.py:498
  15.3 0.2 collective-permute-done.2
  15.5 0.1 collective-permute-start.4
  15.6 1.6 %collective-permute-start.3 = (f32[480,128]{1,0:T(8,128)S(1)}, f32[480,128]{1,0:T(8,128)S(1)}, u32[]{:S(2)}, u32[]{:S(2)}) collective-permute-start(f32[480,128]{1,0:T(8,128)S(1)} %pad_maximum_fusion.refs_3_.refs_7_), channel_id=1, source_target_pairs={{0,3},{1,2},{2,1},{3,0},{4,7},{5,6},{6,5},{7,4},{8,11},{9,10},{10,... | collective-permute-start | bytes 737288 | tf_op jit(solution)/shard_map/ppermute | solution.py:422
  17.3 1.9 %shard_map.99.refs_4_ = f32[16,4,128,128]{3,2,1,0:T(8,128)S(1)} custom-call(s32[16,6]{1,0:T(8,128)S(1)} %get-tuple-element.23.refs_0_, f32[80,128]{1,0:T(8,128)S(1)} %get-tuple-element.20.refs_1_.refs_2_, bf16[16,128,32]{2,1,0:T(8,128)(2,1)S(1)} %get-tuple-element.24.refs_2_, ...), custom_call_target="tpu_custom_call", output_to_operand_aliasing={{}: (4, {})} | custom-call | flops 47185920 | bytes 40960 | tf_op jit(solution)/shard_map/pallas_call | solution.py:498
  19.2 0.0 collective-permute-done.4.refs_3_.refs_8_
  19.2 4.9 %shard_map.100.refs_4_ = f32[16,4,128,128]{3,2,1,0:T(8,128)S(1)} custom-call(s32[16,6]{1,0:T(8,128)S(1)} %get-tuple-element.23.refs_0_, f32[80,128]{1,0:T(8,128)S(1)} %get-tuple-element.20.refs_1_.refs_2_, bf16[16,128,32]{2,1,0:T(8,128)(2,1)S(1)} %get-tuple-element.24.refs_2_, ...), custom_call_target="tpu_custom_call", output_to_operand_aliasing={{}: (4, {})} | custom-call | flops 141557760 | bytes 40960 | tf_op jit(solution)/shard_map/pallas_call | solution.py:498
  24.1 0.0 collective-permute-done.3.refs_3_.refs_9_
  24.1 5.0 %shard_map.101.refs_3_.atomic = f32[48,128]{1,0:T(8,128)S(1)} custom-call(s32[16,6]{1,0:T(8,128)S(1)} %get-tuple-element.23.refs_0_, f32[80,128]{1,0:T(8,128)S(1)} %get-tuple-element.20.refs_1_.refs_2_, bf16[16,128,32]{2,1,0:T(8,128)(2,1)S(1)} %get-tuple-element.24.refs_2_, f32[480,128]{1,0:T(8,128)S(1)} %collective-permute-done.3.refs_3_.refs_9_, ...), custom_call_target="tpu_custom_call" | custom-call | flops 141557760 | bytes 40960 | tf_op jit(solution)/shard_map/pallas_call | solution.py:498
  29.1 2.0 %shard_map.102 = (f32[12,128]{1,0:T(8,128)S(1)}, f32[2,8,128]{2,1,0:T(8,128)S(1)}) custom-call(s32[4,12]{1,0:T(4,128)S(1)} %get-tuple-element.19.refs_0_, f32[80,128]{1,0:T(8,128)S(1)} %get-tuple-element.20.refs_1_.refs_2_, f32[4,128]{1,0:T(4,128)S(1)} %get-tuple-element.21.refs_2_, f32[48,128]{1,0:T(8,128)S(1)} %shard_map.101.refs_3_.atomic, ...), custom_call_target="tpu_custom_call" | custom-call | tf_op jit(solution)/shard_map/pallas_call | solution.py:552
  31.1 1.5 %collective-permute-start.5 = (f32[2,8,128]{2,1,0:T(8,128)S(1)}, f32[2,8,128]{2,1,0:T(8,128)S(1)}, u32[]{:S(2)}, u32[]{:S(2)}) collective-permute-start(f32[2,8,128]{2,1,0:T(8,128)S(1)} %get-tuple-element.35), channel_id=1, source_target_pairs={{0,16},{16,0},{1,17},{17,1},{2,18},{18,2},{3,19},{19,3},{4,20},{20... | collective-permute-start | bytes 24584 | tf_op jit(solution)/shard_map/ppermute | solution.py:581
  32.7 0.9 %shard_map.103 = f32[48,128]{1,0:T(8,128)} custom-call(f32[12,128]{1,0:T(8,128)S(1)} %get-tuple-element.33.scaled, f32[48,128]{1,0:T(8,128)S(1)} %shard_map.101.refs_3_.atomic, f32[1,2048]{1,0:T(1,128)S(1)} %get-tuple-element.34.mass, s32[1,2048]{1,0:T(1,128)S(1)} %get-tuple-element.30.refs_4_.label_ref, bf16[128,2048]{1,0:T(8,128)(2,1)S(1)} %get-tuple-element.32.refs_6_.hot), custom_call_target="tpu_custom_call" | custom-call | tf_op jit(solution)/shard_map/pallas_call | solution.py:572
  33.5 1.3 %collective-permute-done.5 = f32[2,8,128]{2,1,0:T(8,128)S(1)} collective-permute-done((f32[2,8,128]{2,1,0:T(8,128)S(1)}, f32[2,8,128]{2,1,0:T(8,128)S(1)}, u32[]{:S(2)}, u32[]{:S(2)}) %collective-permute-start.5) | collective-permute-done | bytes 8224 | tf_op jit(solution)/shard_map/ppermute | solution.py:581
  34.9 0.6 %copy.21 = f32[1,1,1,2,8,128]{5,4,3,2,1,0:T(8,128)} copy(f32[1,1,1,2,8,128]{5,4,3,2,1,0:T(8,128)S(1)} %bitcast.16) | data formatting | bytes 16384
  (2 shorter events, 0.0 us)
Async XLA Ops:
  2.2 5.0 %collective-permute-start = (f32[80,128]{1,0:T(8,128)S(1)}, f32[80,128]{1,0:T(8,128)S(1)}, u32[]{:S(2)}, u32[]{:S(2)}) collective-permute-start(f32[80,128]{1,0:T(8,128)S(1)} %get-tuple-element.20.refs_1_.refs_2_), channel_id=1, source_target_pairs={{0,16},{16,0},{1,17},{17,1},{2,18},{18,2},{3,19},{19,3},{4,20},{20... | collective-permute-start | bytes 122888 | tf_op jit(solution)/shard_map/ppermute | solution.py:422
  7.2 6.2 %collective-permute-start.1 = (f32[160,128]{1,0:T(8,128)S(1)}, f32[160,128]{1,0:T(8,128)S(1)}, u32[]{:S(2)}, u32[]{:S(2)}) collective-permute-start(f32[160,128]{1,0:T(8,128)S(1)} %pad_maximum_fusion.1.refs_3_), channel_id=1, source_target_pairs={{0,4},{4,0},{8,12},{12,8},{1,5},{5,1},{9,13},{13,9},{2,6},{6,2},{1... | collective-permute-start | bytes 245768 | tf_op jit(solution)/shard_map/ppermute | solution.py:422
  9.3 6.2 %collective-permute-start.2 = (f32[160,128]{1,0:T(8,128)S(1)}, f32[160,128]{1,0:T(8,128)S(1)}, u32[]{:S(2)}, u32[]{:S(2)}) collective-permute-start(f32[160,128]{1,0:T(8,128)S(1)} %pad_maximum_fusion.1.refs_3_), channel_id=1, source_target_pairs={{0,12},{4,8},{8,4},{12,0},{1,13},{5,9},{9,5},{13,1},{2,14},{6,10},... | collective-permute-start | bytes 245768 | tf_op jit(solution)/shard_map/ppermute | solution.py:422
  15.5 3.6 %collective-permute-start.4 = (f32[480,128]{1,0:T(8,128)S(1)}, f32[480,128]{1,0:T(8,128)S(1)}, u32[]{:S(2)}, u32[]{:S(2)}) collective-permute-start(f32[480,128]{1,0:T(8,128)S(1)} %pad_maximum_fusion.refs_3_.refs_7_), channel_id=1, source_target_pairs={{0,1},{1,0},{2,3},{3,2},{4,5},{5,4},{6,7},{7,6},{8,9},{9,8},{10,11... | collective-permute-start | bytes 737288 | tf_op jit(solution)/shard_map/ppermute | solution.py:422
  15.6 8.5 %collective-permute-start.3 = (f32[480,128]{1,0:T(8,128)S(1)}, f32[480,128]{1,0:T(8,128)S(1)}, u32[]{:S(2)}, u32[]{:S(2)}) collective-permute-start(f32[480,128]{1,0:T(8,128)S(1)} %pad_maximum_fusion.refs_3_.refs_7_), channel_id=1, source_target_pairs={{0,3},{1,2},{2,1},{3,0},{4,7},{5,6},{6,5},{7,4},{8,11},{9,10},{10,... | collective-permute-start | bytes 737288 | tf_op jit(solution)/shard_map/ppermute | solution.py:422
  31.1 3.7 %collective-permute-start.5 = (f32[2,8,128]{2,1,0:T(8,128)S(1)}, f32[2,8,128]{2,1,0:T(8,128)S(1)}, u32[]{:S(2)}, u32[]{:S(2)}) collective-permute-start(f32[2,8,128]{2,1,0:T(8,128)S(1)} %get-tuple-element.35), channel_id=1, source_target_pairs={{0,16},{16,0},{1,17},{17,1},{2,18},{18,2},{3,19},{19,3},{4,20},{20... | collective-permute-start | bytes 24584 | tf_op jit(solution)/shard_map/ppermute | solution.py:581

commit v8 on v7

--- a/solution.py
+++ b/solution.py
@@ -138,7 +138,7 @@
 
 
 def pair_plan(tiles, count):
-    held, ahead = (8, 6) if count == 1 else (8, 4) if count == 2 else (2, 1)
+    held, ahead = (8, 6) if count == 1 else (4, 2) if count == 2 else (2, 1)
     unroll = 8 if count < 6 else 4
     if tiles % unroll:
         held, unroll, ahead = 2, 2, 1

time: 35.7 us -> 35.7 us (level)
  transfers between devices with their start and end apart: 6 -> 6, of which waited for: 3 -> 3; matrix products, arithmetic and copies ran while one was open for 0% -> 0% of each run, Pallas kernels for 36% -> 35%
where the time goes in v8:
time: 35.7 us; the launch traced here: 35.4 us
  Pallas kernels  21.1 us (59%)
  starting transfers between devices  10.9 us (31%)
  waiting for transfers between devices  2.18 us (6%)
  between operations  0.73 us (2%)
  local copies, waits for them, and re-layouts  0.6 us (2%)
    pallas_call x6, Pallas kernels, pairs(): pl.pallas_call(functools.partial(pair_kernel, tiles, groups, entries, len...  16.6 us
    ppermute x5, starting transfers between devices, exchange(): lax.ppermute(x, axis, list(enumerate(receivers)))  9.29 us
    pallas_call x1, Pallas kernels, per_device(): pl.pallas_call(functools.partial(record_kernel, tiles, groups, entries, l...  2.02 us
    ppermute x1, starting transfers between devices, per_device(): arrivals = lax.ppermute(record, 'gx', [(0, 1), (1, 0)])  1.56 us
    pallas_call x1, Pallas kernels, per_device(): pl.pallas_call(prepare_kernel, out_shape=(jax.ShapeDtypeStruct((height, L...  1.55 us
    ppermute x1, waiting for transfers between devices, per_device(): arrivals = lax.ppermute(record, 'gx', [(0, 1), (1, 0)])  1.29 us
    ppermute x5, waiting for transfers between devices, exchange(): lax.ppermute(x, axis, list(enumerate(receivers)))  0.9 us
    pallas_call x1, Pallas kernels, per_device(): pl.pallas_call(functools.partial(force_kernel, tiles, groups), out_shape=...  0.87 us
  transfers between devices with their start and end apart: 6, of which 3 were waited for; matrix products, arithmetic and copies ran while one was open for 0% of the time, Pallas kernels for 35%

profile of v8, /device:TPU:0, one launch (start us, length us, event | category | flops | bytes accessed | tf_op | source)
XLA Modules:
  0.0 35.4 jit_solution(16009413193225803515)
XLA Ops:
  0.6 1.5 %shard_map.95 = (f32[80,128]{1,0:T(8,128)S(1)}, f32[4,128]{1,0:T(4,128)S(1)}, bf16[128,2048]{1,0:T(8,128)(2,1)S(1)}, s32[1,2048]{1,0:T(1,128)S(1)}, f32[1,2048]{...) custom-call(s32[1,2048]{1,0:T(1,128)} %bitcast.12, f32[1,2048]{1,0:T(1,128)} %bitcast.13, ...), custom_call_target="tpu_custom_call" | custom-call | tf_op jit(solution)/shard_map/pallas_call | solution.py:469
  2.2 3.0 %collective-permute-start = (f32[80,128]{1,0:T(8,128)S(1)}, f32[80,128]{1,0:T(8,128)S(1)}, u32[]{:S(2)}, u32[]{:S(2)}) collective-permute-start(f32[80,128]{1,0:T(8,128)S(1)} %get-tuple-element.20.refs_1_.refs_2_), channel_id=1, source_target_pairs={{0,16},{16,0},{1,17},{17,1},{2,18},{18,2},{3,19},{19,3},{4,20},{20... | collective-permute-start | bytes 122888 | tf_op jit(solution)/shard_map/ppermute | solution.py:422
  5.2 1.4 %shard_map.96 = (f32[16,4,128,128]{3,2,1,0:T(8,128)S(1)}, s32[16,6]{1,0:T(8,128)S(1)}, bf16[16,128,32]{2,1,0:T(8,128)(2,1)S(1)}) custom-call(s32[16,27]{1,0:T(8,128)S(1)} %get-tuple-element.22.refs_0_, f32[80,128]{1,0:T(8,128)S(1)} %get-tuple-element.20.refs_1_.refs_2_, f32[80,128]{1,0:T(8,128)S(1)} %get-tuple-element.20.refs_1_.refs_2_), custom_call_target="tpu_custom_call" | custom-call | flops 15728640 | bytes 40960 | tf_op jit(solution)/shard_map/pallas_call | solution.py:498
  6.6 0.6 %collective-permute-done = f32[80,128]{1,0:T(8,128)S(1)} collective-permute-done((f32[80,128]{1,0:T(8,128)S(1)}, f32[80,128]{1,0:T(8,128)S(1)}, u32[]{:S(2)}, u32[]{:S(2)}) %collective-permute-start) | collective-permute-done | bytes 40992 | tf_op jit(solution)/shard_map/ppermute | solution.py:422
  7.2 2.1 %collective-permute-start.1 = (f32[160,128]{1,0:T(8,128)S(1)}, f32[160,128]{1,0:T(8,128)S(1)}, u32[]{:S(2)}, u32[]{:S(2)}) collective-permute-start(f32[160,128]{1,0:T(8,128)S(1)} %pad_maximum_fusion.1.refs_3_), channel_id=1, source_target_pairs={{0,4},{4,0},{8,12},{12,8},{1,5},{5,1},{9,13},{13,9},{2,6},{6,2},{1... | collective-permute-start | bytes 245768 | tf_op jit(solution)/shard_map/ppermute | solution.py:422
  9.3 2.5 %collective-permute-start.2 = (f32[160,128]{1,0:T(8,128)S(1)}, f32[160,128]{1,0:T(8,128)S(1)}, u32[]{:S(2)}, u32[]{:S(2)}) collective-permute-start(f32[160,128]{1,0:T(8,128)S(1)} %pad_maximum_fusion.1.refs_3_), channel_id=1, source_target_pairs={{0,12},{4,8},{8,4},{12,0},{1,13},{5,9},{9,5},{13,1},{2,14},{6,10},... | collective-permute-start | bytes 245768 | tf_op jit(solution)/shard_map/ppermute | solution.py:422
  11.8 1.6 %shard_map.97.refs_4_ = f32[16,4,128,128]{3,2,1,0:T(8,128)S(1)} custom-call(s32[16,6]{1,0:T(8,128)S(1)} %get-tuple-element.23.refs_0_, f32[80,128]{1,0:T(8,128)S(1)} %get-tuple-element.20.refs_1_.refs_2_, bf16[16,128,32]{2,1,0:T(8,128)(2,1)S(1)} %get-tuple-element.24.refs_2_, ...), custom_call_target="tpu_custom_call", output_to_operand_aliasing={{}: (4, {})} | custom-call | flops 31457280 | bytes 40960 | tf_op jit(solution)/shard_map/pallas_call | solution.py:498
  13.3 0.0 collective-permute-done.1.refs_3_
  13.3 1.9 %shard_map.98.refs_4_ = f32[16,4,128,128]{3,2,1,0:T(8,128)S(1)} custom-call(s32[16,6]{1,0:T(8,128)S(1)} %get-tuple-element.23.refs_0_, f32[80,128]{1,0:T(8,128)S(1)} %get-tuple-element.20.refs_1_.refs_2_, bf16[16,128,32]{2,1,0:T(8,128)(2,1)S(1)} %get-tuple-element.24.refs_2_, ...), custom_call_target="tpu_custom_call", output_to_operand_aliasing={{}: (4, {})} | custom-call | flops 47185920 | bytes 40960 | tf_op jit(solution)/shard_map/pallas_call | solution.py:498
  15.3 0.3 collective-permute-done.2
  15.5 0.1 collective-permute-start.4
  15.6 1.6 %collective-permute-start.3 = (f32[480,128]{1,0:T(8,128)S(1)}, f32[480,128]{1,0:T(8,128)S(1)}, u32[]{:S(2)}, u32[]{:S(2)}) collective-permute-start(f32[480,128]{1,0:T(8,128)S(1)} %pad_maximum_fusion.refs_3_.refs_7_), channel_id=1, source_target_pairs={{0,3},{1,2},{2,1},{3,0},{4,7},{5,6},{6,5},{7,4},{8,11},{9,10},{10,... | collective-permute-start | bytes 737288 | tf_op jit(solution)/shard_map/ppermute | solution.py:422
  17.3 1.9 %shard_map.99.refs_4_ = f32[16,4,128,128]{3,2,1,0:T(8,128)S(1)} custom-call(s32[16,6]{1,0:T(8,128)S(1)} %get-tuple-element.23.refs_0_, f32[80,128]{1,0:T(8,128)S(1)} %get-tuple-element.20.refs_1_.refs_2_, bf16[16,128,32]{2,1,0:T(8,128)(2,1)S(1)} %get-tuple-element.24.refs_2_, ...), custom_call_target="tpu_custom_call", output_to_operand_aliasing={{}: (4, {})} | custom-call | flops 47185920 | bytes 40960 | tf_op jit(solution)/shard_map/pallas_call | solution.py:498
  19.2 0.0 collective-permute-done.4.refs_3_.refs_8_
  19.2 4.9 %shard_map.100.refs_4_ = f32[16,4,128,128]{3,2,1,0:T(8,128)S(1)} custom-call(s32[16,6]{1,0:T(8,128)S(1)} %get-tuple-element.23.refs_0_, f32[80,128]{1,0:T(8,128)S(1)} %get-tuple-element.20.refs_1_.refs_2_, bf16[16,128,32]{2,1,0:T(8,128)(2,1)S(1)} %get-tuple-element.24.refs_2_, ...), custom_call_target="tpu_custom_call", output_to_operand_aliasing={{}: (4, {})} | custom-call | flops 141557760 | bytes 40960 | tf_op jit(solution)/shard_map/pallas_call | solution.py:498
  24.1 0.0 collective-permute-done.3.refs_3_.refs_9_
  24.1 4.9 %shard_map.101.refs_3_.atomic = f32[48,128]{1,0:T(8,128)S(1)} custom-call(s32[16,6]{1,0:T(8,128)S(1)} %get-tuple-element.23.refs_0_, f32[80,128]{1,0:T(8,128)S(1)} %get-tuple-element.20.refs_1_.refs_2_, bf16[16,128,32]{2,1,0:T(8,128)(2,1)S(1)} %get-tuple-element.24.refs_2_, f32[480,128]{1,0:T(8,128)S(1)} %collective-permute-done.3.refs_3_.refs_9_, ...), custom_call_target="tpu_custom_call" | custom-call | flops 141557760 | bytes 40960 | tf_op jit(solution)/shard_map/pallas_call | solution.py:498
  29.1 2.0 %shard_map.102 = (f32[12,128]{1,0:T(8,128)S(1)}, f32[2,8,128]{2,1,0:T(8,128)S(1)}) custom-call(s32[4,12]{1,0:T(4,128)S(1)} %get-tuple-element.19.refs_0_, f32[80,128]{1,0:T(8,128)S(1)} %get-tuple-element.20.refs_1_.refs_2_, f32[4,128]{1,0:T(4,128)S(1)} %get-tuple-element.21.refs_2_, f32[48,128]{1,0:T(8,128)S(1)} %shard_map.101.refs_3_.atomic, ...), custom_call_target="tpu_custom_call" | custom-call | tf_op jit(solution)/shard_map/pallas_call | solution.py:552
  31.1 1.6 %collective-permute-start.5 = (f32[2,8,128]{2,1,0:T(8,128)S(1)}, f32[2,8,128]{2,1,0:T(8,128)S(1)}, u32[]{:S(2)}, u32[]{:S(2)}) collective-permute-start(f32[2,8,128]{2,1,0:T(8,128)S(1)} %get-tuple-element.35), channel_id=1, source_target_pairs={{0,16},{16,0},{1,17},{17,1},{2,18},{18,2},{3,19},{19,3},{4,20},{20... | collective-permute-start | bytes 24584 | tf_op jit(solution)/shard_map/ppermute | solution.py:581
  32.7 0.9 %shard_map.103 = f32[48,128]{1,0:T(8,128)} custom-call(f32[12,128]{1,0:T(8,128)S(1)} %get-tuple-element.33.scaled, f32[48,128]{1,0:T(8,128)S(1)} %shard_map.101.refs_3_.atomic, f32[1,2048]{1,0:T(1,128)S(1)} %get-tuple-element.34.mass, s32[1,2048]{1,0:T(1,128)S(1)} %get-tuple-element.30.refs_4_.label_ref, bf16[128,2048]{1,0:T(8,128)(2,1)S(1)} %get-tuple-element.32.refs_6_.hot), custom_call_target="tpu_custom_call" | custom-call | tf_op jit(solution)/shard_map/pallas_call | solution.py:572
  33.6 1.3 %collective-permute-done.5 = f32[2,8,128]{2,1,0:T(8,128)S(1)} collective-permute-done((f32[2,8,128]{2,1,0:T(8,128)S(1)}, f32[2,8,128]{2,1,0:T(8,128)S(1)}, u32[]{:S(2)}, u32[]{:S(2)}) %collective-permute-start.5) | collective-permute-done | bytes 8224 | tf_op jit(solution)/shard_map/ppermute | solution.py:581
  34.8 0.6 %copy.21 = f32[1,1,1,2,8,128]{5,4,3,2,1,0:T(8,128)} copy(f32[1,1,1,2,8,128]{5,4,3,2,1,0:T(8,128)S(1)} %bitcast.16) | data formatting | bytes 16384
  (2 shorter events, 0.0 us)
Async XLA Ops:
  2.2 5.0 %collective-permute-start = (f32[80,128]{1,0:T(8,128)S(1)}, f32[80,128]{1,0:T(8,128)S(1)}, u32[]{:S(2)}, u32[]{:S(2)}) collective-permute-start(f32[80,128]{1,0:T(8,128)S(1)} %get-tuple-element.20.refs_1_.refs_2_), channel_id=1, source_target_pairs={{0,16},{16,0},{1,17},{17,1},{2,18},{18,2},{3,19},{19,3},{4,20},{20... | collective-permute-start | bytes 122888 | tf_op jit(solution)/shard_map/ppermute | solution.py:422
  7.2 6.1 %collective-permute-start.1 = (f32[160,128]{1,0:T(8,128)S(1)}, f32[160,128]{1,0:T(8,128)S(1)}, u32[]{:S(2)}, u32[]{:S(2)}) collective-permute-start(f32[160,128]{1,0:T(8,128)S(1)} %pad_maximum_fusion.1.refs_3_), channel_id=1, source_target_pairs={{0,4},{4,0},{8,12},{12,8},{1,5},{5,1},{9,13},{13,9},{2,6},{6,2},{1... | collective-permute-start | bytes 245768 | tf_op jit(solution)/shard_map/ppermute | solution.py:422
  9.3 6.2 %collective-permute-start.2 = (f32[160,128]{1,0:T(8,128)S(1)}, f32[160,128]{1,0:T(8,128)S(1)}, u32[]{:S(2)}, u32[]{:S(2)}) collective-permute-start(f32[160,128]{1,0:T(8,128)S(1)} %pad_maximum_fusion.1.refs_3_), channel_id=1, source_target_pairs={{0,12},{4,8},{8,4},{12,0},{1,13},{5,9},{9,5},{13,1},{2,14},{6,10},... | collective-permute-start | bytes 245768 | tf_op jit(solution)/shard_map/ppermute | solution.py:422
  15.5 3.6 %collective-permute-start.4 = (f32[480,128]{1,0:T(8,128)S(1)}, f32[480,128]{1,0:T(8,128)S(1)}, u32[]{:S(2)}, u32[]{:S(2)}) collective-permute-start(f32[480,128]{1,0:T(8,128)S(1)} %pad_maximum_fusion.refs_3_.refs_7_), channel_id=1, source_target_pairs={{0,1},{1,0},{2,3},{3,2},{4,5},{5,4},{6,7},{7,6},{8,9},{9,8},{10,11... | collective-permute-start | bytes 737288 | tf_op jit(solution)/shard_map/ppermute | solution.py:422
  15.6 8.5 %collective-permute-start.3 = (f32[480,128]{1,0:T(8,128)S(1)}, f32[480,128]{1,0:T(8,128)S(1)}, u32[]{:S(2)}, u32[]{:S(2)}) collective-permute-start(f32[480,128]{1,0:T(8,128)S(1)} %pad_maximum_fusion.refs_3_.refs_7_), channel_id=1, source_target_pairs={{0,3},{1,2},{2,1},{3,0},{4,7},{5,6},{6,5},{7,4},{8,11},{9,10},{10,... | collective-permute-start | bytes 737288 | tf_op jit(solution)/shard_map/ppermute | solution.py:422
  31.1 3.7 %collective-permute-start.5 = (f32[2,8,128]{2,1,0:T(8,128)S(1)}, f32[2,8,128]{2,1,0:T(8,128)S(1)}, u32[]{:S(2)}, u32[]{:S(2)}) collective-permute-start(f32[2,8,128]{2,1,0:T(8,128)S(1)} %get-tuple-element.35), channel_id=1, source_target_pairs={{0,16},{16,0},{1,17},{17,1},{2,18},{18,2},{3,19},{19,3},{4,20},{20... | collective-permute-start | bytes 24584 | tf_op jit(solution)/shard_map/ppermute | solution.py:581
